TPU v7x, 32 devices: a whole 2x2x4 slice. The times are simulated.
32 devices in a mesh: dp: 8 (over z, core), expert: 4 (over y, x).
Axes of the slice: x: 2, y: 2, z: 4, core: 2. Of those that a mesh axis runs over, the one named last changes fastest.
Arguments:
- tokens: bfloat16 [4096, 1536], P(('dp', 'expert')), may hold values from -6 to 6
- cotangent: bfloat16 [4096, 1536], P(('dp', 'expert')), may hold values from -6 to 6
- lengths: int32 [8, 3], P('dp'), may hold values from 1 to 256, 512 in all within a row
- routes: int32 [4096, 6], P(('dp', 'expert')), may hold values from 0 to 15, all different within a row; in each aligned block of 128 rows (0 to 127, 128 to 255, ...) at most 64 rows name the same one
- w_in: float32 [1536, 6448], P(('dp', 'expert')), may hold values from -0.15625 to 0.15625
- w_in_first: float32 [1536, 6448], P(('dp', 'expert'))
- w_in_second: float32 [1536, 6448], P(('dp', 'expert')), as said below
- w_out: float32 [3072, 1536], P(('dp', 'expert')), may hold values from -0.109375 to 0.109375
- w_out_first: float32 [3072, 1536], P(('dp', 'expert'))
- w_out_second: float32 [3072, 1536], P(('dp', 'expert')), as said below
- w_router: float32 [1536, 16], P(('dp', 'expert'))
- w_router_first: float32 [1536, 16], P(('dp', 'expert'))
- w_router_second: float32 [1536, 16], P(('dp', 'expert')), as said below
- w_shared_gu: float32 [1536, 2048], P(('dp', 'expert')), may hold values from -0.15625 to 0.15625
- w_shared_gu_first: float32 [1536, 2048], P(('dp', 'expert'))
- w_shared_gu_second: float32 [1536, 2048], P(('dp', 'expert')), as said below
- w_shared_down: float32 [1024, 1536], P(('dp', 'expert')), may hold values from -0.1875 to 0.1875
- w_shared_down_first: float32 [1024, 1536], P(('dp', 'expert'))
- w_shared_down_second: float32 [1024, 1536], P(('dp', 'expert')), as said below
- w_expert_gu: float32 [16, 1536, 1024], P('expert', 'dp'), may hold values from -0.3125 to 0.3125
- w_expert_gu_first: float32 [16, 1536, 1024], P('expert', 'dp')
- w_expert_gu_second: float32 [16, 1536, 1024], P('expert', 'dp'), as said below
- w_expert_down: float32 [16, 512, 1536], P('expert', 'dp'), may hold values from -0.25 to 0.25
- w_expert_down_first: float32 [16, 512, 1536], P('expert', 'dp')
- w_expert_down_second: float32 [16, 512, 1536], P('expert', 'dp'), as said below
- norm_gains: float32 [2, 1536], replicated, may hold values from 0.5 to 1.5
- norm_gains_first: float32 [2, 1536], replicated
- norm_gains_second: float32 [2, 1536], replicated, as said below
- conv_params: float32 [5, 3328], replicated, may hold values from -0.5 to 0.5
- conv_params_first: float32 [5, 3328], replicated
- conv_params_second: float32 [5, 3328], replicated, as said below
- head_params: float32 [3, 48], replicated, may hold values from -4.5 to 1.5
- head_params_first: float32 [3, 48], replicated
- head_params_second: float32 [3, 48], replicated, as said below
- mixer_gain: float32 [3072], replicated, may hold values from 0.5 to 1.5
- mixer_gain_first: float32 [3072], replicated
- mixer_gain_second: float32 [3072], replicated, as said below
Outputs:
- output: bfloat16 [4096, 1536], P(('dp', 'expert'))
- grad_tokens: bfloat16 [4096, 1536], P(('dp', 'expert'))
- grad_w_in: float32 [1536, 6448], P(('dp', 'expert'))
- new_w_in: float32 [1536, 6448], P(('dp', 'expert'))
- new_w_in_first: float32 [1536, 6448], P(('dp', 'expert'))
- new_w_in_second: float32 [1536, 6448], P(('dp', 'expert'))
- grad_w_out: float32 [3072, 1536], P(('dp', 'expert'))
- new_w_out: float32 [3072, 1536], P(('dp', 'expert'))
- new_w_out_first: float32 [3072, 1536], P(('dp', 'expert'))
- new_w_out_second: float32 [3072, 1536], P(('dp', 'expert'))
- grad_w_router: float32 [1536, 16], P(('dp', 'expert'))
- new_w_router: float32 [1536, 16], P(('dp', 'expert'))
- new_w_router_first: float32 [1536, 16], P(('dp', 'expert'))
- new_w_router_second: float32 [1536, 16], P(('dp', 'expert'))
- grad_w_shared_gu: float32 [1536, 2048], P(('dp', 'expert'))
- new_w_shared_gu: float32 [1536, 2048], P(('dp', 'expert'))
- new_w_shared_gu_first: float32 [1536, 2048], P(('dp', 'expert'))
- new_w_shared_gu_second: float32 [1536, 2048], P(('dp', 'expert'))
- grad_w_shared_down: float32 [1024, 1536], P(('dp', 'expert'))
- new_w_shared_down: float32 [1024, 1536], P(('dp', 'expert'))
- new_w_shared_down_first: float32 [1024, 1536], P(('dp', 'expert'))
- new_w_shared_down_second: float32 [1024, 1536], P(('dp', 'expert'))
- grad_w_expert_gu: float32 [16, 1536, 1024], P('expert', 'dp')
- new_w_expert_gu: float32 [16, 1536, 1024], P('expert', 'dp')
- new_w_expert_gu_first: float32 [16, 1536, 1024], P('expert', 'dp')
- new_w_expert_gu_second: float32 [16, 1536, 1024], P('expert', 'dp')
- grad_w_expert_down: float32 [16, 512, 1536], P('expert', 'dp')
- new_w_expert_down: float32 [16, 512, 1536], P('expert', 'dp')
- new_w_expert_down_first: float32 [16, 512, 1536], P('expert', 'dp')
- new_w_expert_down_second: float32 [16, 512, 1536], P('expert', 'dp')
- grad_norm_gains: float32 [2, 1536], replicated
- change_norm_gains: float32 [2, 1536], replicated
- new_norm_gains_first: float32 [2, 1536], replicated
- new_norm_gains_second: float32 [2, 1536], replicated
- grad_conv_params: float32 [5, 3328], replicated
- change_conv_params: float32 [5, 3328], replicated
- new_conv_params_first: float32 [5, 3328], replicated
- new_conv_params_second: float32 [5, 3328], replicated
- grad_head_params: float32 [3, 48], replicated
- change_head_params: float32 [3, 48], replicated
- new_head_params_first: float32 [3, 48], replicated
- new_head_params_second: float32 [3, 48], replicated
- grad_mixer_gain: float32 [3072], replicated
- change_mixer_gain: float32 [3072], replicated
- new_mixer_gain_first: float32 [3072], replicated
- new_mixer_gain_second: float32 [3072], replicated
Inputs may be any that keep to these rules, and one draw needn't show every extreme that they name: `lengths`: each row lists one sequence's documents in order; they cover its 512 tokens. `routes`: the 6 ids of a row differ; among the 128 rows of one device no expert is named more than 64 times. `w_in_second`: positive. `w_out_second`: positive. `w_router_second`: positive. `w_shared_gu_second`: positive. `w_shared_down_second`: positive. `w_expert_gu_second`: positive. `w_expert_down_second`: positive. `norm_gains_second`: positive. `conv_params_second`: positive. `head_params_second`: positive. `mixer_gain_second`: positive.
All inputs are finite; a program needn't handle non-finite values.
Results may differ from a plain program's by a relative error of at most 0.029.
Values may be sent and summed in bfloat16 or wider, within the bound.
A program may use at most 640 MiB of HBM per device.

v0:
```python
import jax
import jax.numpy as jnp
from jax import lax
from jax.sharding import PartitionSpec as P

D = 1536
HEADS = 48
HEAD_DIM = 64
STATE = 128
CONV = 4
EXPERT_FF = 512
SHARED_FF = 1024
STEP = 3
INNER = 3072
CONV_DIM = 3328


norm_eps = 1e-05
beta_one = 0.9
beta_two = 0.95
adam_eps = 1e-08
learn_rate = 0.02
decay_rate = 0.1
highest = lax.Precision.HIGHEST


def from_behind(value, axis, steps):
    count = lax.axis_size(axis)
    first, last = (max(0, -steps), min(count, count - steps))
    return lax.ppermute(value, axis, [(source, source + steps) for source in range(first, last)])


def carried_in(part, axis, combine, identity):
    place = lax.axis_index(axis)
    gathered = jax.tree.map(lambda a: lax.all_gather(a, axis), part)
    state = jax.tree.map(lambda a, e: jnp.zeros_like(a) + jnp.asarray(e, a.dtype), part, identity)

    def one(turn, state):
        return combine(
            state, jax.tree.map(lambda a: lax.dynamic_index_in_dim(a, turn, 0, False), gathered)
        )

    return lax.fori_loop(0, place, one, state)


def carried_in_2(value, axis, combine, identity):
    count, position = (lax.axis_size(axis), lax.axis_index(axis))
    everything = jax.tree.map(
        lambda part, kind: lax.all_gather(part.astype(kind), axis),
        value,
        jax.tree.map(lambda a: jnp.bfloat16 if a.dtype == jnp.float32 else a.dtype, value),
    )
    start = jax.tree.map(
        lambda part, zero: jnp.broadcast_to(jnp.asarray(zero, part.dtype), part.shape),
        value,
        identity,
    )

    def turn(k, before):
        at = count - 1 - k
        reached = at > position
        new = combine(
            before, jax.tree.map(lambda part, own: part[at].astype(own.dtype), everything, value)
        )
        return jax.tree.map(lambda a, b: jnp.where(reached, a, b), new, before)

    return lax.fori_loop(0, count, turn, start)


def shortened(value):

    def short(part):
        return part.astype(jnp.bfloat16) if part.dtype == jnp.float32 else part

    return jax.tree.map(short, value)


def rms_scale(values):
    return lax.rsqrt(jnp.mean(values * values, axis=-1, keepdims=True) + norm_eps)


def silu_slope(values):
    sigmoid_value = jax.nn.sigmoid(values)
    return sigmoid_value * (1.0 + values * (1.0 - sigmoid_value))


def norm_back(grad_norm, unit_rows, scale_rows, gain):
    scaled = grad_norm * gain
    return scale_rows * (scaled - unit_rows * jnp.mean(scaled * unit_rows, axis=-1, keepdims=True))


def doc_ids(lengths_row, positions):
    starts = jnp.cumsum(lengths_row) - lengths_row
    return jnp.sum((starts[None, :] <= positions[:, None]).astype(jnp.int32), axis=1) - 1


def causal_conv(extended, conv_params, doc_ext, doc_index):
    length = doc_index.shape[0]
    summed = jnp.zeros_like(extended[CONV - 1 :]) + conv_params[CONV]
    for offset in range(CONV):
        start_row = CONV - 1 - offset
        usable = (doc_ext[start_row : start_row + length] == doc_index).astype(extended.dtype)
        summed = (
            summed
            + conv_params[offset] * extended[start_row : start_row + length] * usable[:, None]
        )
    return summed


def ssd_state(values, b_rows, dt_step, log_decay, doc_index):
    cumulated = jnp.cumsum(log_decay, axis=0)
    tail_weight = (
        jnp.exp(cumulated[-1][None, :] - cumulated)
        * (doc_index == doc_index[-1]).astype(cumulated.dtype)[:, None]
    )
    scaled = values * (dt_step * tail_weight)[:, :, None]
    return jnp.einsum("shp,sn->hpn", scaled, b_rows, precision=highest)


def ssd_carry(log_decay, doc_index, prior_doc):
    cumulated = jnp.cumsum(log_decay, axis=0)
    return jnp.exp(cumulated[-1]) * (doc_index[-1] == prior_doc).astype(cumulated.dtype)


def ssd_output(values, b_rows, c_rows, dt_step, log_decay, doc_index, prior_doc, state_in):
    length = values.shape[0]
    cumulated = jnp.cumsum(log_decay, axis=0)
    places = jnp.arange(length, dtype=jnp.int32)
    usable = (doc_index[:, None] == doc_index[None, :]) & (places[:, None] >= places[None, :])
    spread = cumulated.T[:, :, None] - cumulated.T[:, None, :]
    masked = jnp.exp(jnp.where(usable[None], spread, 0.0)) * usable[None].astype(cumulated.dtype)
    scores = jnp.dot(c_rows, b_rows.T, precision=highest)
    within = jnp.einsum(
        "hts,shp->thp", masked * scores[None], values * dt_step[:, :, None], precision=highest
    )
    inflow = jnp.exp(cumulated) * (doc_index == prior_doc).astype(cumulated.dtype)[:, None]
    carried = jnp.einsum("hpn,tn->thp", state_in, c_rows, precision=highest)
    return within + inflow[:, :, None] * carried


def route_slots(routes_blk, experts, capacity):
    flat_ids = routes_blk.reshape(-1)
    route_count = flat_ids.shape[0]
    onehot = (flat_ids[:, None] == jnp.arange(experts, dtype=jnp.int32)[None, :]).astype(jnp.int32)
    earlier = jnp.cumsum(onehot, axis=0) - onehot
    slot_ids = jnp.sum(earlier * onehot, axis=1)
    route_index = flat_ids * capacity + slot_ids
    slot_table = (
        jnp.full((experts * capacity,), route_count, jnp.int32)
        .at[route_index]
        .set(jnp.arange(route_count, dtype=jnp.int32))
    )
    return (route_index, slot_table)


def combine_state(earlier, later):
    return (earlier[0] * later[0], later[0][:, None, None] * earlier[1] + later[1])


def pack_owned(gradients, owners):
    return jnp.concatenate([gradient.reshape(owners, -1) for gradient in gradients], axis=1)


def unpack_owned(summed_row, gradients, owners):
    pieces = []
    start = 0
    for gradient in gradients:
        count = gradient.size // owners
        pieces.append(
            summed_row[0, start : start + count].reshape(
                gradient.shape[0] // owners, gradient.shape[1]
            )
        )
        start = start + count
    return pieces


def adam_step(weight, moment_one, moment_two, gradient):
    moment_one = beta_one * moment_one + (1.0 - beta_one) * gradient
    moment_two = beta_two * moment_two + (1.0 - beta_two) * gradient * gradient
    fixed_one = 1.0 - beta_one**STEP
    fixed_two = 1.0 - beta_two**STEP
    change = (
        moment_one / fixed_one / (jnp.sqrt(moment_two / fixed_two) + adam_eps) + decay_rate * weight
    )
    moved = -learn_rate * change
    return (gradient, weight + moved, moment_one, moment_two, moved)


def on_device(
    tokens,
    cotangent,
    lengths,
    routes,
    w_in,
    w_in_first,
    w_in_second,
    w_out,
    w_out_first,
    w_out_second,
    w_router,
    w_router_first,
    w_router_second,
    w_shared_gu,
    w_shared_gu_first,
    w_shared_gu_second,
    w_shared_down,
    w_shared_down_first,
    w_shared_down_second,
    w_expert_gu,
    w_expert_gu_first,
    w_expert_gu_second,
    w_expert_down,
    w_expert_down_first,
    w_expert_down_second,
    norm_gains,
    norm_gains_first,
    norm_gains_second,
    conv_params,
    conv_params_first,
    conv_params_second,
    head_params,
    head_params_first,
    head_params_second,
    mixer_gain,
    mixer_gain_first,
    mixer_gain_second,
):
    win_full, wout_full, router_full, sgu_full, sd_full = (
        lax.all_gather(w_in.astype(jnp.bfloat16), ("dp", "expert"), axis=0, tiled=True),
        lax.all_gather(w_out.astype(jnp.bfloat16), ("dp", "expert"), axis=0, tiled=True),
        lax.all_gather(w_router.astype(jnp.bfloat16), ("dp", "expert"), axis=0, tiled=True),
        lax.all_gather(w_shared_gu.astype(jnp.bfloat16), ("dp", "expert"), axis=0, tiled=True),
        lax.all_gather(w_shared_down.astype(jnp.bfloat16), ("dp", "expert"), axis=0, tiled=True),
    )
    egu_full, ed_full = (
        lax.all_gather(w_expert_gu.astype(jnp.bfloat16), "dp", axis=1, tiled=True),
        lax.all_gather(w_expert_down.astype(jnp.bfloat16), "dp", axis=1, tiled=True),
    )
    tok_count = tokens.shape[0]
    top_count = routes.shape[1]
    experts = router_full.shape[1]
    capacity = (4 * tok_count * top_count + 3 * experts - 1) // (3 * experts)
    groups = lax.axis_size("expert")
    owners = lax.axis_size("dp") * lax.axis_size("expert")
    shard_base = lax.axis_index("expert") * tok_count
    doc_index = doc_ids(lengths[0], shard_base + jnp.arange(tok_count, dtype=jnp.int32))
    doc_ext = doc_ids(
        lengths[0], shard_base - (CONV - 1) + jnp.arange(tok_count + CONV - 1, dtype=jnp.int32)
    )
    prior_doc = doc_ext[CONV - 2]
    inputs = tokens.astype(jnp.float32)
    scale_one = rms_scale(inputs)
    normed_one = inputs * scale_one
    normed = (normed_one * norm_gains[0]).astype(jnp.bfloat16)
    projected = jnp.dot(normed, win_full, preferred_element_type=jnp.float32)
    split_at = 2 * INNER + 2 * STATE
    packed = projected[:, :split_at].astype(jnp.bfloat16)
    dt_raw = projected[:, split_at:]
    gate_z = packed[:, :INNER].astype(jnp.float32)
    conv_in = packed[:, INNER:]
    conv_tail = from_behind(conv_in[tok_count - (CONV - 1) :], "expert", 1)
    extended = jnp.concatenate([conv_tail, conv_in], axis=0).astype(jnp.float32)
    conv_out = causal_conv(extended, conv_params, doc_ext, doc_index)
    mixed_in = jax.nn.silu(conv_out)
    values = mixed_in[:, :INNER].reshape(tok_count, HEADS, HEAD_DIM)
    b_rows = mixed_in[:, INNER : INNER + STATE]
    c_rows = mixed_in[:, INNER + STATE :]
    pre_step = dt_raw + head_params[1]
    dt_step = jax.nn.softplus(pre_step)
    rate_abs = jnp.exp(head_params[0])
    log_decay = -rate_abs * dt_step
    local_state = ssd_state(values, b_rows, dt_step, log_decay, doc_index)
    local_carry = ssd_carry(log_decay, doc_index, prior_doc)
    identity = (jnp.ones((HEADS,), jnp.float32), jnp.zeros((HEADS, HEAD_DIM, STATE), jnp.float32))
    state_in = carried_in((local_carry, local_state), "expert", combine_state, identity)[1]
    ssd_out = ssd_output(values, b_rows, c_rows, dt_step, log_decay, doc_index, prior_doc, state_in)
    skip_coef = head_params[2]
    full_y = (ssd_out + skip_coef[None, :, None] * values).reshape(tok_count, INNER)
    gate_act = jax.nn.silu(gate_z)
    gated_y = full_y * gate_act
    scale_mix = rms_scale(gated_y)
    normed_mix = gated_y * scale_mix
    mixer_act = (normed_mix * mixer_gain).astype(jnp.bfloat16)
    mixer_res = jnp.dot(mixer_act, wout_full, preferred_element_type=jnp.float32)
    hidden = inputs + mixer_res
    scale_two = rms_scale(hidden)
    two_unit = hidden * scale_two
    normed_two = (two_unit * norm_gains[1]).astype(jnp.bfloat16)
    logits = jnp.dot(normed_two, router_full, preferred_element_type=jnp.float32)
    picked = jnp.take_along_axis(logits, routes, axis=1)
    weights = jax.nn.softmax(picked, axis=-1)
    shared_gu = jnp.dot(normed_two, sgu_full, preferred_element_type=jnp.float32)
    shared_gate = shared_gu[:, :SHARED_FF]
    shared_up = shared_gu[:, SHARED_FF:]
    shared_silu = jax.nn.silu(shared_gate)
    shared_mid = (shared_silu * shared_up).astype(jnp.bfloat16)
    shared_out = jnp.dot(shared_mid, sd_full, preferred_element_type=jnp.float32)
    route_index, slot_table = route_slots(routes, experts, capacity)
    tok_index = slot_table // top_count
    padded_in = jnp.concatenate([normed_two, jnp.zeros((1, D), jnp.bfloat16)], axis=0)
    padded_grad = jnp.concatenate([cotangent, jnp.zeros((1, D), jnp.bfloat16)], axis=0)
    weight_flat = jnp.concatenate([weights.reshape(-1), jnp.zeros((1,), jnp.float32)])
    send_in = padded_in[tok_index].reshape(groups, -1, D)
    send_grad = (
        (padded_grad[tok_index].astype(jnp.float32) * weight_flat[slot_table][:, None])
        .astype(jnp.bfloat16)
        .reshape(groups, -1, D)
    )
    recv_in, recv_grad = (
        lax.all_to_all(send_in, "expert", split_axis=0, concat_axis=0, tiled=True),
        lax.all_to_all(send_grad, "expert", split_axis=0, concat_axis=0, tiled=True),
    )
    local_experts = egu_full.shape[0]
    recv_in = recv_in.reshape(groups, local_experts, capacity, D)
    recv_grad = recv_grad.reshape(groups, local_experts, capacity, D)
    gate_up = jnp.einsum("secd,edf->secf", recv_in, egu_full, preferred_element_type=jnp.float32)
    gate_part = gate_up[..., :EXPERT_FF]
    up_part = gate_up[..., EXPERT_FF:]
    gate_silu = jax.nn.silu(gate_part)
    middle = (gate_silu * up_part).astype(jnp.bfloat16)
    slot_out = jnp.einsum(
        "secf,efd->secd", middle, ed_full, preferred_element_type=jnp.float32
    ).astype(jnp.bfloat16)
    grad_mid = jnp.einsum("secd,efd->secf", recv_grad, ed_full, preferred_element_type=jnp.float32)
    grad_ed = jnp.einsum("secf,secd->efd", middle, recv_grad, preferred_element_type=jnp.float32)
    grad_gu = jnp.concatenate(
        [grad_mid * up_part * silu_slope(gate_part), grad_mid * gate_silu], axis=-1
    ).astype(jnp.bfloat16)
    grad_egu = jnp.einsum("secd,secf->edf", recv_in, grad_gu, preferred_element_type=jnp.float32)
    slot_back = jnp.einsum(
        "secf,edf->secd", grad_gu, egu_full, preferred_element_type=jnp.float32
    ).astype(jnp.bfloat16)
    ret_out, ret_back = (
        lax.all_to_all(
            slot_out.reshape(groups, -1, D), "expert", split_axis=0, concat_axis=0, tiled=True
        ),
        lax.all_to_all(
            slot_back.reshape(groups, -1, D), "expert", split_axis=0, concat_axis=0, tiled=True
        ),
    )
    chosen = (
        ret_out.reshape(-1, D)[route_index].reshape(tok_count, top_count, D).astype(jnp.float32)
    )
    back_rows = (
        ret_back.reshape(-1, D)[route_index].reshape(tok_count, top_count, D).astype(jnp.float32)
    )
    expert_mix = jnp.einsum("tk,tkd->td", weights, chosen)
    output = (hidden + shared_out + expert_mix).astype(jnp.bfloat16)
    grad_top = cotangent.astype(jnp.float32)
    grad_shared_mid = jnp.dot(cotangent, sd_full.T, preferred_element_type=jnp.float32)
    grad_sd = jnp.dot(shared_mid.T, cotangent, preferred_element_type=jnp.float32)
    grad_sgu_act = jnp.concatenate(
        [grad_shared_mid * shared_up * silu_slope(shared_gate), grad_shared_mid * shared_silu],
        axis=-1,
    ).astype(jnp.bfloat16)
    grad_sgu = jnp.dot(normed_two.T, grad_sgu_act, preferred_element_type=jnp.float32)
    grad_weights = jnp.einsum("td,tkd->tk", grad_top, chosen)
    grad_picked = weights * (grad_weights - jnp.sum(weights * grad_weights, axis=-1, keepdims=True))
    expert_ids = jnp.arange(experts, dtype=jnp.int32)
    grad_logits = jnp.sum(
        grad_picked[:, :, None]
        * (routes[:, :, None] == expert_ids[None, None, :]).astype(jnp.float32),
        axis=1,
    ).astype(jnp.bfloat16)
    grad_router = jnp.dot(normed_two.T, grad_logits, preferred_element_type=jnp.float32)
    grad_norm_two = (
        jnp.dot(grad_sgu_act, sgu_full.T, preferred_element_type=jnp.float32)
        + jnp.dot(grad_logits, router_full.T, preferred_element_type=jnp.float32)
        + jnp.sum(back_rows, axis=1)
    )
    grad_gain_two = jnp.sum(grad_norm_two * two_unit, axis=0)
    grad_hidden = grad_top + norm_back(grad_norm_two, two_unit, scale_two, norm_gains[1])
    hidden_low = grad_hidden.astype(jnp.bfloat16)
    grad_mix_act = jnp.dot(hidden_low, wout_full.T, preferred_element_type=jnp.float32)
    grad_out = jnp.dot(mixer_act.T, hidden_low, preferred_element_type=jnp.float32)
    side_list = (grad_out, grad_router, grad_sgu, grad_sd)
    grad_mixer_gain = jnp.sum(grad_mix_act * normed_mix, axis=0)
    grad_gated = norm_back(grad_mix_act, normed_mix, scale_mix, mixer_gain)
    grad_full_y = grad_gated * gate_act
    grad_gate_z = grad_gated * full_y * silu_slope(gate_z)
    grad_three = grad_full_y.reshape(tok_count, HEADS, HEAD_DIM)
    grad_skip = jnp.sum(grad_three * values, axis=(0, 2))
    inflow = (
        jnp.exp(jnp.cumsum(log_decay, axis=0))
        * (doc_index == prior_doc).astype(jnp.float32)[:, None]
    )
    state_grad = jnp.einsum(
        "thp,tn->hpn", grad_three * inflow[:, :, None], c_rows, precision=highest
    )
    later_grad = carried_in_2((local_carry, state_grad), "expert", combine_state, identity)[1]
    grad_carry = jnp.sum(state_in * later_grad, axis=(1, 2))

    def ssd_all(vals_in, b_in, c_in, step_in, decay_in, state_arg):
        return (
            ssd_output(vals_in, b_in, c_in, step_in, decay_in, doc_index, prior_doc, state_arg),
            ssd_state(vals_in, b_in, step_in, decay_in, doc_index),
            ssd_carry(decay_in, doc_index, prior_doc),
        )

    unused_out, pullback = jax.vjp(ssd_all, values, b_rows, c_rows, dt_step, log_decay, state_in)
    grad_vals, grad_b, grad_c, grad_step, grad_decay, ignored_state = pullback(
        (grad_three, later_grad, grad_carry)
    )
    grad_vals = grad_vals + grad_three * skip_coef[None, :, None]
    grad_step = grad_step - grad_decay * rate_abs
    grad_log_rate = jnp.sum(grad_decay * log_decay, axis=0)
    grad_pre = grad_step * jax.nn.sigmoid(pre_step)
    grad_bias = jnp.sum(grad_pre, axis=0)
    grad_mixed = jnp.concatenate([grad_vals.reshape(tok_count, INNER), grad_b, grad_c], axis=1)
    grad_conv = grad_mixed * silu_slope(conv_out)
    grad_conv_bias = jnp.sum(grad_conv, axis=0)
    grad_ext = jnp.zeros((tok_count + CONV - 1, CONV_DIM), jnp.float32)
    tap_grads = []
    for offset in range(CONV):
        start_row = CONV - 1 - offset
        usable = (doc_ext[start_row : start_row + tok_count] == doc_index).astype(jnp.float32)[
            :, None
        ]
        masked_grad = grad_conv * usable
        tap_grads.append(jnp.sum(masked_grad * extended[start_row : start_row + tok_count], axis=0))
        grad_ext = grad_ext + jnp.pad(
            conv_params[offset] * masked_grad, ((start_row, offset), (0, 0))
        )
    spill = from_behind(shortened(grad_ext[: CONV - 1]), "expert", -1)
    grad_conv_in = grad_ext[CONV - 1 :] + jnp.pad(spill, ((tok_count - (CONV - 1), 0), (0, 0)))
    grad_proj = jnp.concatenate([grad_gate_z, grad_conv_in, grad_pre], axis=1).astype(jnp.bfloat16)
    grad_in = jnp.dot(normed.T, grad_proj, preferred_element_type=jnp.float32)
    grad_norm_one = jnp.dot(grad_proj, win_full.T, preferred_element_type=jnp.float32)
    grad_gain_one = jnp.sum(grad_norm_one * normed_one, axis=0)
    grad_tokens = (
        grad_hidden + norm_back(grad_norm_one, normed_one, scale_one, norm_gains[0])
    ).astype(jnp.bfloat16)
    sum_gains, sum_conv, sum_head, sum_mixer = lax.psum(
        (
            jnp.stack([grad_gain_one, grad_gain_two]),
            jnp.concatenate([jnp.stack(tap_grads), grad_conv_bias[None]], axis=0),
            jnp.stack([grad_log_rate, grad_bias, grad_skip]),
            grad_mixer_gain,
        ),
        ("dp", "expert"),
    )
    sum_egu, sum_ed = (
        lax.psum_scatter(
            grad_egu.astype(jnp.bfloat16), "dp", scatter_dimension=1, tiled=True
        ).astype(jnp.float32),
        lax.psum_scatter(
            grad_ed.astype(jnp.bfloat16), "dp", scatter_dimension=1, tiled=True
        ).astype(jnp.float32),
    )
    dense_list = (grad_in,) + side_list
    dense_row = lax.psum_scatter(
        pack_owned(dense_list, owners), ("dp", "expert"), scatter_dimension=0, tiled=True
    )
    sum_in, sum_out, sum_router, sum_sgu, sum_sd = unpack_owned(dense_row, dense_list, owners)
    up_in = adam_step(w_in, w_in_first, w_in_second, sum_in)
    up_out = adam_step(w_out, w_out_first, w_out_second, sum_out)
    up_router = adam_step(w_router, w_router_first, w_router_second, sum_router)
    up_sgu = adam_step(w_shared_gu, w_shared_gu_first, w_shared_gu_second, sum_sgu)
    up_sd = adam_step(w_shared_down, w_shared_down_first, w_shared_down_second, sum_sd)
    up_egu = adam_step(w_expert_gu, w_expert_gu_first, w_expert_gu_second, sum_egu)
    up_ed = adam_step(w_expert_down, w_expert_down_first, w_expert_down_second, sum_ed)
    up_gains = adam_step(norm_gains, norm_gains_first, norm_gains_second, sum_gains)
    up_conv = adam_step(conv_params, conv_params_first, conv_params_second, sum_conv)
    up_head = adam_step(head_params, head_params_first, head_params_second, sum_head)
    up_mixer = adam_step(mixer_gain, mixer_gain_first, mixer_gain_second, sum_mixer)
    return (
        output,
        grad_tokens,
        up_in[0],
        up_in[1],
        up_in[2],
        up_in[3],
        up_out[0],
        up_out[1],
        up_out[2],
        up_out[3],
        up_router[0],
        up_router[1],
        up_router[2],
        up_router[3],
        up_sgu[0],
        up_sgu[1],
        up_sgu[2],
        up_sgu[3],
        up_sd[0],
        up_sd[1],
        up_sd[2],
        up_sd[3],
        up_egu[0],
        up_egu[1],
        up_egu[2],
        up_egu[3],
        up_ed[0],
        up_ed[1],
        up_ed[2],
        up_ed[3],
        up_gains[0],
        up_gains[4],
        up_gains[2],
        up_gains[3],
        up_conv[0],
        up_conv[4],
        up_conv[2],
        up_conv[3],
        up_head[0],
        up_head[4],
        up_head[2],
        up_head[3],
        up_mixer[0],
        up_mixer[4],
        up_mixer[2],
        up_mixer[3],
    )


def solution(mesh):
    return jax.shard_map(
        on_device,
        mesh=mesh,
        in_specs=(
            P(("dp", "expert"), None),
            P(("dp", "expert"), None),
            P("dp", None),
            P(("dp", "expert"), None),
            P(("dp", "expert"), None),
            P(("dp", "expert"), None),
            P(("dp", "expert"), None),
            P(("dp", "expert"), None),
            P(("dp", "expert"), None),
            P(("dp", "expert"), None),
            P(("dp", "expert"), None),
            P(("dp", "expert"), None),
            P(("dp", "expert"), None),
            P(("dp", "expert"), None),
            P(("dp", "expert"), None),
            P(("dp", "expert"), None),
            P(("dp", "expert"), None),
            P(("dp", "expert"), None),
            P(("dp", "expert"), None),
            P("expert", "dp", None),
            P("expert", "dp", None),
            P("expert", "dp", None),
            P("expert", "dp", None),
            P("expert", "dp", None),
            P("expert", "dp", None),
            P(),
            P(),
            P(),
            P(),
            P(),
            P(),
            P(),
            P(),
            P(),
            P(),
            P(),
            P(),
        ),
        out_specs=(
            P(("dp", "expert"), None),
            P(("dp", "expert"), None),
            P(("dp", "expert"), None),
            P(("dp", "expert"), None),
            P(("dp", "expert"), None),
            P(("dp", "expert"), None),
            P(("dp", "expert"), None),
            P(("dp", "expert"), None),
            P(("dp", "expert"), None),
            P(("dp", "expert"), None),
            P(("dp", "expert"), None),
            P(("dp", "expert"), None),
            P(("dp", "expert"), None),
            P(("dp", "expert"), None),
            P(("dp", "expert"), None),
            P(("dp", "expert"), None),
            P(("dp", "expert"), None),
            P(("dp", "expert"), None),
            P(("dp", "expert"), None),
            P(("dp", "expert"), None),
            P(("dp", "expert"), None),
            P(("dp", "expert"), None),
            P("expert", "dp", None),
            P("expert", "dp", None),
            P("expert", "dp", None),
            P("expert", "dp", None),
            P("expert", "dp", None),
            P("expert", "dp", None),
            P("expert", "dp", None),
            P("expert", "dp", None),
            P(),
            P(),
            P(),
            P(),
            P(),
            P(),
            P(),
            P(),
            P(),
            P(),
            P(),
            P(),
            P(),
            P(),
            P(),
            P(),
        ),
        check_vma=False,
    )
```

profile of v0, /device:TPU:0, one launch (start us, length us, event | category | flops | bytes accessed | tf_op | source)
XLA Modules:
  0.0 2201.8 jit_solution(5223882220801345550)
XLA Ops:
  15.5 128.9 %all-gather.14.cloned.1.call-done = bf16[1536,6448]{1,0:T(8,128)(2,1)} async-done(((bf16[48,6448]{1,0:T(8,128)(2,1)}), bf16[1536,6448]{1,0:T(8,128)(2,1)}) %all-gather.14.cloned.1.call-update) | async-done | bytes 19808272 | tf_op jit(solution)/shard_map/all_gather | solution.py:230
  144.5 13.8 fusion.196
  158.9 3.3 collective-permute-start
  166.7 5.9 fusion.48
  187.8 3.8 scatter_custom_fusion
  193.7 8.0 all-gather.2
  203.5 41.4 %all-gather.26.cloned.1.call-done = f32[192,64,128]{2,1,0:T(8,128)} async-done(((f32[48,64,128]{2,1,0:T(8,128)}), f32[192,64,128]{2,1,0:T(8,128)}) %all-gather.26.cloned.1.call-update) | async-done | bytes 6291472 | tf_op jit(solution)/shard_map/all_gather | solution.py:35
  248.1 6.4 fusion.60
  256.9 73.6 %all-gather.16.cloned.1.call-done = bf16[3072,1536]{1,0:T(8,128)(2,1)} async-done(((bf16[96,1536]{1,0:T(8,128)(2,1)}), bf16[3072,1536]{1,0:T(8,128)(2,1)}) %all-gather.16.cloned.1.call-update) | async-done | bytes 9437200 | tf_op jit(solution)/shard_map/all_gather | solution.py:231
  330.5 5.3 multiply_reduce_fusion.14
  336.9 5.6 gather_fusion
  342.5 3.9 all-to-all-start
  346.4 101.5 %all-gather.22.cloned.1.call-done = bf16[4,1536,1024]{2,1,0:T(8,128)(2,1)} async-done(((bf16[4,192,1024]{2,1,0:T(8,128)(2,1)}), bf16[4,1536,1024]{2,1,0:T(8,128)(2,1)}) %all-gather.22.cloned.1.call-update) | async-done | bytes 12582928 | tf_op jit(solution)/shard_map/all_gather | solution.py:237
  449.6 6.4 fusion.35
  458.6 54.2 %all-gather.24.cloned.1.call-done = bf16[4,512,1536]{2,1,0:T(8,128)(2,1)} async-done(((bf16[4,64,1536]{2,1,0:T(8,128)(2,1)}), bf16[4,512,1536]{2,1,0:T(8,128)(2,1)}) %all-gather.24.cloned.1.call-update) | async-done | bytes 6291472 | tf_op jit(solution)/shard_map/all_gather | solution.py:238
  512.9 4.6 fusion.16
  519.3 4.8 all-to-all-start.1
  524.9 98.6 %all-gather.3 = bf16[32,48,16]{1,2,0:T(8,128)(2,1)S(1)} all-gather(bf16[1,48,16]{1,2,0:T(8,128)(2,1)S(1)} %convert_bitcast_fusion), channel_id=1, replica_groups=mesh['dp'=8,'expert'=4] {'dp','expert'}, dimensions={0}, use_global_device_ids=true | all-gather | bytes 50688 | tf_op jit(solution)/shard_map/all_gather | solution.py:232
  624.1 5.6 gather_fusion.2
  629.9 5.1 gather_fusion.5
  635.8 8.2 gather_fusion.1
  644.0 3.5 reshape.454
  647.6 3.7 fusion.110
  654.7 5.1 gather_fusion.3
  662.6 35.3 %all_to_all.20 = bf16[4,256,1536]{2,1,0:T(8,128)(2,1)S(1)} all-to-all(bf16[4,256,1536]{2,1,0:T(8,128)(2,1)S(1)} %fusion.5), channel_id=1, replica_groups=mesh['dp'=8,'expert'=4] {'expert'}, dimensions={0} | all-to-all | bytes 6291456 | tf_op jit(solution)/shard_map/all_to_all | solution.py:312
  697.9 3.8 fusion.41
  701.7 8.7 fusion.19
  712.4 3.7 all-to-all-start.3
  716.6 4.7 fusion.197
  721.3 4.3 multiply_convert_fusion.4
  729.4 17.2 all-to-all-done.3
  746.6 3.9 gather_fusion.4
  750.6 4.9 reshape.469
  755.5 4.8 reduce_sum.335
  762.8 6.9 multiply_reduce_fusion.5
  769.7 4.4 multiply_reduce_fusion.6
  776.7 6.4 bitcast_convert_fusion.2
  783.1 7.9 all-gather.4
  791.6 7.5 fusion.124
  799.2 9.9 reshape.464
  809.1 4.7 fusion.200
  813.8 6.2 reshape.465
  823.3 10.5 bitcast_convert_fusion.1
  834.7 4.6 fusion.26
  839.4 8.0 fusion.46
  852.5 8.2 fusion.127
  860.7 21.5 reshape.462
  883.4 6.8 while.29
  891.6 3.3 fusion.96
  895.0 4.6 multiply_reduce_fusion.9
  904.6 10.0 multiply_reduce_fusion.1
  932.2 16.0 fusion.119
  948.2 52.6 %reshape.461 = f32[32,309504]{1,0:T(8,128)} reshape(f32[1536,6448]{1,0:T(8,128)} %fusion.119) | data formatting | bytes 79233024 | tf_op jit(solution)/shard_map/reshape | solution.py:161
  1000.8 28.6 %constant_dynamic-update-slice_fusion.4 = f32[32,605184]{1,0:T(8,128)} fusion(f32[32,309504]{1,0:T(8,128)} %reshape.461), kind=kLoop, calls=%fused_computation.270 | loop fusion | bytes 79233024
  1029.4 12.7 constant_dynamic-update-slice_fusion.3
  1042.8 10.0 constant_dynamic-update-slice_fusion.1
  1062.2 19.7 fusion.108
  1081.9 39.6 %all-reduce.9 = (f32[2,1536]{1,0:T(2,128)S(1)}, f32[3,48]{1,0:T(4,128)S(1)}, f32[3072]{0:T(1024)S(1)}) all-reduce(f32[2,1536]{1,0:T(2,128)S(1)} %pad_maximum_fusion.7, f32[3,48]{1,0:T(4,128)S(1)} %pad_maximum_fusion.9, f32[3072]{0:T(1024)S(1)} %copy-done.115), channel_id=1, replica_groups=mesh['dp'=8,'expert'=4] {'dp','expert'}, use_global_device_ids=true, to_apply=%region_39.40 | all-reduce | flops 6288 | bytes 50304 | tf_op jit(solution)/shard_map/psum | solution.py:434
  1125.6 6.1 multiply_add_fusion.3
  1131.8 7.3 multiply_add_fusion
  1139.1 1014.5 %all-reduce.13.cloned.1.call-done = (f32[32,605184]{1,0:T(8,128)}, f32[5,3328]{1,0:T(8,128)}) async-done(((f32[32,605184]{1,0:T(8,128)}, f32[5,3328]{1,0:T(8,128)}), (f32[32,605184]{1,0:T(8,128)}, f32[5,3328]{1,0:T(8,128)})) %all-reduce.13.cloned.1.call-update) | async-done | bytes 77530128
  2153.6 14.7 dynamic-slice_reduce_fusion
  2169.0 8.4 dynamic-slice_reduce_fusion.1
  2184.8 4.3 multiply_add_fusion.5
  (576 shorter events, 131.1 us)
Async XLA Ops:
  7.3 137.2 %all-gather.14.cloned.1.call-start = ((), (), s32[]{:S(2)}) async-start(), calls=%async_computation.6 | async-start | bytes 20680704 | tf_op jit(solution)/shard_map/all_gather | solution.py:230
  9.6 235.3 %all-gather.26.cloned.1.call-start = ((), (), s32[]{:S(2)}) async-start(), calls=%async_computation.14 | async-start | bytes 7864320 | tf_op jit(solution)/shard_map/all_gather | solution.py:35
  10.6 147.6 %copy-start.181 = (s32[128]{0:T(128)}, s32[128]{0:T(128)S(1)}, u32[]{:S(2)}) copy-start(s32[128]{0:T(128)S(1)} %broadcast_add_fusion.1) | copy-start | bytes 1540
  13.2 145.1 %copy-start.66 = (f32[1536]{0:T(1024)}, f32[1536]{0:T(1024)S(1)}, u32[]{:S(2)}) copy-start(f32[1536]{0:T(1024)S(1)} %get-tuple-element.448) | copy-start | bytes 18436
  13.4 153.3 %copy-start.92 = (f32[3328]{0:T(1024)}, f32[3328]{0:T(1024)S(1)}, u32[]{:S(2)}) copy-start(f32[3328]{0:T(1024)S(1)} %get-tuple-element.443) | copy-start | bytes 39940
  13.4 153.3 %copy-start.94 = (f32[3328]{0:T(1024)}, f32[3328]{0:T(1024)S(1)}, u32[]{:S(2)}) copy-start(f32[3328]{0:T(1024)S(1)} %get-tuple-element.444) | copy-start | bytes 39940
  13.4 153.3 %copy-start.96 = (f32[3328]{0:T(1024)}, f32[3328]{0:T(1024)S(1)}, u32[]{:S(2)}) copy-start(f32[3328]{0:T(1024)S(1)} %get-tuple-element.445) | copy-start | bytes 39940
  13.4 153.3 %copy-start.98 = (f32[3328]{0:T(1024)}, f32[3328]{0:T(1024)S(1)}, u32[]{:S(2)}) copy-start(f32[3328]{0:T(1024)S(1)} %get-tuple-element.446) | copy-start | bytes 39940
  13.6 144.7 %copy-start.135 = (f32[128]{0:T(128)}, f32[128]{0:T(128)S(1)}, u32[]{:S(2)}) copy-start(f32[128]{0:T(128)S(1)} %add_rsqrt_fusion.2) | copy-start | bytes 1540
  14.1 148.1 %copy-start.166 = (f32[48]{0:T(128)}, f32[48]{0:T(128)S(1)}, u32[]{:S(2)}) copy-start(f32[48]{0:T(128)S(1)} %get-tuple-element.546) | copy-start | bytes 580
  15.5 149.1 %copy-start.149 = (f32[128]{0:T(128)}, f32[128]{0:T(128)S(1)}, u32[]{:S(2)}) copy-start(f32[128]{0:T(128)S(1)} %get-tuple-element.555) | copy-start | bytes 1540
  15.5 149.1 %copy-start.168 = (f32[128]{0:T(128)}, f32[128]{0:T(128)S(1)}, u32[]{:S(2)}) copy-start(f32[128]{0:T(128)S(1)} %get-tuple-element.552) | copy-start | bytes 1540
  15.5 151.2 %copy-start.152 = (f32[128]{0:T(128)}, f32[128]{0:T(128)S(1)}, u32[]{:S(2)}) copy-start(f32[128]{0:T(128)S(1)} %get-tuple-element.548) | copy-start | bytes 1540
  15.5 151.2 %copy-start.154 = (f32[128]{0:T(128)}, f32[128]{0:T(128)S(1)}, u32[]{:S(2)}) copy-start(f32[128]{0:T(128)S(1)} %get-tuple-element.549) | copy-start | bytes 1540
  15.5 151.2 %copy-start.156 = (f32[128]{0:T(128)}, f32[128]{0:T(128)S(1)}, u32[]{:S(2)}) copy-start(f32[128]{0:T(128)S(1)} %get-tuple-element.550) | copy-start | bytes 1540
  15.5 151.2 %copy-start.158 = (f32[128]{0:T(128)}, f32[128]{0:T(128)S(1)}, u32[]{:S(2)}) copy-start(f32[128]{0:T(128)S(1)} %get-tuple-element.551) | copy-start | bytes 1540
  158.9 6.5 collective-permute-start
  172.8 75.2 %copy-start.10 = (f32[128,3072]{0,1:T(8,128)}, f32[128,3072]{0,1:T(8,128)S(1)}, u32[]{:S(2)}) copy-start(f32[128,3072]{0,1:T(8,128)S(1)} %slice.209) | copy-start | bytes 4718596
  176.4 154.1 %all-gather.16.cloned.1.call-start = ((), (), s32[]{:S(2)}) async-start(), calls=%async_computation.7 | async-start | bytes 9732096 | tf_op jit(solution)/shard_map/all_gather | solution.py:231
  177.3 270.6 %all-gather.22.cloned.1.call-start = ((), (), s32[]{:S(2)}) async-start(), calls=%async_computation.10 | async-start | bytes 14155776 | tf_op jit(solution)/shard_map/all_gather | solution.py:237
  180.6 332.2 %all-gather.24.cloned.1.call-start = ((), (), s32[]{:S(2)}) async-start(), calls=%async_computation.11 | async-start | bytes 7077888 | tf_op jit(solution)/shard_map/all_gather | solution.py:238
  183.2 10.5 copy-start.179
  183.2 533.3 %all-gather.18.cloned.1.call-start = ((), (), s32[]{:S(2)}) async-start(), calls=%async_computation.8 | async-start | bytes 6488064 | tf_op jit(solution)/shard_map/all_gather | solution.py:233
  187.8 57.3 %copy-start.137 = (s32[768]{0:T(1024)}, s32[768]{0:T(1024)S(1)}, u32[]{:S(2)}) copy-start(s32[768]{0:T(1024)S(1)} %fusion.165) | copy-start | bytes 9220
  254.6 75.9 %copy-start.61 = (f32[3072]{0:T(1024)S(1)}, f32[3072]{0:T(1024)}, u32[]{:S(2)}) copy-start(f32[3072]{0:T(1024)} %param.75) | copy-start | bytes 36868
  256.9 78.9 %copy-start.3 = (f32[128,3072]{0,1:T(8,128)}, f32[128,3072]{0,1:T(8,128)S(1)}, u32[]{:S(2)}) copy-start(f32[128,3072]{0,1:T(8,128)S(1)} %get-tuple-element.519) | copy-start | bytes 4718596
  256.9 78.9 %copy-start.132 = (f32[128]{0:T(128)}, f32[128]{0:T(128)S(1)}, u32[]{:S(2)}) copy-start(f32[128]{0:T(128)S(1)} %add_rsqrt_fusion.1) | copy-start | bytes 1540
  342.5 105.4 %all-to-all-start = ((bf16[4,256,1536]{2,1,0:T(8,128)(2,1)}), bf16[4,256,1536]{2,1,0:T(8,128)(2,1)S(1)}, u32[]{:S(2)}, u32[]{:S(2)}) async-start(bf16[4,256,1536]{2,1,0:T(8,128)(2,1)} %bitcast.240), calls=%async_computation | async-start | bytes 6291456 | tf_op jit(solution)/shard_map/all_to_all | solution.py:311
  458.6 58.8 %copy-start.35 = (bf16[4,4,64,512]{3,2,0,1:T(8,128)(2,1)}, bf16[4,4,64,512]{3,2,0,1:T(8,128)(2,1)S(1)}, u32[]{:S(2)}) copy-start(bf16[4,4,64,512]{3,2,0,1:T(8,128)(2,1)S(1)} %multiply_convert_fusion) | copy-start | bytes 3145732
  519.3 104.7 %copy-start.39 = (bf16[128,1536]{1,0:T(8,128)(2,1)S(1)}, bf16[128,1536]{1,0:T(8,128)(2,1)}, u32[]{:S(2)}) copy-start(bf16[128,1536]{1,0:T(8,128)(2,1)} %param.42) | copy-start | bytes 1179652
  519.3 116.5 %all-to-all-start.1 = ((bf16[4,256,1536]{2,1,0:T(8,128)(2,1)}), bf16[4,256,1536]{2,1,0:T(8,128)(2,1)}, u32[]{:S(2)}, u32[]{:S(2)}) async-start(bf16[4,256,1536]{2,1,0:T(8,128)(2,1)} %bitcast.30), calls=%async_computation.1 | async-start | bytes 6291456 | tf_op jit(solution)/shard_map/all_to_all | solution.py:335
  524.1 99.9 %copy-start.123 = (s32[1024]{0:T(1024)S(1)}, s32[1024]{0:T(1024)}, u32[]{:S(2)}) copy-start(s32[1024]{0:T(1024)} %get-tuple-element.543) | copy-start | bytes 12292
  524.1 197.2 %all-gather.20.cloned.1.call-start = ((), (), s32[]{:S(2)}) async-start(), calls=%async_computation.9 | async-start | bytes 3244032 | tf_op jit(solution)/shard_map/all_gather | solution.py:234
  654.7 43.2 %slice-start.2 = ((s8[6291456]{0:T(1024)(128)(4,1)}), s8[2097152]{0:T(1024)(128)(4,1)S(1)}, s32[]{:S(2)}) async-start(s8[6291456]{0:T(1024)(128)(4,1)} %bitcast.243), calls=%async_computation.19 | async-start | bytes 4194304
  659.8 38.1 %slice-start.3 = ((s8[6291456]{0:T(1024)(128)(4,1)}), s8[4194304]{0:T(1024)(128)(4,1)S(1)}, s32[]{:S(2)}) async-start(s8[6291456]{0:T(1024)(128)(4,1)} %bitcast.243), calls=%async_computation.20 | async-start | bytes 8388608
  662.6 35.3 %copy-start.38 = (f32[4,4,64,1024]{3,2,0,1:T(8,128)S(1)}, f32[4,4,64,1024]{3,2,0,1:T(8,128)}, u32[]{:S(2)}) copy-start(f32[4,4,64,1024]{3,2,0,1:T(8,128)} %copy-done.37) | copy-start | bytes 12582916
  712.4 34.3 %all-to-all-start.3 = ((bf16[4,256,1536]{2,1,0:T(8,128)(2,1)}), bf16[4,256,1536]{2,1,0:T(8,128)(2,1)S(1)}, u32[]{:S(2)}, u32[]{:S(2)}) async-start(bf16[4,256,1536]{2,1,0:T(8,128)(2,1)} %bitcast.239), calls=%async_computation.3 | async-start | bytes 6291456 | tf_op jit(solution)/shard_map/all_to_all | solution.py:338
  716.1 167.3 %all-gather.28.cloned.1.call-start = ((), (), s32[]{:S(2)}) async-start(), calls=%async_computation.15 | async-start | bytes 3932160 | tf_op jit(solution)/shard_map/all_gather | solution.py:49
  774.1 65.2 %copy-start.7 = (f32[128,3072]{0,1:T(8,128)}, f32[128,3072]{0,1:T(8,128)S(1)}, u32[]{:S(2)}) copy-start(f32[128,3072]{0,1:T(8,128)S(1)} %get-tuple-element.489) | copy-start | bytes 4718596
  776.4 349.2 %reduce-scatter.5.cloned.1.call-start = ((), (), s32[]{:S(2)}) async-start(), calls=%async_computation.13 | async-start | bytes 7077888 | tf_op jit(solution)/shard_map/reduce_scatter | solution.py:447
  783.1 348.7 %reduce-scatter.3.cloned.1.call-start = ((), (), s32[]{:S(2)}) async-start(), calls=%async_computation.12 | async-start | bytes 14155776 | tf_op jit(solution)/shard_map/reduce_scatter | solution.py:444
  833.9 1319.7 %all-reduce.13.cloned.1.call-start = ((), (), s32[]{:S(2)}) async-start(), calls=%async_computation.16 | async-start | bytes 155140096
  847.4 34.9 %copy-start.83 = (f32[128,128]{1,0:T(8,128)}, f32[128,128]{1,0:T(8,128)S(1)}, u32[]{:S(2)}) copy-start(f32[128,128]{1,0:T(8,128)S(1)} %get-tuple-element.432) | copy-start | bytes 196612
  860.7 22.6 %copy-start.183 = (bf16[4,1,48]{2,0,1:T(4,128)(2,1)S(1)}, bf16[4,1,48]{2,0,1:T(4,128)(2,1)}, u32[]{:S(2)}) copy-start(bf16[4,1,48]{2,0,1:T(4,128)(2,1)} %copy.322) | copy-start | bytes 1156
  904.6 10.1 copy-start.93
  904.6 10.1 copy-start.95
  904.6 10.1 copy-start.97
  922.2 5.7 collective-permute-start.1
  948.2 104.6 %slice-start = ((s8[6291456]{0:T(1024)(128)(4,1)}), s8[2097152]{0:T(1024)(128)(4,1)S(1)}, s32[]{:S(2)}) async-start(s8[6291456]{0:T(1024)(128)(4,1)} %bitcast.232), calls=%async_computation.17 | async-start | bytes 4194304
  1000.8 51.9 %slice-start.1 = ((s8[6291456]{0:T(1024)(128)(4,1)}), s8[4194304]{0:T(1024)(128)(4,1)S(1)}, s32[]{:S(2)}) async-start(s8[6291456]{0:T(1024)(128)(4,1)} %bitcast.232), calls=%async_computation.18 | async-start | bytes 8388608
  1029.4 12.7 copy-start.71
  1062.0 19.8 copy-start.115
  1062.1 59.5 %copy-start.163 = (f32[3,48]{1,0:T(4,128)S(1)}, f32[3,48]{1,0:T(4,128)}, u32[]{:S(2)}) copy-start(f32[3,48]{1,0:T(4,128)} %param.72) | copy-start | bytes 1732
  1062.1 59.5 %copy-start.176 = (f32[3,48]{1,0:T(4,128)S(1)}, f32[3,48]{1,0:T(4,128)}, u32[]{:S(2)}) copy-start(f32[3,48]{1,0:T(4,128)} %param.73) | copy-start | bytes 1732
  1062.1 59.4 %copy-start.177 = (f32[3,48]{1,0:T(4,128)S(1)}, f32[3,48]{1,0:T(4,128)}, u32[]{:S(2)}) copy-start(f32[3,48]{1,0:T(4,128)} %param.74) | copy-start | bytes 1732
  1062.1 60.0 %copy-start.141 = (f32[3072]{0:T(1024)S(1)}, f32[3072]{0:T(1024)}, u32[]{:S(2)}) copy-start(f32[3072]{0:T(1024)} %param.76) | copy-start | bytes 36868
  1062.1 60.0 %copy-start.142 = (f32[3072]{0:T(1024)S(1)}, f32[3072]{0:T(1024)}, u32[]{:S(2)}) copy-start(f32[3072]{0:T(1024)} %param.77) | copy-start | bytes 36868
  1062.1 60.7 %copy-start.118 = (f32[2,1536]{1,0:T(2,128)S(1)}, f32[2,1536]{1,0:T(2,128)}, u32[]{:S(2)}) copy-start(f32[2,1536]{1,0:T(2,128)} %param.66) | copy-start | bytes 36868
  1062.1 60.6 %copy-start.143 = (f32[2,1536]{1,0:T(2,128)S(1)}, f32[2,1536]{1,0:T(2,128)}, u32[]{:S(2)}) copy-start(f32[2,1536]{1,0:T(2,128)} %param.67) | copy-start | bytes 36868
  1062.1 60.6 %copy-start.144 = (f32[2,1536]{1,0:T(2,128)S(1)}, f32[2,1536]{1,0:T(2,128)}, u32[]{:S(2)}) copy-start(f32[2,1536]{1,0:T(2,128)} %param.68) | copy-start | bytes 36868
  1062.2 61.3 %copy-start.20 = (f32[128,1536]{1,0:T(8,128)S(1)}, f32[128,1536]{1,0:T(8,128)}, u32[]{:S(2)}) copy-start(f32[128,1536]{1,0:T(8,128)} %copy-done.18) | copy-start | bytes 2359300
  1121.5 10.3 copy-start.178
  2169.0 15.7 copy-start.34
  2179.4 11.4 copy-start.127
  (141 other events, 522.7 us)
Sparse Core Ops, SparseCore 0:
  11.6 132.8 all-gather.13
  176.5 68.3 all-gather.25
  248.4 82.0 all-gather.15
  332.5 115.3 all-gather.21
  449.9 62.8 all-gather.23
  516.2 85.8 all-gather.17
  605.5 57.7 all-gather.19
  776.5 41.1 all-gather.27
  820.1 69.7 reduce-scatter.4
  892.1 127.5 reduce-scatter.2
  1056.0 1097.4 all-reduce.12
where the time goes:
time: 2210 us; the launch traced here: 2200 us
  waiting for transfers between devices  1430 us (65%)
  local copies, waits for them, and re-layouts  255 us (12%)
  blocking collectives  189 us (9%)
  matrix products  186 us (8%)
  other arithmetic  101 us (5%)
    unnamed x12, waiting for transfers between devices  1010 us
    all_gather x1, waiting for transfers between devices, on_device(): lax.all_gather(w_in.astype(jnp.bfloat16), ('dp', 'expert'), axis=0, tiled...  129 us
    all_gather x1, waiting for transfers between devices, on_device(): lax.all_gather(w_expert_gu.astype(jnp.bfloat16), 'dp', axis=1, tiled=True)  102 us
    all_gather x1, blocking collectives, on_device(): lax.all_gather(w_router.astype(jnp.bfloat16), ('dp', 'expert'), axis=0, t...  98.6 us
    reshape x5, local copies, waits for them, and re-layouts, pack_owned(): gradient.reshape(owners, -1)  92.4 us
    all_gather x1, waiting for transfers between devices, on_device(): lax.all_gather(w_out.astype(jnp.bfloat16), ('dp', 'expert'), axis=0, tile...  73.6 us
    unnamed x387, local copies, waits for them, and re-layouts  69 us
    all_gather x1, waiting for transfers between devices, on_device(): lax.all_gather(w_expert_down.astype(jnp.bfloat16), 'dp', axis=1, tiled=True)  54.2 us
  transfers between devices with their start and end apart: 16, of which 8 were waited for; matrix products, arithmetic and copies ran while one was open for 20% of the time, Pallas kernels for 0%

commit v1 on v0

v1 whole, which is shorter than its diff:
```python
import jax
import jax.numpy as jnp
from jax import lax
from jax.sharding import PartitionSpec as P

D = 1536
HEADS = 48
HEAD_DIM = 64
STATE = 128
CONV = 4
EXPERT_FF = 512
SHARED_FF = 1024
STEP = 3
INNER = 3072
CONV_DIM = 3328
LANES = 128

norm_eps = 1e-05
beta_one = 0.9
beta_two = 0.95
adam_eps = 1e-08
learn_rate = 0.02
decay_rate = 0.1
highest = lax.Precision.HIGHEST
bf16 = jnp.bfloat16
f32 = jnp.float32


def dot(left, right):
    return jnp.dot(left, right, preferred_element_type=f32)


def dot_nt(left, right):
    return lax.dot_general(left, right, (((1,), (1,)), ((), ())), preferred_element_type=f32)


def dot_tn(left, right):
    return lax.dot_general(left, right, (((0,), (0,)), ((), ())), preferred_element_type=f32)


def swap(pieces, axis):
    return lax.all_to_all(pieces, axis, split_axis=0, concat_axis=0, tiled=True)


def spread(block, axis):
    count = lax.axis_size(axis)
    return swap(jnp.broadcast_to(block[None], (count,) + block.shape), axis)


def rms_scale(values):
    return lax.rsqrt(jnp.mean(values * values, axis=-1, keepdims=True) + norm_eps)


def silu_slope(values):
    sigmoid_value = jax.nn.sigmoid(values)
    return sigmoid_value * (1.0 + values * (1.0 - sigmoid_value))


def norm_back(grad_norm, unit_rows, scale_rows, gain):
    scaled = grad_norm * gain
    return scale_rows * (scaled - unit_rows * jnp.mean(scaled * unit_rows, axis=-1, keepdims=True))


def adam_step(weight, moment_one, moment_two, gradient):
    moment_one = beta_one * moment_one + (1.0 - beta_one) * gradient
    moment_two = beta_two * moment_two + (1.0 - beta_two) * gradient * gradient
    fixed_one = 1.0 - beta_one**STEP
    fixed_two = 1.0 - beta_two**STEP
    change = (
        moment_one / fixed_one / (jnp.sqrt(moment_two / fixed_two) + adam_eps) + decay_rate * weight
    )
    moved = -learn_rate * change
    return (gradient, weight + moved, moment_one, moment_two, moved)


def split_words(value):
    high = value.astype(bf16)
    rest = value - high.astype(f32)
    mid = rest.astype(bf16)
    low = (rest - mid.astype(f32)).astype(bf16)
    return high, mid, low


def join_words(words):
    return words[0].astype(f32) + words[1].astype(f32) + words[2].astype(f32)


def conv_taps(same_doc, length):
    return [same_doc[:, offset][:, None] for offset in range(CONV)]


def shifted(array, offset):
    if offset == 0:
        return array
    if offset > 0:
        return jnp.pad(array[:-offset], ((offset, 0), (0, 0)))
    return jnp.pad(array[-offset:], ((0, -offset), (0, 0)))


def ssd_forward(values, b_rows, c_rows, dt_step, cum, usable):
    heads = dt_step.shape[1]
    scores = dot_nt(c_rows.astype(bf16), b_rows.astype(bf16))
    diff = cum.T[:, :, None] - cum.T[:, None, :]
    decay = jnp.exp(jnp.where(usable[None], diff, -1e30))
    mixed = (decay * scores[None]).astype(bf16)
    scaled = (values.reshape(-1, heads, HEAD_DIM) * dt_step[:, :, None]).astype(bf16)
    out = jnp.einsum("hts,shp->thp", mixed, scaled, preferred_element_type=f32)
    return out.reshape(values.shape)


def ssd_backward(grad_y, values, b_rows, c_rows, dt_step, cum, usable):
    heads = dt_step.shape[1]
    b_low, c_low = b_rows.astype(bf16), c_rows.astype(bf16)
    scores = dot_nt(c_low, b_low)
    diff = cum.T[:, :, None] - cum.T[:, None, :]
    decay = jnp.exp(jnp.where(usable[None], diff, -1e30))
    mixed = decay * scores[None]
    vals = values.reshape(-1, heads, HEAD_DIM)
    scaled = (vals * dt_step[:, :, None]).astype(bf16)
    gy = grad_y.reshape(-1, heads, HEAD_DIM).astype(bf16)
    grad_scaled = jnp.einsum("hts,thp->shp", mixed.astype(bf16), gy, preferred_element_type=f32)
    grad_mixed = jnp.einsum("thp,shp->hts", gy, scaled, preferred_element_type=f32)
    grad_scores = jnp.sum(grad_mixed * decay, axis=0).astype(bf16)
    product = grad_mixed * mixed
    grad_cum = (jnp.sum(product, axis=2) - jnp.sum(product, axis=1)).T
    grad_c = dot(grad_scores, b_low)
    grad_b = dot_tn(grad_scores, c_low)
    grad_vals = grad_scaled * dt_step[:, :, None]
    grad_step = jnp.sum(grad_scaled * vals, axis=2)
    return grad_vals.reshape(values.shape), grad_b, grad_c, grad_step, grad_cum


def on_device(
    tokens, cotangent, lengths, routes,
    w_in, w_in_first, w_in_second,
    w_out, w_out_first, w_out_second,
    w_router, w_router_first, w_router_second,
    w_shared_gu, w_shared_gu_first, w_shared_gu_second,
    w_shared_down, w_shared_down_first, w_shared_down_second,
    w_expert_gu, w_expert_gu_first, w_expert_gu_second,
    w_expert_down, w_expert_down_first, w_expert_down_second,
    norm_gains, norm_gains_first, norm_gains_second,
    conv_params, conv_params_first, conv_params_second,
    head_params, head_params_first, head_params_second,
    mixer_gain, mixer_gain_first, mixer_gain_second,
):
    groups = lax.axis_size("expert")
    copies = lax.axis_size("dp")
    place = lax.axis_index("expert")
    tok = tokens.shape[0]
    length = tok * groups
    top = routes.shape[1]
    experts = w_router.shape[1]
    own_experts = w_expert_gu.shape[0]
    capacity = (4 * tok * top + 3 * experts - 1) // (3 * experts)
    inner = INNER // groups
    heads = HEADS // groups
    rows_in = w_in.shape[0]
    rows_out = w_out.shape[0]
    rows_sd = w_shared_down.shape[0]
    own_ff = SHARED_FF // groups
    per_pair = copies // groups
    conv_cols = inner + 2 * STATE
    body = 2 * inner + 2 * STATE

    w_in_low = w_in.astype(bf16)
    z_cols = w_in_low[:, :INNER].reshape(rows_in, groups, inner)
    x_cols = w_in_low[:, INNER : 2 * INNER].reshape(rows_in, groups, inner)
    bc_cols = jnp.broadcast_to(
        w_in_low[:, None, 2 * INNER : 2 * INNER + 2 * STATE], (rows_in, groups, 2 * STATE)
    )
    dt_cols = w_in_low[:, 2 * INNER + 2 * STATE :].reshape(rows_in, groups, heads)
    router_cols = jnp.broadcast_to(
        w_router.astype(bf16)[:, None], (rows_in, groups, experts)
    )
    fill = jnp.zeros((rows_in, groups, LANES - heads - experts), bf16)
    win_pieces = jnp.concatenate(
        [z_cols, x_cols, bc_cols, dt_cols, router_cols, fill], axis=2
    ).transpose(1, 0, 2)
    win_rows = swap(win_pieces, "expert").reshape(groups * rows_in, -1)
    win = lax.all_gather(win_rows, "dp", axis=0, tiled=True)
    router = win[:, body + heads : body + heads + experts]
    x_all = spread(tokens, "expert").reshape(length, D)
    cot_all = spread(cotangent, "expert").reshape(length, D)
    routes_all = spread(routes, "expert").reshape(length, top)

    wout_shards = lax.all_gather(w_out.astype(bf16), "dp", axis=0, tiled=False)
    wout = (
        swap(wout_shards.reshape(groups, per_pair * rows_out, D), "expert")
        .reshape(groups, per_pair, rows_out, D)
        .transpose(1, 0, 2, 3)
        .reshape(inner, D)
    )
    sgu_pieces = (
        w_shared_gu.astype(bf16)
        .reshape(rows_in, 2, copies, groups, rows_sd)
        .transpose(3, 0, 1, 2, 4)
        .reshape(groups, rows_in, 2 * own_ff)
    )
    sgu = lax.all_gather(
        swap(sgu_pieces, "expert").reshape(groups * rows_in, 2 * own_ff), "dp", axis=0, tiled=True
    )
    sd = lax.all_gather(w_shared_down.astype(bf16), "dp", axis=0, tiled=True)
    egu = lax.all_gather(w_expert_gu.astype(bf16), "dp", axis=1, tiled=True)
    ed = lax.all_gather(w_expert_down.astype(bf16), "dp", axis=1, tiled=True)

    positions = jnp.arange(length, dtype=jnp.int32)
    starts = jnp.cumsum(lengths[0]) - lengths[0]
    doc_index = jnp.sum((starts[None, :] <= positions[:, None]).astype(jnp.int32), axis=1) - 1
    usable = (doc_index[:, None] == doc_index[None, :]) & (
        positions[:, None] >= positions[None, :]
    )
    usable_low = usable.astype(f32)
    earlier_doc = [
        jnp.concatenate([jnp.full((offset,), -1, jnp.int32), doc_index[: length - offset]])
        for offset in range(CONV)
    ]
    taps = [(earlier == doc_index).astype(f32)[:, None] for earlier in earlier_doc]

    own_x = place * inner
    conv_own = jnp.concatenate(
        [
            lax.dynamic_slice_in_dim(conv_params, own_x, inner, axis=1),
            conv_params[:, INNER:],
        ],
        axis=1,
    )
    head_own = lax.dynamic_slice_in_dim(head_params, place * heads, heads, axis=1)
    gain_own = lax.dynamic_slice_in_dim(mixer_gain, own_x, inner, axis=0)

    inputs = x_all.astype(f32)
    scale_one = rms_scale(inputs)
    normed_one = inputs * scale_one
    normed = (normed_one * norm_gains[0]).astype(bf16)
    projected = dot(normed, win)
    packed = projected[:, :body].astype(bf16)
    dt_raw = projected[:, body : body + heads]
    gate_z = packed[:, :inner].astype(f32)
    conv_in = packed[:, inner:].astype(f32)
    conv_out = conv_own[CONV]
    for offset in range(CONV):
        conv_out = conv_out + conv_own[offset] * shifted(conv_in, offset) * taps[offset]
    mixed_in = jax.nn.silu(conv_out)
    values = mixed_in[:, :inner]
    b_rows = mixed_in[:, inner : inner + STATE]
    c_rows = mixed_in[:, inner + STATE :]
    pre_step = dt_raw + head_own[1]
    dt_step = jax.nn.softplus(pre_step)
    rate_abs = jnp.exp(head_own[0])
    log_decay = -rate_abs * dt_step
    cum = jnp.dot(usable_low, log_decay, precision=highest)
    ssd_out = ssd_forward(values, b_rows, c_rows, dt_step, cum, usable)
    skip_cols = jnp.repeat(head_own[2], HEAD_DIM)
    full_y = ssd_out + skip_cols * values
    gate_act = jax.nn.silu(gate_z)
    gated_y = full_y * gate_act
    square_sum = jnp.sum(gated_y * gated_y, axis=1)
    partial_res = dot((gated_y * gain_own).astype(bf16), wout).astype(bf16)
    side = jnp.pad(jnp.stack(split_words(square_sum), axis=1), ((0, 0), (0, LANES - 3)))
    got = swap(jnp.concatenate([partial_res, side], axis=1).reshape(groups, tok, -1), "expert")
    squares = jnp.sum(
        got[:, :, D].astype(f32) + got[:, :, D + 1].astype(f32) + got[:, :, D + 2].astype(f32),
        axis=0,
    )[:, None]
    scale_mix = lax.rsqrt(squares / INNER + norm_eps)
    mixer_res = jnp.sum(got[:, :, :D].astype(f32), axis=0) * scale_mix
    hidden = tokens.astype(f32) + mixer_res
    scale_two = rms_scale(hidden)
    two_unit = hidden * scale_two
    normed_two_own = (two_unit * norm_gains[1]).astype(bf16)
    side = jnp.pad(jnp.concatenate(split_words(scale_mix), axis=1), ((0, 0), (0, LANES - 3)))
    got = spread(jnp.concatenate([normed_two_own, side], axis=1), "expert").reshape(length, -1)
    normed_two = got[:, :D]
    scale_mix_all = join_words([got[:, D + i : D + i + 1] for i in range(3)])

    logits = dot(normed_two, router)
    expert_ids = jnp.arange(experts, dtype=jnp.int32)
    named = jnp.any(routes_all[:, :, None] == expert_ids[None, None, :], axis=1)
    top_logit = jnp.max(jnp.where(named, logits, -jnp.inf), axis=1, keepdims=True)
    raised = jnp.where(named, jnp.exp(logits - top_logit), 0.0)
    weights = raised / jnp.sum(raised, axis=1, keepdims=True)

    shared_gu = dot(normed_two, sgu)
    shared_gate = shared_gu[:, :own_ff]
    shared_up = shared_gu[:, own_ff:]
    shared_silu = jax.nn.silu(shared_gate)
    shared_mid = (shared_silu * shared_up).astype(bf16)
    grad_shared_mid = dot_nt(cot_all, sd)
    grad_sgu_act = jnp.concatenate(
        [grad_shared_mid * shared_up * silu_slope(shared_gate), grad_shared_mid * shared_silu],
        axis=-1,
    ).astype(bf16)

    own_cols = place * own_experts
    named_own = lax.dynamic_slice_in_dim(named, own_cols, own_experts, axis=1)
    weights_own = lax.dynamic_slice_in_dim(weights, own_cols, own_experts, axis=1)
    named_blk = named_own.reshape(groups, tok, own_experts).astype(f32)
    before = jnp.tril(jnp.ones((tok, tok), f32), -1)
    slot_of = jnp.einsum("ts,gse->gte", before, named_blk)
    slots = jnp.arange(capacity, dtype=f32)
    pick = (
        (slot_of.transpose(0, 2, 1)[:, :, None, :] == slots[None, None, :, None])
        & (named_blk.transpose(0, 2, 1)[:, :, None, :] > 0)
    ).astype(bf16)
    pick_rows = pick.reshape(groups, own_experts * capacity, tok)
    two_blk = normed_two.reshape(groups, tok, D)
    cot_blk = cot_all.reshape(groups, tok, D)
    slot_in = jnp.einsum("gst,gtd->gsd", pick_rows, two_blk, preferred_element_type=f32)
    slot_in = slot_in.astype(bf16).reshape(groups, own_experts, capacity, D)
    slot_cot = jnp.einsum("gst,gtd->gsd", pick_rows, cot_blk, preferred_element_type=f32).reshape(
        groups, own_experts, capacity, D
    )
    slot_weight = jnp.sum(
        pick.astype(f32)
        * weights_own.reshape(groups, tok, own_experts).transpose(0, 2, 1)[:, :, None, :],
        axis=3,
    )
    slot_grad = (slot_cot * slot_weight[..., None]).astype(bf16)
    gate_up = jnp.einsum("gecd,edf->gecf", slot_in, egu, preferred_element_type=f32)
    gate_part = gate_up[..., :EXPERT_FF]
    up_part = gate_up[..., EXPERT_FF:]
    gate_silu = jax.nn.silu(gate_part)
    middle = (gate_silu * up_part).astype(bf16)
    slot_out = jnp.einsum("gecf,efd->gecd", middle, ed, preferred_element_type=f32)
    grad_mid = jnp.einsum("gecd,efd->gecf", slot_grad, ed, preferred_element_type=f32)
    grad_gu = jnp.concatenate(
        [grad_mid * up_part * silu_slope(gate_part), grad_mid * gate_silu], axis=-1
    ).astype(bf16)
    slot_back = jnp.einsum("gecf,edf->gecd", grad_gu, egu, preferred_element_type=f32).astype(bf16)
    grad_ed = jnp.einsum("gecf,gecd->efd", middle, slot_grad, preferred_element_type=f32)
    grad_egu = jnp.einsum("gecd,gecf->edf", slot_in, grad_gu, preferred_element_type=f32)
    slot_q = jnp.sum(slot_cot * slot_out, axis=3)
    token_q = jnp.sum(pick.astype(f32) * slot_q[..., None], axis=2)
    token_q = token_q.transpose(0, 2, 1).reshape(length, own_experts)

    def back_to_tokens(rows):
        rows = rows.reshape(groups, own_experts * capacity, D)
        return jnp.einsum("gst,gsd->gtd", pick_rows, rows, preferred_element_type=f32).reshape(
            length, D
        )

    expert_mix = back_to_tokens((slot_out * slot_weight[..., None]).astype(bf16))
    out_part = (dot(shared_mid, sd) + expert_mix).astype(bf16)
    back_part = (dot_nt(grad_sgu_act, sgu) + back_to_tokens(slot_back)).astype(bf16)
    side = jnp.pad(
        jnp.concatenate(split_words(token_q), axis=1), ((0, 0), (0, LANES - 3 * own_experts))
    )
    got = swap(jnp.concatenate([back_part, side], axis=1).reshape(groups, tok, -1), "expert")
    got_out = swap(out_part.reshape(groups, tok, D), "expert")
    output = (hidden + jnp.sum(got_out.astype(f32), axis=0)).astype(bf16)
    words = [
        got[:, :, D + i * own_experts : D + (i + 1) * own_experts].astype(f32) for i in range(3)
    ]
    q_own = (words[0] + words[1] + words[2]).transpose(1, 0, 2).reshape(tok, experts)
    weights_tok = lax.dynamic_slice_in_dim(weights, place * tok, tok, axis=0)
    grad_logits = (
        weights_tok * (q_own - jnp.sum(weights_tok * q_own, axis=1, keepdims=True))
    ).astype(bf16)
    grad_router = dot_tn(normed_two_own, grad_logits)
    grad_norm_two = jnp.sum(got[:, :, :D].astype(f32), axis=0) + dot_nt(grad_logits, router)
    grad_gain_two = jnp.sum(grad_norm_two * two_unit, axis=0)
    grad_hidden = cotangent.astype(f32) + norm_back(
        grad_norm_two, two_unit, scale_two, norm_gains[1]
    )
    hidden_low = grad_hidden.astype(bf16)
    row_mean = jnp.sum(hidden_low.astype(f32) * mixer_res, axis=1, keepdims=True) / INNER
    side = jnp.pad(jnp.concatenate(split_words(row_mean), axis=1), ((0, 0), (0, LANES - 3)))
    got = spread(jnp.concatenate([hidden_low, side], axis=1), "expert").reshape(length, -1)
    hidden_all = got[:, :D]
    row_mean_all = join_words([got[:, D + i : D + i + 1] for i in range(3)])

    grad_sgu = dot_tn(normed_two, grad_sgu_act).astype(bf16)
    grad_sd = dot_tn(shared_mid, cot_all).astype(bf16)
    sum_egu = lax.psum_scatter(
        grad_egu.astype(bf16), "dp", scatter_dimension=1, tiled=True
    ).astype(f32)
    sum_ed = lax.psum_scatter(grad_ed.astype(bf16), "dp", scatter_dimension=1, tiled=True).astype(
        f32
    )
    sgu_mine = lax.psum_scatter(grad_sgu, "dp", scatter_dimension=0, tiled=True)
    sum_sgu = (
        swap(sgu_mine.reshape(groups, rows_in, 2 * own_ff), "expert")
        .reshape(groups, rows_in, 2, copies, rows_sd)
        .transpose(1, 2, 3, 0, 4)
        .reshape(rows_in, 2 * SHARED_FF)
        .astype(f32)
    )
    sum_sd = lax.psum_scatter(grad_sd, "dp", scatter_dimension=0, tiled=True).astype(f32)

    normed_mix = gated_y * scale_mix_all
    mixer_act = (normed_mix * gain_own).astype(bf16)
    grad_wout = dot_tn(mixer_act, hidden_all).astype(bf16)
    wout_send = (
        grad_wout.reshape(per_pair, groups, rows_out, D)
        .transpose(1, 0, 2, 3)
        .reshape(groups, per_pair * rows_out, D)
    )
    wout_got = swap(wout_send, "expert").reshape(copies * rows_out, D)
    sum_out = lax.psum_scatter(wout_got, "dp", scatter_dimension=0, tiled=True).astype(f32)
    grad_mix_act = dot_nt(hidden_all, wout)
    grad_gain_mix = jnp.sum(grad_mix_act * normed_mix, axis=0)
    grad_gated = scale_mix_all * (grad_mix_act * gain_own - normed_mix * row_mean_all)
    grad_full_y = grad_gated * gate_act
    grad_gate_z = grad_gated * full_y * silu_slope(gate_z)
    grad_skip = jnp.sum(jnp.sum(grad_full_y * values, axis=0).reshape(heads, HEAD_DIM), axis=1)
    grad_vals, grad_b, grad_c, grad_step, grad_cum = ssd_backward(
        grad_full_y, values, b_rows, c_rows, dt_step, cum, usable
    )
    grad_vals = grad_vals + grad_full_y * skip_cols
    grad_decay = lax.dot_general(
        usable_low, grad_cum, (((0,), (0,)), ((), ())), precision=highest
    )
    grad_step = grad_step - grad_decay * rate_abs
    grad_log_rate = jnp.sum(grad_decay * log_decay, axis=0)
    grad_pre = grad_step * jax.nn.sigmoid(pre_step)
    grad_bias = jnp.sum(grad_pre, axis=0)
    grad_mixed = jnp.concatenate([grad_vals, grad_b, grad_c], axis=1)
    grad_conv = grad_mixed * silu_slope(conv_out)
    conv_grads = []
    grad_conv_in = jnp.zeros_like(grad_conv)
    for offset in range(CONV):
        masked = grad_conv * taps[offset]
        conv_grads.append(jnp.sum(masked * shifted(conv_in, offset), axis=0))
        grad_conv_in = grad_conv_in + shifted(conv_own[offset] * masked, -offset)
    conv_grads.append(jnp.sum(grad_conv, axis=0))
    conv_grads = jnp.stack(conv_grads)
    grad_proj = jnp.concatenate(
        [
            grad_gate_z.astype(bf16),
            grad_conv_in.astype(bf16),
            grad_pre.astype(bf16),
            jnp.zeros((length, LANES - heads), bf16),
        ],
        axis=1,
    )
    grad_win = dot_tn(normed, grad_proj)
    grad_win = jnp.concatenate(
        [
            grad_win[:, : body + heads],
            grad_router,
            jnp.zeros((D, LANES - heads - experts), f32),
        ],
        axis=1,
    ).astype(bf16)
    one_part = dot_nt(grad_proj, win)
    grad_gain_one = jnp.sum(one_part * normed_one, axis=0)
    got = swap(one_part.astype(bf16).reshape(groups, tok, D), "expert")
    grad_norm_one = jnp.sum(got.astype(f32), axis=0)
    own_in = tokens.astype(f32)
    own_scale = rms_scale(own_in)
    grad_tokens = (
        grad_hidden + norm_back(grad_norm_one, own_in * own_scale, own_scale, norm_gains[0])
    ).astype(bf16)

    pieces = [
        conv_grads[:, :inner].reshape(-1),
        grad_gain_mix,
        grad_log_rate,
        grad_bias,
        grad_skip,
        conv_grads[:, inner:].reshape(-1),
        grad_gain_one,
        grad_gain_two,
    ]
    sizes = [piece.size for piece in pieces]
    total = sum(sizes)
    unit = copies * LANES
    small = jnp.pad(jnp.concatenate(pieces), (0, -total % unit)).reshape(copies, -1)
    small = jnp.sum(swap(small, "dp"), axis=0)
    small = lax.all_gather(small, ("expert", "dp"), axis=0, tiled=True).reshape(groups, -1)
    parts = []
    start = 0
    for size in sizes:
        parts.append(small[:, start : start + size])
        start += size
    sum_conv = jnp.concatenate(
        [
            parts[0].reshape(groups, CONV + 1, inner).transpose(1, 0, 2).reshape(CONV + 1, INNER),
            jnp.sum(parts[5], axis=0).reshape(CONV + 1, 2 * STATE),
        ],
        axis=1,
    )
    sum_mixer = parts[1].reshape(INNER)
    sum_head = jnp.stack([parts[2].reshape(HEADS), parts[3].reshape(HEADS), parts[4].reshape(HEADS)])
    sum_gains = jnp.stack([jnp.sum(parts[6], axis=0), jnp.sum(parts[7], axis=0)])

    win_mine = lax.psum_scatter(grad_win, "dp", scatter_dimension=0, tiled=True)
    win_got = swap(win_mine.reshape(groups, rows_in, -1), "expert").astype(f32)

    def laid(start, size):
        return win_got[:, :, start : start + size].transpose(1, 0, 2).reshape(rows_in, -1)

    sum_in = jnp.concatenate(
        [
            laid(0, inner),
            laid(inner, inner),
            jnp.sum(win_got[:, :, 2 * inner : body], axis=0),
            laid(body, heads),
        ],
        axis=1,
    )
    sum_router = jnp.sum(win_got[:, :, body + heads : body + heads + experts], axis=0)

    up_in = adam_step(w_in, w_in_first, w_in_second, sum_in)
    up_out = adam_step(w_out, w_out_first, w_out_second, sum_out)
    up_router = adam_step(w_router, w_router_first, w_router_second, sum_router)
    up_sgu = adam_step(w_shared_gu, w_shared_gu_first, w_shared_gu_second, sum_sgu)
    up_sd = adam_step(w_shared_down, w_shared_down_first, w_shared_down_second, sum_sd)
    up_egu = adam_step(w_expert_gu, w_expert_gu_first, w_expert_gu_second, sum_egu)
    up_ed = adam_step(w_expert_down, w_expert_down_first, w_expert_down_second, sum_ed)
    up_gains = adam_step(norm_gains, norm_gains_first, norm_gains_second, sum_gains)
    up_conv = adam_step(conv_params, conv_params_first, conv_params_second, sum_conv)
    up_head = adam_step(head_params, head_params_first, head_params_second, sum_head)
    up_mixer = adam_step(mixer_gain, mixer_gain_first, mixer_gain_second, sum_mixer)
    large = (up_in, up_out, up_router, up_sgu, up_sd, up_egu, up_ed)
    little = (up_gains, up_conv, up_head, up_mixer)
    return (
        (output, grad_tokens)
        + tuple(part for one in large for part in one[:4])
        + tuple(part for one in little for part in (one[0], one[4], one[2], one[3]))
    )


def solution(mesh):
    rows = P(("dp", "expert"), None)
    expert_rows = P("expert", "dp", None)
    whole = P()
    return jax.shard_map(
        on_device,
        mesh=mesh,
        in_specs=(rows, rows, P("dp", None), rows)
        + (rows,) * 15
        + (expert_rows,) * 6
        + (whole,) * 12,
        out_specs=(rows, rows) + (rows,) * 20 + (expert_rows,) * 8 + (whole,) * 16,
        check_vma=False,
    )
```

time: 2210 us -> 827 us (0.37)
  waiting for transfers between devices: 1430 us -> 293 us
  local copies, waits for them, and re-layouts: 255 us -> 132 us
  blocking collectives: 189 us -> 88.9 us
  matrix products: 186 us -> 145 us
  starting transfers between devices: 18 us -> 58.3 us
    unnamed x12 -> x11, waiting for transfers between devices: 1010 us -> 0.18 us
    all_gather x8 -> x5, waiting for transfers between devices: 400 us -> 51.4 us  [the longest x1 45.9 us: on_device(): ed = lax.all_gather(w_expert_down.astype(bf16), 'dp', axis=1, tiled=True)]
    reduce_scatter x2 -> x6, waiting for transfers between devices: 0.01 us -> 119 us  [the longest x1 115 us: on_device(): lax.psum_scatter(grad_egu.astype(bf16), 'dp', scatter_dimension=1, tiled=...]
    all_to_all x3 -> x14, waiting for transfers between devices: 17.3 us -> 122 us  [swap(): return lax.all_to_all(pieces, axis, split_axis=0, concat_axis=0, tiled=True)]
    reshape x7 -> x20, local copies, waits for them, and re-layouts: 96 us -> 19.2 us  [the longest x1 3.61 us: on_device(): jnp.concatenate([partial_res, side], axis=1).reshape(groups, tok, -1)]
    all_gather x3 -> x2, blocking collectives: 114 us -> 64.1 us  [the longest x1 42.7 us: on_device(): lax.all_gather(small, ('expert', 'dp'), axis=0, tiled=True)]
    all_to_all x3 -> x14, starting transfers between devices: 12.4 us -> 57.7 us  [swap(): return lax.all_to_all(pieces, axis, split_axis=0, concat_axis=0, tiled=True)]
    unnamed x387 -> x241, local copies, waits for them, and re-layouts: 69 us -> 24.8 us
  transfers between devices with their start and end apart: 16 -> 25, of which waited for: 8 -> 15; matrix products, arithmetic and copies ran while one was open for 20% -> 37% of each run, Pallas kernels for 0% -> 0%
where the time goes in v1:
time: 827 us; the launch traced here: 819 us
  waiting for transfers between devices  293 us (35%)
  matrix products  145 us (18%)
  local copies, waits for them, and re-layouts  132 us (16%)
  blocking collectives  88.9 us (11%)
  other arithmetic  85.7 us (10%)
  starting transfers between devices  58.3 us (7%)
  between operations  15.9 us (2%)
    all_to_all x14, waiting for transfers between devices, swap(): return lax.all_to_all(pieces, axis, split_axis=0, concat_axis=0, tiled=True)  122 us
    reduce_scatter x1, waiting for transfers between devices, on_device(): lax.psum_scatter(grad_egu.astype(bf16), 'dp', scatter_dimension=1, tiled=...  115 us
    all_to_all x14, starting transfers between devices, swap(): return lax.all_to_all(pieces, axis, split_axis=0, concat_axis=0, tiled=True)  57.7 us
    all_gather x1, waiting for transfers between devices, on_device(): ed = lax.all_gather(w_expert_down.astype(bf16), 'dp', axis=1, tiled=True)  45.9 us
    all_gather x1, blocking collectives, on_device(): lax.all_gather(small, ('expert', 'dp'), axis=0, tiled=True)  42.7 us
    concatenate x1, local copies, waits for them, and re-layouts, on_device(): jnp.concatenate([grad_win[:, :body + heads], grad_router, jnp.zeros((D, L...  28.7 us
    add x7, other arithmetic, adam_step(): return (gradient, weight + moved, moment_one, moment_two, moved)  25.7 us
    unnamed x241, local copies, waits for them, and re-layouts  24.8 us
  transfers between devices with their start and end apart: 25, of which 15 were waited for; matrix products, arithmetic and copies ran while one was open for 37% of the time, Pallas kernels for 0%

profile of v1, /device:TPU:0, one launch (start us, length us, event | category | flops | bytes accessed | tf_op | source)
XLA Modules:
  0.0 819.2 jit_solution(950802073147134774)
XLA Ops:
  12.3 16.1 %all_to_all.84 = bf16[4,48,1920]{2,1,0:T(8,128)(2,1)} all-to-all(bf16[4,48,1920]{2,1,0:T(8,128)(2,1)S(1)} %copy.504), channel_id=1, replica_groups=mesh['dp'=8,'expert'=4] {'expert'}, dimensions={0} | all-to-all | bytes 1474560 | tf_op jit(solution)/shard_map/all_to_all | solution.py:42
  33.9 8.6 %all_to_all.85 = bf16[4,48,512]{2,1,0:T(8,128)(2,1)} all-to-all(bf16[4,48,512]{2,1,0:T(8,128)(2,1)S(1)} %reshape.543), channel_id=1, replica_groups=mesh['dp'=8,'expert'=4] {'expert'}, dimensions={0} | all-to-all | bytes 393216 | tf_op jit(solution)/shard_map/all_to_all | solution.py:42
  45.3 3.6 all-to-all-start
  54.5 11.7 %all-to-all-done = bf16[4,128,1536]{2,1,0:T(8,128)(2,1)S(1)} async-done(((bf16[4,128,1536]{2,1,0:T(8,128)(2,1)}), bf16[4,128,1536]{2,1,0:T(8,128)(2,1)S(1)}, u32[]{:S(2)}, u32[]{:S(2)}) %all-to-all-start) | async-done | bytes 1572896 | tf_op jit(solution)/shard_map/all_to_all | solution.py:42
  66.1 4.8 all-to-all-start.2
  74.6 23.7 %all-to-all-done.2 = bf16[4,192,1536]{2,1,0:T(8,128)(2,1)} async-done(((bf16[4,192,1536]{2,1,0:T(8,128)(2,1)}), bf16[4,192,1536]{2,1,0:T(8,128)(2,1)}, u32[]{:S(2)}, u32[]{:S(2)}) %all-to-all-start.2) | async-done | bytes 2359328 | tf_op jit(solution)/shard_map/all_to_all | solution.py:42
  98.2 3.3 copy.508
  101.5 5.5 all-gather.8.cloned.1.call-done
  107.0 8.1 fusion.172
  116.1 3.2 fusion.167
  131.0 4.3 fusion.11
  138.3 4.1 multiply_reduce_fusion.9
  142.6 4.4 convolution_convert_fusion.3
  148.3 3.6 copy.510
  151.9 4.5 all-to-all-start.3
  157.8 20.0 %all-to-all-done.3 = bf16[4,128,1664]{1,2,0:T(8,128)(2,1)} async-done(((bf16[4,128,1664]{1,2,0:T(8,128)(2,1)}), bf16[4,128,1664]{1,2,0:T(8,128)(2,1)}, u32[]{:S(2)}, u32[]{:S(2)}) %all-to-all-start.3) | async-done | bytes 1703968 | tf_op jit(solution)/shard_map/all_to_all | solution.py:42
  178.4 3.3 all-to-all-start.6
  189.5 4.4 all-to-all-start.8
  198.7 14.2 %all-to-all-done.8 = bf16[4,128,1536]{2,1,0:T(8,128)(2,1)} async-done(((bf16[4,128,1536]{2,1,0:T(8,128)(2,1)}), bf16[4,128,1536]{2,1,0:T(8,128)(2,1)}, u32[]{:S(2)}, u32[]{:S(2)}) %all-to-all-start.8) | async-done | bytes 1572896 | tf_op jit(solution)/shard_map/all_to_all | solution.py:42
  215.4 4.5 all-to-all-start.4
  219.9 21.4 %all_gather.28 = bf16[256,1536]{1,0:T(8,128)(2,1)} all-gather(bf16[32,1536]{1,0:T(8,128)(2,1)S(1)} %copy-done.38), channel_id=1, replica_groups=mesh['dp'=8,'expert'=4] {'dp'}, dimensions={0}, use_global_device_ids=true | all-gather | bytes 884736 | tf_op jit(solution)/shard_map/all_gather | solution.py:203
  241.8 5.0 fusion.174
  246.8 3.7 copy.518
  263.9 8.0 fusion.41
  275.5 45.9 %all-gather.14.cloned.1.call-done = bf16[4,512,1536]{2,1,0:T(8,128)(2,1)} async-done(((bf16[4,64,1536]{2,1,0:T(8,128)(2,1)}), bf16[4,512,1536]{2,1,0:T(8,128)(2,1)}) %all-gather.14.cloned.1.call-update) | async-done | bytes 6291472 | tf_op jit(solution)/shard_map/all_gather | solution.py:205
  321.3 9.5 %fusion.18 = (f32[4,4,64]{2,0,1:T(4,128)S(1)}, f32[4,4,64,1536]{3,2,1,0:T(8,128)}) fusion(f32[4,4,64,1536]{3,2,1,0:T(8,128)} %bitcast.248, bf16[4,4,64,512]{3,2,0,1:T(8,128)(2,1)} %multiply_convert_fusion.2, bf16[4,512,1536]{2,1,0:T(8,128)(2,1)} %all-gather.14.cloned.1.call-done), kind=kOutput, calls=%fused_computation.23 | convolution fusion | flops 1613757440 | bytes 19927040 | tf_op jit(solution)/shard_map/gecf,efd->gecd/dot_general | solution.py:324
  331.4 7.7 fusion.47
  339.1 10.4 %fusion.34 = bf16[4,4,64,1536]{3,2,0,1:T(8,128)(2,1)} fusion(bf16[4,1536,1024]{2,1,0:T(8,128)(2,1)} %all-gather.12.cloned.1.call-done, bf16[4,4,64,512]{3,2,0,1:T(8,128)(2,1)} %get-tuple-element.490, bf16[4,4,64,512]{3,2,0,1:T(8,128)(2,1)} %get-tuple-element.489), kind=kOutput, calls=%fused_computation.44 | convolution fusion | flops 3226992640 | bytes 17825792 | tf_op jit(solution)/shard_map/gecf,edf->gecd/dot_general | solution.py:329
  355.4 3.6 fusion.39
  360.3 3.6 copy.531
  363.9 4.4 all-to-all-start.9
  368.5 3.7 convolution_convert_fusion.2
  372.3 17.4 %all-to-all-done.9 = bf16[4,128,1664]{1,2,0:T(8,128)(2,1)} async-done(((bf16[4,128,1664]{1,2,0:T(8,128)(2,1)}), bf16[4,128,1664]{1,2,0:T(8,128)(2,1)}, u32[]{:S(2)}, u32[]{:S(2)}) %all-to-all-start.9) | async-done | bytes 1703968 | tf_op jit(solution)/shard_map/all_to_all | solution.py:42
  404.9 4.4 all-to-all-start.10
  413.7 16.2 %all-to-all-done.10 = bf16[4,128,1664]{1,2,0:T(8,128)(2,1)} async-done(((bf16[4,128,1664]{1,2,0:T(8,128)(2,1)}), bf16[4,128,1664]{1,2,0:T(8,128)(2,1)}, u32[]{:S(2)}, u32[]{:S(2)}) %all-to-all-start.10) | async-done | bytes 1703968 | tf_op jit(solution)/shard_map/all_to_all | solution.py:42
  429.9 3.7 copy.535
  433.6 3.4 convolution_convert_fusion.1
  438.5 4.7 all-to-all-start.13
  444.7 7.5 multiply_reduce_fusion.7
  456.6 6.2 fusion.62
  465.9 4.5 all-to-all-done.13
  470.5 8.8 %fusion.7 = (f32[12,512]{1,0:T(8,128)S(1)}, f32[12,512]{1,0:T(8,128)S(1)}, bf16[512,512]{1,0:T(8,128)(2,1)}) fusion(f32[512,512]{1,0:T(8,128)} %copy-done.34, f32[12,512]{1,0:T(8,128)S(1)} %copy-done.116, pred[512,512]{1,0:T(8,128)(4,1)S(1)} %copy-done.40, bf16[512,12,64]{0,2,1:T(8,128)(2,1)} %bitcast.286, f32[512,12,64]{0,2,1:T(8,128)} %bitcast.281, ...), kind=kOutput, calls=%fused_computation.12 | convolution fusion | flops 428331008 | bytes 4292608 | tf_op jit(solution)/shard_map/thp,shp->hts/dot_general | solution.py:122
  493.5 5.3 fusion.176
  501.7 28.7 %concatenate.83 = bf16[1536,1920]{0,1:T(8,128)(2,1)} concatenate(bf16[1536,1804]{0,1:T(8,128)(2,1)} %slice.421, bf16[1536,16]{0,1:T(8,128)(2,1)S(1)} %convolution_convert_fusion.5, bf16[1536,100]{0,1:T(8,128)(2,1)S(1)} %broadcast_in_dim.67), dimensions={1} | concatenate | bytes 11796480 | tf_op jit(solution)/shard_map/concatenate | solution.py:437
  530.4 8.9 %copy.565 = bf16[1536,1920]{1,0:T(8,128)(2,1)} copy(bf16[1536,1920]{0,1:T(8,128)(2,1)} %concatenate.83) | data formatting | bytes 11796480
  540.6 7.4 bitcast_convert_fusion.1
  549.5 8.5 %bitcast_convert_fusion = bf16[4,1536,1024]{2,1,0:T(8,128)(2,1)} fusion(bf16[4,4,64,1536]{3,2,1,0:T(8,128)(2,1)} %bitcast.267, bf16[4,4,64,512]{3,2,0,1:T(8,128)(2,1)S(1)} %copy-done.114, bf16[4,4,64,512]{3,2,0,1:T(8,128)(2,1)S(1)} %copy-done.113), kind=kOutput, calls=%fused_computation | convolution fusion | flops 3231711232 | bytes 17825792 | tf_op jit(solution)/shard_map/gecd,gecf->edf/dot_general | solution.py:331
  558.7 3.4 all-to-all-start.14
  563.9 3.3 all-to-all-done.14
  570.9 3.4 fusion.17
  577.4 4.5 all-to-all-start.7
  584.7 8.0 multiply_reduce_fusion.1
  593.4 6.5 all-to-all-done.7
  599.9 3.3 all-to-all-start.15
  605.9 3.1 all-to-all-done.15
  609.0 4.5 all-to-all-start.11
  613.6 42.7 %all-gather.1 = f32[32,1,1152]{2,1,0:T(1,128)S(1)} all-gather(f32[1,1,1152]{2,1,0:T(1,128)S(1)} %reshape.583), channel_id=1, replica_groups=mesh['dp'=8,'expert'=4] {'expert','dp'}, dimensions={0}, use_global_device_ids=true | all-gather | bytes 152064 | tf_op jit(solution)/shard_map/all_gather | solution.py:470
  664.7 3.2 multiply_add_fusion.10
  667.8 3.5 all-to-all-start.12
  671.3 4.0 reduce-scatter.17.cloned.1.call-done
  675.3 5.3 multiply_add_fusion.3
  685.4 5.1 multiply_add_fusion.7
  690.5 114.8 %reduce-scatter.15.cloned.1.call-done = bf16[4,192,1024]{2,1,0:T(8,128)(2,1)} async-done(((bf16[4,1536,1024]{2,1,0:T(8,128)(2,1)}), bf16[4,192,1024]{2,1,0:T(8,128)(2,1)}) %reduce-scatter.15.cloned.1.call-update) | async-done | bytes 1572880 | tf_op jit(solution)/shard_map/reduce_scatter | solution.py:374
  805.2 7.3 multiply_add_fusion
  (458 shorter events, 159.4 us)
Async XLA Ops:
  7.2 58.9 %all-gather.16.cloned.1.call-start = ((), (), s32[]{:S(2)}) async-start(), calls=%async_computation.31 | async-start | bytes 2654208 | tf_op jit(solution)/shard_map/all_gather | solution.py:187
  9.1 97.9 %all-gather.8.cloned.1.call-start = ((), (), s32[]{:S(2)}) async-start(), calls=%async_computation.22 | async-start | bytes 6635520 | tf_op jit(solution)/shard_map/all_gather | solution.py:181
  12.2 16.3 %copy-start.30 = (f32[48,2048]{1,0:T(8,128)S(1)}, f32[48,2048]{1,0:T(8,128)}, u32[]{:S(2)}) copy-start(f32[48,2048]{1,0:T(8,128)} %param.50) | copy-start | bytes 1179652
  28.4 14.2 %copy-start.4 = (f32[4,192,1024]{2,1,0:T(8,128)S(1)}, f32[4,192,1024]{2,1,0:T(8,128)}, u32[]{:S(2)}) copy-start(f32[4,192,1024]{2,1,0:T(8,128)} %param.56) | copy-start | bytes 9437188
  28.4 226.7 %all-gather.10.cloned.1.call-start = ((), (), s32[]{:S(2)}) async-start(), calls=%async_computation.23 | async-start | bytes 1769472 | tf_op jit(solution)/shard_map/all_gather | solution.py:200
  42.5 221.4 %all-gather.12.cloned.1.call-start = ((), (), s32[]{:S(2)}) async-start(), calls=%async_computation.24 | async-start | bytes 14155776 | tf_op jit(solution)/shard_map/all_gather | solution.py:204
  45.3 20.9 %all-to-all-start = ((bf16[4,128,1536]{2,1,0:T(8,128)(2,1)}), bf16[4,128,1536]{2,1,0:T(8,128)(2,1)S(1)}, u32[]{:S(2)}, u32[]{:S(2)}) async-start(bf16[4,128,1536]{2,1,0:T(8,128)(2,1)} %broadcast_in_dim.49), calls=%async_computation | async-start | bytes 3145728 | tf_op jit(solution)/shard_map/all_to_all | solution.py:42
  48.8 272.5 %all-gather.14.cloned.1.call-start = ((), (), s32[]{:S(2)}) async-start(), calls=%async_computation.25 | async-start | bytes 7077888 | tf_op jit(solution)/shard_map/all_gather | solution.py:205
  54.4 19.1 %copy-start.44 = (f32[1536]{0:T(1024)}, f32[1536]{0:T(1024)S(1)}, u32[]{:S(2)}) copy-start(f32[1536]{0:T(1024)S(1)} %get-tuple-element.424) | copy-start | bytes 18436
  66.1 7.5 copy-start.1
  66.1 32.1 %all-to-all-start.2 = ((bf16[4,192,1536]{2,1,0:T(8,128)(2,1)}), bf16[4,192,1536]{2,1,0:T(8,128)(2,1)}, u32[]{:S(2)}, u32[]{:S(2)}) async-start(bf16[4,192,1536]{2,1,0:T(8,128)(2,1)} %bitcast.277), calls=%async_computation.2 | async-start | bytes 4718592 | tf_op jit(solution)/shard_map/all_to_all | solution.py:42
  74.6 32.4 %copy-start.29 = (bf16[512,1536]{1,0:T(8,128)(2,1)}, bf16[512,1536]{1,0:T(8,128)(2,1)S(1)}, u32[]{:S(2)}) copy-start(bf16[512,1536]{1,0:T(8,128)(2,1)S(1)} %multiply_convert_fusion.1) | copy-start | bytes 4718596
  119.4 11.3 %copy-start.27 = (bf16[512,1024]{1,0:T(8,128)(2,1)}, bf16[512,1024]{1,0:T(8,128)(2,1)S(1)}, u32[]{:S(2)}) copy-start(bf16[512,1024]{1,0:T(8,128)(2,1)S(1)} %get-tuple-element.485) | copy-start | bytes 3145732
  151.9 25.8 %copy-start.96 = (s32[128,6]{0,1:T(8,128)S(1)}, s32[128,6]{0,1:T(8,128)}, u32[]{:S(2)}) copy-start(s32[128,6]{0,1:T(8,128)} %param.40) | copy-start | bytes 9220
  151.9 25.8 %all-to-all-start.3 = ((bf16[4,128,1664]{1,2,0:T(8,128)(2,1)}), bf16[4,128,1664]{1,2,0:T(8,128)(2,1)}, u32[]{:S(2)}, u32[]{:S(2)}) async-start(bf16[4,128,1664]{1,2,0:T(8,128)(2,1)} %copy.510), calls=%async_computation.3 | async-start | bytes 3407872 | tf_op jit(solution)/shard_map/all_to_all | solution.py:42
  157.8 30.4 %copy-start.22 = (bf16[128,1536]{1,0:T(8,128)(2,1)S(1)}, bf16[128,1536]{1,0:T(8,128)(2,1)}, u32[]{:S(2)}) copy-start(bf16[128,1536]{1,0:T(8,128)(2,1)} %param.38) | copy-start | bytes 1179652
  178.4 9.8 %all-to-all-start.6 = ((s32[4,128,6]{1,2,0:T(8,128)}), s32[4,128,6]{1,2,0:T(8,128)S(1)}, u32[]{:S(2)}, u32[]{:S(2)}) async-start(s32[4,128,6]{1,2,0:T(8,128)} %broadcast_in_dim.57), calls=%async_computation.6 | async-start | bytes 32768 | tf_op jit(solution)/shard_map/all_to_all | solution.py:42
  185.1 8.7 %copy-start.105 = (f32[128]{0:T(128)}, f32[128]{0:T(128)S(1)}, u32[]{:S(2)}) copy-start(f32[128]{0:T(128)S(1)} %get-tuple-element.536) | copy-start | bytes 1540
  189.5 23.5 %all-to-all-start.8 = ((bf16[4,128,1536]{2,1,0:T(8,128)(2,1)}), bf16[4,128,1536]{2,1,0:T(8,128)(2,1)}, u32[]{:S(2)}, u32[]{:S(2)}) async-start(bf16[4,128,1536]{2,1,0:T(8,128)(2,1)} %broadcast_in_dim.64), calls=%async_computation.8 | async-start | bytes 3145728 | tf_op jit(solution)/shard_map/all_to_all | solution.py:42
  195.8 17.1 %copy-start.92 = (f32[128]{0:T(128)}, f32[128]{0:T(128)S(1)}, u32[]{:S(2)}) copy-start(f32[128]{0:T(128)S(1)} %add_rsqrt_fusion.1) | copy-start | bytes 1540
  215.4 26.0 %copy-start.55 = (s32[4,128,6]{1,2,0:T(8,128)S(1)}, s32[4,128,6]{1,2,0:T(8,128)}, u32[]{:S(2)}) copy-start(s32[4,128,6]{1,2,0:T(8,128)} %copy-done.54) | copy-start | bytes 36868
  215.4 26.3 %copy-start.95 = (f32[256]{0:T(256)S(1)}, f32[256]{0:T(256)}, u32[]{:S(2)}) copy-start(f32[256]{0:T(256)} %eq.82) | copy-start | bytes 3076
  215.4 31.4 %all-to-all-start.4 = ((bf16[4,128,1664]{1,2,0:T(8,128)(2,1)}), bf16[4,128,1664]{1,2,0:T(8,128)(2,1)}, u32[]{:S(2)}, u32[]{:S(2)}) async-start(bf16[4,128,1664]{1,2,0:T(8,128)(2,1)} %broadcast_in_dim.56), calls=%async_computation.4 | async-start | bytes 3407872 | tf_op jit(solution)/shard_map/all_to_all | solution.py:42
  321.3 10.0 %copy-start.15 = (bf16[4,512,1536]{2,1,0:T(8,128)(2,1)S(1)}, bf16[4,512,1536]{2,1,0:T(8,128)(2,1)}, u32[]{:S(2)}) copy-start(bf16[4,512,1536]{2,1,0:T(8,128)(2,1)} %all-gather.14.cloned.1.call-done) | copy-start | bytes 18874372
  331.4 7.7 copy-start.72
  363.9 25.8 %all-to-all-start.9 = ((bf16[4,128,1664]{1,2,0:T(8,128)(2,1)}), bf16[4,128,1664]{1,2,0:T(8,128)(2,1)}, u32[]{:S(2)}, u32[]{:S(2)}) async-start(bf16[4,128,1664]{1,2,0:T(8,128)(2,1)} %copy.531), calls=%async_computation.9 | async-start | bytes 3407872 | tf_op jit(solution)/shard_map/all_to_all | solution.py:42
  368.3 190.4 %reduce-scatter.11.cloned.1.call-start = ((), (), s32[]{:S(2)}) async-start(), calls=%async_computation.27 | async-start | bytes 1769472 | tf_op jit(solution)/shard_map/reduce_scatter | solution.py:380
  372.2 23.2 %copy-start.51 = (f32[512,16]{0,1:T(8,128)S(1)}, f32[512,16]{0,1:T(8,128)}, u32[]{:S(2)}) copy-start(f32[512,16]{0,1:T(8,128)} %copy-done.50) | copy-start | bytes 98308
  372.2 23.2 %copy-start.93 = (f32[128]{0:T(128)S(1)}, f32[128]{0:T(128)}, u32[]{:S(2)}) copy-start(f32[128]{0:T(128)} %copy-done.92) | copy-start | bytes 1540
  404.9 25.0 %all-to-all-start.10 = ((bf16[4,128,1664]{1,2,0:T(8,128)(2,1)}), bf16[4,128,1664]{1,2,0:T(8,128)(2,1)}, u32[]{:S(2)}, u32[]{:S(2)}) async-start(bf16[4,128,1664]{1,2,0:T(8,128)(2,1)} %broadcast_in_dim.65), calls=%async_computation.10 | async-start | bytes 3407872 | tf_op jit(solution)/shard_map/all_to_all | solution.py:42
  409.3 152.7 %reduce-scatter.13.cloned.1.call-start = ((), (), s32[]{:S(2)}) async-start(), calls=%async_computation.28 | async-start | bytes 884736 | tf_op jit(solution)/shard_map/reduce_scatter | solution.py:388
  412.4 21.2 %copy-start.98 = (f32[768]{0:T(1024)S(1)}, f32[768]{0:T(1024)}, u32[]{:S(2)}) copy-start(f32[768]{0:T(1024)} %dynamic_slice.20) | copy-start | bytes 9220
  438.5 31.9 %all-to-all-start.13 = ((bf16[4,192,1536]{2,1,0:T(8,128)(2,1)}), bf16[4,192,1536]{2,1,0:T(8,128)(2,1)}, u32[]{:S(2)}, u32[]{:S(2)}) async-start(bf16[4,192,1536]{2,1,0:T(8,128)(2,1)} %bitcast.260), calls=%async_computation.13 | async-start | bytes 4718592 | tf_op jit(solution)/shard_map/all_to_all | solution.py:42
  443.2 221.5 %reduce-scatter.9.cloned.1.call-start = ((), (), s32[]{:S(2)}) async-start(), calls=%async_computation.26 | async-start | bytes 2654208 | tf_op jit(solution)/shard_map/reduce_scatter | solution.py:399
  470.4 8.9 %copy-start.46 = (f32[512,12]{0,1:T(8,128)S(1)}, f32[512,12]{0,1:T(8,128)}, u32[]{:S(2)}) copy-start(f32[512,12]{0,1:T(8,128)} %copy.569) | copy-start | bytes 73732
  470.4 8.9 %copy-start.100 = (f32[12]{0:T(128)S(1)}, f32[12]{0:T(128)}, u32[]{:S(2)}) copy-start(f32[12]{0:T(128)} %get-tuple-element.527) | copy-start | bytes 148
  470.4 8.9 %copy-start.109 = (f32[12]{0:T(128)S(1)}, f32[12]{0:T(128)}, u32[]{:S(2)}) copy-start(f32[12]{0:T(128)} %get-tuple-element.524) | copy-start | bytes 148
  470.4 8.9 %copy-start.110 = (f32[12]{0:T(128)S(1)}, f32[12]{0:T(128)}, u32[]{:S(2)}) copy-start(f32[12]{0:T(128)} %get-tuple-element.526) | copy-start | bytes 148
  470.5 197.4 %reduce-scatter.19.cloned.1.call-start = ((), (), s32[]{:S(2)}) async-start(), calls=%async_computation.32 | async-start | bytes 6635520 | tf_op jit(solution)/shard_map/reduce_scatter | solution.py:487
  539.4 135.9 %reduce-scatter.17.cloned.1.call-start = ((), (), s32[]{:S(2)}) async-start(), calls=%async_computation.30 | async-start | bytes 7077888 | tf_op jit(solution)/shard_map/reduce_scatter | solution.py:377
  548.0 257.3 %reduce-scatter.15.cloned.1.call-start = ((), (), s32[]{:S(2)}) async-start(), calls=%async_computation.29 | async-start | bytes 14155776 | tf_op jit(solution)/shard_map/reduce_scatter | solution.py:374
  558.7 8.5 %all-to-all-start.14 = ((bf16[4,48,512]{2,1,0:T(8,128)(2,1)}), bf16[4,48,512]{2,1,0:T(8,128)(2,1)S(1)}, u32[]{:S(2)}, u32[]{:S(2)}) async-start(bf16[4,48,512]{2,1,0:T(8,128)(2,1)} %bitcast.290), calls=%async_computation.16 | async-start | bytes 393216 | tf_op jit(solution)/shard_map/all_to_all | solution.py:42
  570.9 11.1 %copy-start.32 = (f32[48,2048]{1,0:T(8,128)}, f32[48,2048]{1,0:T(8,128)S(1)}, u32[]{:S(2)}) copy-start(f32[48,2048]{1,0:T(8,128)S(1)} %copy.557) | copy-start | bytes 1179652
  577.4 22.5 %all-to-all-start.7 = ((bf16[4,128,1536]{2,1,0:T(8,128)(2,1)}), bf16[4,128,1536]{2,1,0:T(8,128)(2,1)}, u32[]{:S(2)}, u32[]{:S(2)}) async-start(bf16[4,128,1536]{2,1,0:T(8,128)(2,1)} %bitcast.45), calls=%async_computation.7 | async-start | bytes 3145728 | tf_op jit(solution)/shard_map/all_to_all | solution.py:42
  584.7 8.0 copy-start.99
  584.7 8.0 copy-start.107
  584.7 8.0 copy-start.108
  599.9 9.0 %all-to-all-start.15 = ((f32[8,1,1152]{2,1,0:T(1,128)}), f32[8,1,1152]{2,1,0:T(1,128)S(1)}, u32[]{:S(2)}, u32[]{:S(2)}) async-start(f32[8,1,1152]{2,1,0:T(1,128)} %bitcast.87), calls=%async_computation.20 | async-start | bytes 73728 | tf_op jit(solution)/shard_map/all_to_all | solution.py:42
  605.9 51.3 %copy-start.89 = (f32[3,48]{1,0:T(4,128)S(1)}, f32[3,48]{1,0:T(4,128)}, u32[]{:S(2)}) copy-start(f32[3,48]{1,0:T(4,128)} %param.68) | copy-start | bytes 1732
  605.9 51.3 %copy-start.101 = (f32[3,48]{1,0:T(4,128)S(1)}, f32[3,48]{1,0:T(4,128)}, u32[]{:S(2)}) copy-start(f32[3,48]{1,0:T(4,128)} %param.69) | copy-start | bytes 1732
  605.9 51.3 %copy-start.102 = (f32[3,48]{1,0:T(4,128)S(1)}, f32[3,48]{1,0:T(4,128)}, u32[]{:S(2)}) copy-start(f32[3,48]{1,0:T(4,128)} %param.70) | copy-start | bytes 1732
  605.9 51.9 %copy-start.56 = (f32[2,1536]{1,0:T(2,128)S(1)}, f32[2,1536]{1,0:T(2,128)}, u32[]{:S(2)}) copy-start(f32[2,1536]{1,0:T(2,128)} %param.62) | copy-start | bytes 36868
  605.9 51.9 %copy-start.82 = (f32[2,1536]{1,0:T(2,128)S(1)}, f32[2,1536]{1,0:T(2,128)}, u32[]{:S(2)}) copy-start(f32[2,1536]{1,0:T(2,128)} %param.63) | copy-start | bytes 36868
  605.9 51.9 %copy-start.83 = (f32[2,1536]{1,0:T(2,128)S(1)}, f32[2,1536]{1,0:T(2,128)}, u32[]{:S(2)}) copy-start(f32[2,1536]{1,0:T(2,128)} %param.64) | copy-start | bytes 36868
  609.0 49.7 %copy-start.74 = (f32[3072]{0:T(1024)S(1)}, f32[3072]{0:T(1024)}, u32[]{:S(2)}) copy-start(f32[3072]{0:T(1024)} %param.71) | copy-start | bytes 36868
  609.0 49.7 %copy-start.84 = (f32[3072]{0:T(1024)S(1)}, f32[3072]{0:T(1024)}, u32[]{:S(2)}) copy-start(f32[3072]{0:T(1024)} %param.72) | copy-start | bytes 36868
  609.0 49.7 %copy-start.85 = (f32[3072]{0:T(1024)S(1)}, f32[3072]{0:T(1024)}, u32[]{:S(2)}) copy-start(f32[3072]{0:T(1024)} %param.73) | copy-start | bytes 36868
  609.0 50.4 %copy-start.43 = (f32[5,3328]{1,0:T(8,128)S(1)}, f32[5,3328]{1,0:T(8,128)}, u32[]{:S(2)}) copy-start(f32[5,3328]{1,0:T(8,128)} %param.65) | copy-start | bytes 199684
  609.0 50.4 %copy-start.48 = (f32[5,3328]{1,0:T(8,128)S(1)}, f32[5,3328]{1,0:T(8,128)}, u32[]{:S(2)}) copy-start(f32[5,3328]{1,0:T(8,128)} %param.66) | copy-start | bytes 199684
  609.0 50.4 %copy-start.49 = (f32[5,3328]{1,0:T(8,128)S(1)}, f32[5,3328]{1,0:T(8,128)}, u32[]{:S(2)}) copy-start(f32[5,3328]{1,0:T(8,128)} %param.67) | copy-start | bytes 199684
  609.0 51.2 %all-to-all-start.11 = ((bf16[4,128,1536]{2,1,0:T(8,128)(2,1)}), bf16[4,128,1536]{2,1,0:T(8,128)(2,1)}, u32[]{:S(2)}, u32[]{:S(2)}) async-start(bf16[4,128,1536]{2,1,0:T(8,128)(2,1)} %bitcast.67), calls=%async_computation.11 | async-start | bytes 3145728 | tf_op jit(solution)/shard_map/all_to_all | solution.py:42
  664.7 10.6 %copy-start.17 = (f32[4,64,1536]{2,1,0:T(8,128)S(1)}, f32[4,64,1536]{2,1,0:T(8,128)}, u32[]{:S(2)}) copy-start(f32[4,64,1536]{2,1,0:T(8,128)} %param.59) | copy-start | bytes 4718596
  667.8 14.5 %all-to-all-start.12 = ((bf16[4,48,1920]{2,1,0:T(8,128)(2,1)}), bf16[4,48,1920]{2,1,0:T(8,128)(2,1)S(1)}, u32[]{:S(2)}, u32[]{:S(2)}) async-start(bf16[4,48,1920]{2,1,0:T(8,128)(2,1)} %bitcast.288), calls=%async_computation.12 | async-start | bytes 1474560 | tf_op jit(solution)/shard_map/all_to_all | solution.py:42
  685.4 119.8 %copy-start.5 = (f32[4,192,1024]{2,1,0:T(8,128)S(1)}, f32[4,192,1024]{2,1,0:T(8,128)}, u32[]{:S(2)}) copy-start(f32[4,192,1024]{2,1,0:T(8,128)} %param.56) | copy-start | bytes 9437188
  (79 other events, 211.2 us)
Sparse Core Ops, SparseCore 0:
  10.3 34.3 all-gather.15
  46.3 60.6 all-gather.7
  108.6 23.6 all-gather.9
  133.8 122.5 all-gather.11
  258.4 62.8 all-gather.13
  372.4 33.1 reduce-scatter.10
  412.5 30.7 reduce-scatter.12
  470.5 34.0 reduce-scatter.8
  539.5 63.9 reduce-scatter.18
  605.6 69.6 reduce-scatter.16
  677.6 127.5 reduce-scatter.14

commit v2 on v1

v2 whole, which is shorter than its diff:
```python
import functools
import math

import jax
import jax.numpy as jnp
from jax import lax
from jax.experimental import pallas as pl
from jax.experimental.pallas import tpu as pltpu
from jax.sharding import Mesh
from jax.sharding import PartitionSpec as P

D = 1536
HEADS = 48
HEAD_DIM = 64
STATE = 128
CONV = 4
EXPERT_FF = 512
SHARED_FF = 1024
STEP = 3
INNER = 3072
CONV_DIM = 3328
LANES = 128

DP = ("zhi", "zlo", "core")
MATES = ("zlo", "core")
ALL = DP + ("expert",)

norm_eps = 1e-05
beta_one = 0.9
beta_two = 0.95
adam_eps = 1e-08
learn_rate = 0.02
decay_rate = 0.1
highest = lax.Precision.HIGHEST
bf16 = jnp.bfloat16
f32 = jnp.float32


def dot(left, right):
    return jnp.dot(left, right, preferred_element_type=f32)


def dot_nt(left, right):
    return lax.dot_general(left, right, (((1,), (1,)), ((), ())), preferred_element_type=f32)


def dot_tn(left, right):
    return lax.dot_general(left, right, (((0,), (0,)), ((), ())), preferred_element_type=f32)


def swap(pieces, axis):
    return lax.all_to_all(pieces, axis, split_axis=0, concat_axis=0, tiled=True)


def spread(block, axis):
    axes = (axis,) if isinstance(axis, str) else axis
    count = math.prod(lax.axis_size(one) for one in axes)
    return swap(jnp.broadcast_to(block[None], (count,) + block.shape), axis)


def to_partner(value):
    return lax.ppermute(value, "zhi", [(0, 1), (1, 0)])


def rms_scale(values):
    return lax.rsqrt(jnp.mean(values * values, axis=-1, keepdims=True) + norm_eps)


def silu_slope(values):
    sigmoid_value = jax.nn.sigmoid(values)
    return sigmoid_value * (1.0 + values * (1.0 - sigmoid_value))


def norm_back(grad_norm, unit_rows, scale_rows, gain):
    scaled = grad_norm * gain
    return scale_rows * (scaled - unit_rows * jnp.mean(scaled * unit_rows, axis=-1, keepdims=True))


def adam_step(weight, moment_one, moment_two, gradient):
    moment_one = beta_one * moment_one + (1.0 - beta_one) * gradient
    moment_two = beta_two * moment_two + (1.0 - beta_two) * gradient * gradient
    fixed_one = 1.0 - beta_one**STEP
    fixed_two = 1.0 - beta_two**STEP
    change = (
        moment_one / fixed_one / (jnp.sqrt(moment_two / fixed_two) + adam_eps) + decay_rate * weight
    )
    moved = -learn_rate * change
    return (gradient, weight + moved, moment_one, moment_two, moved)


def split_words(value):
    high = value.astype(bf16)
    rest = value - high.astype(f32)
    mid = rest.astype(bf16)
    low = (rest - mid.astype(f32)).astype(bf16)
    return high, mid, low


def join_words(words):
    return words[0].astype(f32) + words[1].astype(f32) + words[2].astype(f32)


def conv_rows(block, masks, params):
    total = params[CONV : CONV + 1] + params[0:1] * block
    for offset in range(1, CONV):
        total = total + params[offset : offset + 1] * (
            pltpu.roll(block, offset, 0) * masks[:, offset : offset + 1]
        )
    return total


def conv_rows_back(grad, block, masks, params):
    length = block.shape[0]
    taps = [jnp.sum(grad * block, axis=0, keepdims=True)]
    rows = params[0:1] * grad
    for offset in range(1, CONV):
        masked = grad * masks[:, offset : offset + 1]
        taps.append(jnp.sum(masked * pltpu.roll(block, offset, 0), axis=0, keepdims=True))
        rows = rows + pltpu.roll(params[offset : offset + 1] * masked, length - offset, 0)
    taps.append(jnp.sum(grad, axis=0, keepdims=True))
    return rows, taps


def dot_words(exact, value, contract):
    total = None
    for word in split_words(value):
        part = lax.dot_general(exact, word, (contract, ((), ())), preferred_element_type=f32)
        total = part if total is None else total + part
    return total


def dot_words_left(value, exact):
    total = None
    for word in split_words(value):
        part = jnp.dot(word, exact, preferred_element_type=f32)
        total = part if total is None else total + part
    return total


def softplus(value):
    return jnp.maximum(value, 0.0) + jnp.log1p(jnp.exp(-jnp.abs(value)))


def head_lanes(pair, transposed=False):
    rows = lax.broadcasted_iota(jnp.int32, (LANES, LANES), 0)
    lanes = lax.broadcasted_iota(jnp.int32, (LANES, LANES), 1)
    if transposed:
        rows, lanes = lanes, rows
    return (rows == 2 * pair + lanes // HEAD_DIM).astype(f32).astype(bf16)


def lane_of(matrix, lane):
    lanes = lax.broadcasted_iota(jnp.int32, matrix.shape, 1)
    return jnp.sum(jnp.where(lanes == lane, matrix, 0.0), axis=1, keepdims=True)


def scan_setup(dt_ref, packed_ref, conv_ref, masks, head_ref, doc_col, doc_row, inner,
               neg_ref, scores_ref, cum_ref, cum_t_ref):
    length = dt_ref.shape[0]
    pre_step = dt_ref[...] + head_ref[1:2]
    dt_step = softplus(pre_step)
    log_decay = -head_ref[0:1] * dt_step
    at = lax.broadcasted_iota(jnp.int32, (length, length), 0)
    to = lax.broadcasted_iota(jnp.int32, (length, length), 1)
    usable = (doc_col == doc_row) & (at >= to)
    neg_ref[...] = jnp.where(usable, 0.0, -1e30)
    exact = usable.astype(f32).astype(bf16)
    cum_ref[...] = dot_words(exact, log_decay, ((1,), (0,)))
    cum_t_ref[...] = cum_ref[...].T
    start = 2 * inner
    b_in = packed_ref[:, start : start + STATE].astype(f32)
    c_in = packed_ref[:, start + STATE : start + 2 * STATE].astype(f32)
    b_out = conv_rows(b_in, masks, conv_ref[:, inner : inner + STATE])
    c_out = conv_rows(c_in, masks, conv_ref[:, inner + STATE : inner + 2 * STATE])
    b_low = jax.nn.silu(b_out).astype(bf16)
    c_low = jax.nn.silu(c_out).astype(bf16)
    scores_ref[...] = dot_nt(c_low, b_low)
    return pre_step, dt_step, log_decay, exact, b_out, c_out, b_low, c_low


def pair_slices(pair, inner):
    at = pl.ds(pl.multiple_of(pair * LANES, LANES), LANES)
    x_at = pl.ds(pl.multiple_of(inner + pair * LANES, LANES), LANES)
    return at, x_at


def forward_kernel(x_ref, win_ref, gain_ref, conv_ref, masks_ref, head_ref, cols_ref, doc_col_ref,
                   doc_row_ref, wout_ref, packed_ref, dt_ref, y_ref, out_ref,
                   normed_ref, neg_ref, scores_ref, cum_ref, cum_t_ref, act_ref, square_ref):
    length = x_ref.shape[0]
    inner = wout_ref.shape[0]
    body = packed_ref.shape[1]
    step = 2 * LANES

    @pl.loop(0, length // LANES)
    def _(part):
        rows = pl.ds(pl.multiple_of(part * LANES, LANES), LANES)
        block = x_ref[rows, :].astype(f32)
        scale = lax.rsqrt(jnp.mean(block * block, axis=1, keepdims=True) + norm_eps)
        normed_ref[rows, :] = (block * scale * gain_ref[0:1]).astype(bf16)

    @pl.loop(0, body // step)
    def _(part):
        at = pl.ds(pl.multiple_of(part * step, step), step)
        packed_ref[:, at] = dot(normed_ref[...], win_ref[:, at]).astype(bf16)

    dt_ref[...] = dot(normed_ref[...], win_ref[:, body:])
    masks = masks_ref[...]
    _, dt_step, *_ = scan_setup(
        dt_ref, packed_ref, conv_ref, masks, head_ref, doc_col_ref[...], doc_row_ref[...], inner,
        neg_ref, scores_ref, cum_ref, cum_t_ref,
    )
    square_ref[...] = jnp.zeros_like(square_ref)
    lanes = lax.broadcasted_iota(jnp.int32, (LANES, LANES), 1)

    @pl.loop(0, inner // LANES)
    def _(pair):
        at, x_at = pair_slices(pair, inner)
        values = jax.nn.silu(conv_rows(packed_ref[:, x_at].astype(f32), masks, conv_ref[:, at]))
        dt_wide = dot_words_left(dt_step, head_lanes(pair))
        scaled = (values * dt_wide).astype(bf16)
        cum_cols = [lane_of(cum_ref[...], 2 * pair + k) for k in range(2)]
        cum_rows = [cum_t_ref[pl.ds(2 * pair + k, 1), :] for k in range(2)]
        outs = []
        for part in range(length // LANES):
            rows = slice(part * LANES, (part + 1) * LANES)
            wide = (part + 1) * LANES
            pieces = []
            for k in range(2):
                decay = jnp.exp(cum_cols[k][rows] - cum_rows[k][:, :wide] + neg_ref[rows, :wide])
                mixed = (decay * scores_ref[rows, :wide]).astype(bf16)
                pieces.append(dot(mixed, scaled[:wide]))
            outs.append(jnp.where(lanes < HEAD_DIM, pieces[0], pieces[1]))
        full_y = jnp.concatenate(outs, axis=0) + cols_ref[1:2, at] * values
        y_ref[:, at] = full_y.astype(bf16)
        gated = full_y * jax.nn.silu(packed_ref[:, at].astype(f32))
        square_ref[...] += gated * gated
        act_ref[:, at] = (gated * cols_ref[0:1, at]).astype(bf16)

    @pl.loop(0, D // step)
    def _(part):
        at = pl.ds(pl.multiple_of(part * step, step), step)
        out_ref[:, at] = dot(act_ref[...], wout_ref[:, at]).astype(bf16)

    squares = jnp.sum(square_ref[...], axis=1, keepdims=True)
    out_ref[:, D:] = word_lanes(squares)


def word_lanes(column):
    lanes = lax.broadcasted_iota(jnp.int32, (column.shape[0], LANES), 1)
    words = [word.astype(f32) for word in split_words(column)]
    row = jnp.where(lanes == 0, words[0], jnp.where(lanes == 1, words[1], words[2]))
    return jnp.where(lanes < 3, row, 0.0).astype(bf16)


def word_sum(words):
    return words[:, 0:1].astype(f32) + words[:, 1:2].astype(f32) + words[:, 2:3].astype(f32)


def backward_kernel(hid_ref, scale_ref, wout_ref, conv_ref, masks_ref, head_ref, cols_ref,
                    doc_col_ref, doc_row_ref, packed_ref, dt_ref, y_ref,
                    proj_ref, conv_grad_ref, cols_grad_ref, head_grad_ref,
                    neg_ref, scores_ref, cum_ref, cum_t_ref, grad_scores_ref, row_ref, col_ref,
                    step_ref, scaled_ref, low_ref):
    length = dt_ref.shape[0]
    inner = wout_ref.shape[0]
    body = packed_ref.shape[1]
    masks = masks_ref[...]
    pre_step, dt_step, log_decay, exact, b_out, c_out, b_low, c_low = scan_setup(
        dt_ref, packed_ref, conv_ref, masks, head_ref, doc_col_ref[...], doc_row_ref[...], inner,
        neg_ref, scores_ref, cum_ref, cum_t_ref,
    )
    grad_scores_ref[...] = jnp.zeros_like(grad_scores_ref)
    row_ref[...] = jnp.zeros_like(row_ref)
    col_ref[...] = jnp.zeros_like(col_ref)
    step_ref[...] = jnp.zeros_like(step_ref)
    conv_grad_ref[...] = jnp.zeros_like(conv_grad_ref)
    cols_grad_ref[...] = jnp.zeros_like(cols_grad_ref)
    head_grad_ref[...] = jnp.zeros_like(head_grad_ref)
    scale_mix = word_sum(scale_ref[...])
    row_mean = word_sum(hid_ref[:, D:])
    lanes_all = lax.broadcasted_iota(jnp.int32, (length, LANES), 1)
    lanes = lax.broadcasted_iota(jnp.int32, (LANES, LANES), 1)

    @pl.loop(0, inner // LANES)
    def _(pair):
        at, x_at = pair_slices(pair, inner)
        grad_act = dot_nt(hid_ref[:, :D], wout_ref[at, :])
        conv_in = packed_ref[:, x_at].astype(f32)
        conv_out = conv_rows(conv_in, masks, conv_ref[:, at])
        values = jax.nn.silu(conv_out)
        gate_z = packed_ref[:, at].astype(f32)
        gate_act = jax.nn.silu(gate_z)
        full_y = y_ref[:, at].astype(f32)
        normed_mix = full_y * gate_act * scale_mix
        gain = cols_ref[0:1, at]
        skip = cols_ref[1:2, at]
        cols_grad_ref[0:1, at] = jnp.sum(grad_act * normed_mix, axis=0, keepdims=True)
        grad_gated = scale_mix * (grad_act * gain - normed_mix * row_mean)
        grad_y = grad_gated * gate_act
        proj_ref[:, at] = (grad_gated * full_y * silu_slope(gate_z)).astype(bf16)
        cols_grad_ref[1:2, at] = jnp.sum(grad_y * values, axis=0, keepdims=True)
        dt_wide = dot_words_left(dt_step, head_lanes(pair))
        scaled_low = (values * dt_wide).astype(bf16)
        low_ref[...] = grad_y.astype(bf16)
        scaled_ref[...] = jnp.zeros_like(scaled_ref)
        for k in range(2):
            head = 2 * pair + k
            cum_col = lane_of(cum_ref[...], head)
            cum_row = cum_t_ref[pl.ds(head, 1), :]
            for part in range(length // LANES):
                rows = slice(part * LANES, (part + 1) * LANES)
                wide = (part + 1) * LANES
                decay = jnp.exp(cum_col[rows] - cum_row[:, :wide] + neg_ref[rows, :wide])
                mixed = decay * scores_ref[rows, :wide]
                mine = jnp.where(lanes // HEAD_DIM == k, low_ref[rows, :].astype(f32), 0.0)
                mine = mine.astype(bf16)
                grad_mixed = dot_nt(mine, scaled_low[:wide])
                grad_scores_ref[rows, :wide] += grad_mixed * decay
                product = grad_mixed * mixed
                row_ref[rows, :] += jnp.where(
                    lanes == head, jnp.sum(product, axis=1, keepdims=True), 0.0
                )
                sums = jnp.sum(product, axis=0, keepdims=True)
                if part < length // LANES - 1:
                    sums = jnp.concatenate(
                        [sums, jnp.zeros((1, length - wide), f32)], axis=1
                    )
                col_sums = sums if part == 0 else col_sums + sums
                scaled_ref[:wide, :] += dot_tn(mixed.astype(bf16), mine)
            col_ref[pl.ds(head, 1), :] = col_sums
        grad_scaled = scaled_ref[...]
        step_ref[...] += dot_words_left(grad_scaled * values, head_lanes(pair, True))
        grad_values = grad_scaled * dt_wide + grad_y * skip
        grad_rows, taps = conv_rows_back(
            grad_values * silu_slope(conv_out), conv_in, masks, conv_ref[:, at]
        )
        proj_ref[:, x_at] = grad_rows.astype(bf16)
        for k in range(CONV + 1):
            conv_grad_ref[k : k + 1, at] = taps[k]

    grad_scores = grad_scores_ref[...].astype(bf16)
    for number, (grad, before) in enumerate(
        ((dot_tn(grad_scores, c_low), b_out), (dot(grad_scores, b_low), c_out))
    ):
        start = inner + number * STATE
        conv_in = packed_ref[:, inner + start : inner + start + STATE].astype(f32)
        grad_rows, taps = conv_rows_back(
            grad * silu_slope(before), conv_in, masks, conv_ref[:, start : start + STATE]
        )
        proj_ref[:, inner + start : inner + start + STATE] = grad_rows.astype(bf16)
        for k in range(CONV + 1):
            conv_grad_ref[k : k + 1, start : start + STATE] = taps[k]
    grad_cum = row_ref[...] - col_ref[...].T
    grad_decay = dot_words(exact, grad_cum, ((0,), (0,)))
    rate_abs = head_ref[0:1]
    grad_pre = (step_ref[...] - grad_decay * rate_abs) * jax.nn.sigmoid(pre_step)
    head_grad_ref[0:1] = jnp.sum(grad_decay * log_decay, axis=0, keepdims=True)
    head_grad_ref[1:2] = jnp.sum(grad_pre, axis=0, keepdims=True)
    proj_ref[:, body:] = grad_pre.astype(bf16)


def route_kernel(two_ref, cot_ref, routes_ref, router_ref, ids_ref,
                 in_ref, top_ref, grad_ref, weights_ref, pick_ref):
    tok = two_ref.shape[0]
    held, capacity, _ = in_ref.shape
    rows = two_ref[:, :D]
    logits = dot(rows, router_ref[...])
    lanes = lax.broadcasted_iota(jnp.int32, (tok, LANES), 1)
    named = lanes < 0
    for k in range(routes_ref.shape[1]):
        named = named | (lanes == routes_ref[:, k : k + 1])
    top_logit = jnp.max(jnp.where(named, logits, -1e30), axis=1, keepdims=True)
    raised = jnp.where(named, jnp.exp(jnp.where(named, logits - top_logit, 0.0)), 0.0)
    weights = raised / jnp.sum(raised, axis=1, keepdims=True)
    weights_ref[...] = weights
    at = lax.broadcasted_iota(jnp.int32, (tok, tok), 0)
    to = lax.broadcasted_iota(jnp.int32, (tok, tok), 1)
    named_f = named.astype(f32)
    slot = dot((at > to).astype(f32).astype(bf16), named_f.astype(bf16))
    slots = lax.broadcasted_iota(jnp.int32, (tok, capacity), 1).astype(f32)
    picks = []
    for expert in range(held):
        lane = ids_ref[0] + expert
        mine = (lane_of(slot, lane) == slots) & (lane_of(named_f, lane) > 0.0)
        pick = mine.astype(f32).astype(bf16)
        picks.append(pick)
        in_ref[expert] = dot_tn(pick, rows).astype(bf16)
        top = dot_tn(pick, cot_ref[...])
        top_ref[expert] = top.astype(bf16)
        words = word_lanes(lane_of(weights, lane))
        slot_weight = jnp.sum(dot_tn(pick, words), axis=1, keepdims=True)
        grad_ref[expert] = (top * slot_weight).astype(bf16)
    pick_ref[0] = jnp.concatenate(picks, axis=1)


def shared_kernel(two_ref, cot_ref, sgu_ref, sd_ref, out_ref, back_ref, grad_gu_ref, grad_down_ref,
                  mid_ref, act_ref):
    width = sd_ref.shape[0]
    gate = dot(two_ref[:, :D], sgu_ref[:, :width])
    up = dot(two_ref[:, :D], sgu_ref[:, width:])
    silu = jax.nn.silu(gate)
    mid_ref[...] = (silu * up).astype(bf16)
    grad_mid = dot_nt(cot_ref[...], sd_ref[...])
    act_ref[:, :width] = (grad_mid * up * silu_slope(gate)).astype(bf16)
    act_ref[:, width:] = (grad_mid * silu).astype(bf16)

    @pl.loop(0, D // 256)
    def _(part):
        at = pl.ds(pl.multiple_of(part * 256, 256), 256)
        out_ref[:, at] = dot(mid_ref[...], sd_ref[:, at]).astype(bf16)
        back_ref[:, at] = dot_nt(act_ref[...], sgu_ref[at, :]).astype(bf16)
        grad_gu_ref[at, :] = dot_tn(two_ref[:, at], act_ref[...]).astype(bf16)
        grad_down_ref[:, at] = dot_tn(mid_ref[...], cot_ref[:, at]).astype(bf16)


def expert_kernel(in_ref, top_ref, grad_ref, gu_ref, down_ref, out_ref, back_ref, q_ref, sums_ref,
                  mid_ref, act_ref):
    mates, _, halves, rows_gu, _ = gu_ref.shape
    rows_down = down_ref.shape[3]
    shards = [(h, m) for h in range(halves) for m in range(mates)]

    def gu(at, which=shards):
        return jnp.concatenate([gu_ref[m, 0, h, :, at] for h, m in which], axis=0)

    def down(at):
        return jnp.concatenate([down_ref[m, 0, h, :, at] for h, m in shards], axis=0)

    for part in range(EXPERT_FF // 256):
        at = slice(part * 256, (part + 1) * 256)
        up_at = slice(EXPERT_FF + part * 256, EXPERT_FF + (part + 1) * 256)
        gate = dot(in_ref[0], gu(at))
        up = dot(in_ref[0], gu(up_at))
        silu = jax.nn.silu(gate)
        mid_ref[:, at] = (silu * up).astype(bf16)
        each = 256 // rows_down
        rows = jnp.concatenate(
            [down_ref[m, 0, h, :, :] for h, m in shards[part * each : (part + 1) * each]], axis=0
        )
        grad_mid = dot_nt(grad_ref[0], rows)
        act_ref[:, at] = (grad_mid * up * silu_slope(gate)).astype(bf16)
        act_ref[:, up_at] = (grad_mid * silu).astype(bf16)
    step = 384
    each = step // rows_gu
    q = jnp.zeros((in_ref.shape[1], 1), f32)
    for part in range(D // step):
        at = slice(part * step, (part + 1) * step)
        rows = dot(mid_ref[...], down(at))
        out_ref[0, :, at] = rows.astype(bf16)
        q = q + jnp.sum(rows * top_ref[0, :, at].astype(f32), axis=1, keepdims=True)
        chosen = shards[part * each : (part + 1) * each]
        back_ref[0, :, at] = dot_nt(act_ref[...], gu(slice(None), chosen)).astype(bf16)
        for number in range(2):
            half_at = slice(number * EXPERT_FF, (number + 1) * EXPERT_FF)
            total = dot_tn(in_ref[0, :, at], act_ref[:, half_at]).astype(bf16)
            for k, (h, m) in enumerate(chosen):
                sums_ref[m, h, 0, number * rows_gu : (number + 1) * rows_gu, :] = total[
                    k * rows_gu : (k + 1) * rows_gu
                ]
    q_ref[0] = jnp.broadcast_to(q, q_ref.shape[1:])
    for part in range(D // EXPERT_FF):
        total = dot_tn(mid_ref[...], grad_ref[0, :, part * EXPERT_FF : (part + 1) * EXPERT_FF])
        total = total.astype(bf16)
        start = 2 * rows_gu + part * rows_down
        for k, (h, m) in enumerate(shards):
            sums_ref[m, h, 0, start : start + rows_down, :] = total[
                k * rows_down : (k + 1) * rows_down
            ]


def combine_kernel(pick_ref, weights_ref, ids_ref, out_ref, back_ref, q_ref, own_out_ref,
                   own_back_ref, mix_ref, rows_ref):
    held = out_ref.shape[0]
    capacity = out_ref.shape[1]
    block = pl.program_id(0)
    own = (block < pl.num_programs(0) // 2).astype(f32)
    picks = [pick_ref[0, :, e * capacity : (e + 1) * capacity] for e in range(held)]
    mix = own_out_ref[...].astype(f32) * own
    back = own_back_ref[...].astype(f32) * own
    lanes = lax.broadcasted_iota(jnp.int32, (pick_ref.shape[1], LANES), 1)
    words = jnp.zeros((pick_ref.shape[1], LANES), f32)
    for expert in range(held):
        weight = lane_of(weights_ref[...], ids_ref[0] + expert)
        mix = mix + weight * dot(picks[expert], out_ref[expert])
        back = back + dot(picks[expert], back_ref[expert])
        token_q = jnp.sum(dot(picks[expert], word_lanes(q_ref[expert, :, :1])), axis=1,
                          keepdims=True)
        for k, word in enumerate(split_words(token_q)):
            words = jnp.where(lanes == k * held + expert, word.astype(f32), words)
    mix_ref[...] = mix.astype(bf16)
    rows_ref[:, :D] = back.astype(bf16)
    rows_ref[:, D:] = words.astype(bf16)


def peers():
    count = lax.axis_size("expert")
    me = lax.axis_index("expert")
    return count, me, [lax.rem(me + step, count) for step in range(1, count)]


def greet(with_partner):
    count, me, others = peers()
    barrier = pltpu.get_barrier_semaphore()
    for other in others:
        pl.semaphore_signal(
            barrier, inc=1, device_id={"expert": other}, device_id_type=pl.DeviceIdType.MESH
        )
    if with_partner:
        pl.semaphore_signal(
            barrier, inc=1, device_id={"zhi": 1 - lax.axis_index("zhi")},
            device_id_type=pl.DeviceIdType.MESH,
        )
    pl.semaphore_wait(barrier, count - 1 + (1 if with_partner else 0))


def remote(src, dst, sems, number, target):
    return pltpu.make_async_remote_copy(
        src_ref=src, dst_ref=dst, send_sem=sems[0].at[number], recv_sem=sems[1].at[number],
        device_id=target, device_id_type=pl.DeviceIdType.MESH,
    )


def spread_copies(src, dst, sems, base):
    _, me, others = peers()
    return [
        remote(src, dst.at[me], sems, base + number, {"expert": other})
        for number, other in enumerate(others)
    ]


def reduce_copies(src, dst, sems, base, rows, start):
    _, _, others = peers()
    return [
        remote(
            src.at[pl.ds(pl.multiple_of(start + other * rows, rows), rows)],
            dst.at[number], sems, base + number, {"expert": other},
        )
        for number, other in enumerate(others)
    ]


def reduced(src, dst, rows, start, columns):
    _, me, others = peers()
    total = src[pl.ds(pl.multiple_of(start + me * rows, rows), rows), columns].astype(f32)
    for number in range(len(others)):
        total = total + dst[number, :, columns].astype(f32)
    return total


def hidden_kernel(part_ref, tokens_ref, gain_ref, hidden_ref, res_ref, two_ref,
                  got_ref, send_sems, recv_sems):
    tok = tokens_ref.shape[0]
    sems = (send_sems, recv_sems)
    greet(False)
    copies = reduce_copies(part_ref, got_ref, sems, 0, tok, 0)
    for copy in copies:
        copy.start()
    for copy in copies:
        copy.wait()
    squares = word_sum(reduced(part_ref, got_ref, tok, 0, slice(D, D + LANES)))
    scale_mix = lax.rsqrt(squares / INNER + norm_eps)
    res = reduced(part_ref, got_ref, tok, 0, slice(0, D)) * scale_mix
    res_ref[...] = res
    hidden = tokens_ref[...].astype(f32) + res
    hidden_ref[...] = hidden
    scale = lax.rsqrt(jnp.mean(hidden * hidden, axis=1, keepdims=True) + norm_eps)
    two_ref[:, :D] = (hidden * scale * gain_ref[1:2]).astype(bf16)
    two_ref[:, D:] = word_lanes(scale_mix)


def share_kernel(two_ref, own_ref, other_ref, came_ref, send_sems, recv_sems, local_sems):
    count, me, _ = peers()
    sems = (send_sems, recv_sems)
    greet(True)
    over = remote(two_ref, came_ref, sems, 0, {"zhi": 1 - lax.axis_index("zhi")})
    over.start()
    first = spread_copies(two_ref, own_ref, sems, 1)
    for copy in first:
        copy.start()
    mine = pltpu.make_async_copy(two_ref, own_ref.at[me], local_sems.at[0])
    mine.start()
    over.wait()
    second = spread_copies(came_ref, other_ref, sems, count)
    for copy in second:
        copy.start()
    theirs = pltpu.make_async_copy(came_ref, other_ref.at[me], local_sems.at[1])
    theirs.start()
    for copy in first + second:
        copy.wait()
    mine.wait()
    theirs.wait()


def q_lanes(sources, held, own_experts, half):
    lanes = lax.broadcasted_iota(jnp.int32, sources[0][1].shape, 1)
    total = jnp.zeros(lanes.shape, f32)
    for place, words in sources:
        for expert in range(held):
            value = sum(
                words[:, k * held + expert : k * held + expert + 1].astype(f32) for k in range(3)
            )
            lane = place * own_experts + half * held + expert
            total = jnp.where(lanes == lane, value, total)
    return total


def back_kernel(back_ref, hidden_ref, res_ref, cot_ref, weights_ref, router_ref, gain_ref,
                all_ref, grad_hidden_ref, grad_logits_ref, gain_grad_ref,
                got_other_ref, got_own_ref, send_ref, came_ref, low_ref, send_sems, recv_sems,
                local_sem, *, own_experts):
    tok = cot_ref.shape[0]
    length = back_ref.shape[0] // 2
    held = own_experts // 2
    count, me, others = peers()
    half = lax.axis_index("zhi")
    sems = (send_sems, recv_sems)
    words_at = slice(D, D + LANES)
    greet(True)
    first = reduce_copies(back_ref, got_other_ref, sems, 0, tok, length)
    second = reduce_copies(back_ref, got_own_ref, sems, count - 1, tok, 0)
    for copy in first + second:
        copy.start()

    def q_of(start, slots):
        mine = back_ref[pl.ds(pl.multiple_of(start + me * tok, tok), tok), words_at]
        sources = [(me, mine)]
        for number in range(count - 1):
            sources.append((lax.rem(me + count - 1 - number, count), slots[number, :, words_at]))
        return q_lanes(sources, held, own_experts, half)

    for copy in first:
        copy.wait()
    send_ref[:, :D] = reduced(back_ref, got_other_ref, tok, length, slice(0, D)).astype(bf16)
    lanes = lax.broadcasted_iota(jnp.int32, (tok, LANES), 1)
    words = jnp.zeros((tok, LANES), f32)
    shift = LANES // 4
    for k, word in enumerate(split_words(q_of(length, got_other_ref))):
        placed = word.astype(f32) if k == 0 else pltpu.roll(word.astype(f32), k * shift, 1)
        words = words + placed
    send_ref[:, D:] = words.astype(bf16)
    over = remote(send_ref, came_ref, sems, 2 * (count - 1), {"zhi": 1 - half})
    over.start()
    for copy in second:
        copy.wait()
    q_own = q_of(0, got_own_ref)
    total = reduced(back_ref, got_own_ref, tok, 0, slice(0, D))
    over.wait()
    came = came_ref[:, D:].astype(f32)
    came = came + pltpu.roll(came, LANES - shift, 1) + pltpu.roll(came, LANES - 2 * shift, 1)
    q = q_own + jnp.where(lanes < shift, came, 0.0)
    weights = weights_ref[...]
    grad_logits = weights * (q - jnp.sum(weights * q, axis=1, keepdims=True))
    grad_logits_ref[...] = grad_logits.astype(bf16)
    total = total + came_ref[:, :D].astype(f32) + dot_nt(grad_logits_ref[...], router_ref[...])
    hidden = hidden_ref[...]
    scale = lax.rsqrt(jnp.mean(hidden * hidden, axis=1, keepdims=True) + norm_eps)
    unit = hidden * scale
    gain_grad_ref[...] = jnp.broadcast_to(
        jnp.sum(total * unit, axis=0, keepdims=True), gain_grad_ref.shape
    )
    grad_hidden = cot_ref[...].astype(f32) + norm_back(total, unit, scale, gain_ref[1:2])
    grad_hidden_ref[...] = grad_hidden
    low_ref[:, :D] = grad_hidden.astype(bf16)
    row_mean = jnp.sum(low_ref[:, :D].astype(f32) * res_ref[...], axis=1, keepdims=True) / INNER
    low_ref[:, D:] = word_lanes(row_mean)
    third = spread_copies(low_ref, all_ref, sems, 2 * count - 1)
    for copy in third:
        copy.start()
    mine = pltpu.make_async_copy(low_ref, all_ref.at[me], local_sem)
    mine.start()
    for copy in third:
        copy.wait()
    mine.wait()


def remote_call(kernel, number, out_shapes, scratch, sems, *operands):
    spec = pl.BlockSpec(memory_space=pltpu.VMEM)
    return pl.pallas_call(
        kernel,
        out_shape=out_shapes,
        in_specs=[spec] * len(operands),
        out_specs=[spec] * len(out_shapes),
        scratch_shapes=[pltpu.VMEM(shape, dtype) for shape, dtype in scratch] + sems,
        compiler_params=pltpu.CompilerParams(
            collective_id=number, has_side_effects=True, vmem_limit_bytes=48 * 1024 * 1024
        ),
    )(*operands)


def vmem_call(kernel, out_shapes, scratch, *operands):
    spec = pl.BlockSpec(memory_space=pltpu.VMEM)
    return pl.pallas_call(
        kernel,
        out_shape=out_shapes,
        in_specs=[spec] * len(operands),
        out_specs=[spec] * len(out_shapes),
        scratch_shapes=[pltpu.VMEM(shape, dtype) for shape, dtype in scratch],
        compiler_params=pltpu.CompilerParams(vmem_limit_bytes=56 * 1024 * 1024),
    )(*operands)


def grid_call(kernel, steps, in_specs, out_specs, out_shapes, scratch, *operands):
    return pl.pallas_call(
        kernel,
        grid=(steps,),
        out_shape=out_shapes,
        in_specs=in_specs,
        out_specs=out_specs,
        scratch_shapes=[pltpu.VMEM(shape, dtype) for shape, dtype in scratch],
        compiler_params=pltpu.CompilerParams(vmem_limit_bytes=56 * 1024 * 1024),
    )(*operands)


def sgu_rows(grad):
    copies = lax.axis_size("zhi") * lax.axis_size("zlo") * lax.axis_size("core")
    wide = D // grad.shape[1]
    pieces = grad.reshape(copies, wide, -1, grad.shape[1])
    return jnp.concatenate([pieces[:, k] for k in range(wide)], axis=2)


def on_device(
    tokens, cotangent, lengths, routes,
    w_in, w_in_first, w_in_second,
    w_out, w_out_first, w_out_second,
    w_router, w_router_first, w_router_second,
    w_shared_gu, w_shared_gu_first, w_shared_gu_second,
    w_shared_down, w_shared_down_first, w_shared_down_second,
    w_expert_gu, w_expert_gu_first, w_expert_gu_second,
    w_expert_down, w_expert_down_first, w_expert_down_second,
    norm_gains, norm_gains_first, norm_gains_second,
    conv_params, conv_params_first, conv_params_second,
    head_params, head_params_first, head_params_second,
    mixer_gain, mixer_gain_first, mixer_gain_second,
):
    groups = lax.axis_size("expert")
    copies = (lax.axis_size("zhi") * lax.axis_size("zlo") * lax.axis_size("core"))
    place = lax.axis_index("expert")
    tok = tokens.shape[0]
    length = tok * groups
    top = routes.shape[1]
    experts = w_router.shape[1]
    own_experts = w_expert_gu.shape[0]
    capacity = (4 * tok * top + 3 * experts - 1) // (3 * experts)
    inner = INNER // groups
    heads = HEADS // groups
    rows_in = w_in.shape[0]
    rows_out = w_out.shape[0]
    rows_sd = w_shared_down.shape[0]
    own_ff = SHARED_FF // groups
    per_pair = copies // groups
    conv_cols = inner + 2 * STATE
    body = 2 * inner + 2 * STATE

    w_in_low = w_in.astype(bf16)
    z_cols = w_in_low[:, :INNER].reshape(rows_in, groups, inner)
    x_cols = w_in_low[:, INNER : 2 * INNER].reshape(rows_in, groups, inner)
    bc_cols = jnp.broadcast_to(
        w_in_low[:, None, 2 * INNER : 2 * INNER + 2 * STATE], (rows_in, groups, 2 * STATE)
    )
    dt_cols = w_in_low[:, 2 * INNER + 2 * STATE :].reshape(rows_in, groups, heads)
    router_cols = jnp.broadcast_to(
        w_router.astype(bf16)[:, None], (rows_in, groups, experts)
    )
    fill = jnp.zeros((rows_in, groups, LANES - heads - experts), bf16)
    win_pieces = jnp.concatenate(
        [z_cols, x_cols, bc_cols, dt_cols, router_cols, fill], axis=2
    ).transpose(1, 0, 2)
    win_rows = swap(win_pieces, "expert").reshape(groups * rows_in, -1)
    down_own = jnp.concatenate([w_out.astype(bf16), w_shared_down.astype(bf16)], axis=0)
    win = lax.all_gather(win_rows, DP, axis=0, tiled=True)
    router = win[:, body + heads : body + heads + experts]
    both_all = spread(jnp.stack([tokens, cotangent]), "expert").transpose(1, 0, 2, 3)
    x_all = both_all[0].reshape(length, D)
    cot_all = both_all[1].reshape(length, D)
    routes_two = spread(jnp.stack([routes, to_partner(routes)]), "expert")
    routes_two = routes_two.transpose(1, 0, 2, 3).reshape(2 * length, top)

    rows_two = rows_out + rows_sd
    down_rows = lax.all_gather(down_own, DP, axis=0, tiled=False)
    sd = down_rows[:, rows_out:].reshape(own_ff, D)
    wout = (
        swap(down_rows[:, :rows_out].reshape(groups, per_pair * rows_out, D), "expert")
        .reshape(groups, per_pair, rows_out, D)
        .transpose(1, 0, 2, 3)
        .reshape(inner, D)
    )
    sgu_pieces = (
        w_shared_gu.astype(bf16)
        .reshape(rows_in, 2, copies, groups, rows_sd)
        .transpose(3, 0, 1, 2, 4)
        .reshape(groups, rows_in, 2 * own_ff)
    )
    sgu = lax.all_gather(
        swap(sgu_pieces, "expert").reshape(groups * rows_in, 2 * own_ff), DP, axis=0, tiled=True
    )

    half = lax.axis_index("zhi")
    held = own_experts // 2
    rows_egu, rows_ed = w_expert_gu.shape[1], w_expert_down.shape[1]

    def halves(shard):
        kept = lax.dynamic_slice_in_dim(shard, half * held, held, axis=0)
        sent = lax.dynamic_slice_in_dim(shard, (1 - half) * held, held, axis=0)
        return kept, sent

    def gathered(kept, came):
        both = jnp.where(half == 0, jnp.stack([kept, came], 1), jnp.stack([came, kept], 1))
        return lax.all_gather(both, MATES, axis=0, tiled=False)

    egu_own, ed_own = w_expert_gu.astype(bf16), w_expert_down.astype(bf16)
    win, wout, routes_two, x_all, egu_own, ed_own, cot_own = lax.optimization_barrier(
        (win, wout, routes_two, x_all, egu_own, ed_own, cotangent)
    )
    cot_other = to_partner(cot_own)
    egu_kept, egu_sent = halves(egu_own)
    ed_kept, ed_sent = halves(ed_own)
    egu_came = to_partner(egu_sent)
    ed_came = to_partner(ed_sent)

    positions = jnp.arange(length, dtype=jnp.int32)
    starts = jnp.cumsum(lengths[0]) - lengths[0]
    doc_index = jnp.sum((starts[None, :] <= positions[:, None]).astype(jnp.int32), axis=1) - 1
    earlier_doc = [
        jnp.concatenate([jnp.full((offset,), -1, jnp.int32), doc_index[: length - offset]])
        for offset in range(CONV)
    ]
    masks = jnp.stack([(earlier == doc_index).astype(f32) for earlier in earlier_doc], axis=1)
    masks = jnp.pad(masks, ((0, 0), (0, LANES - CONV)))
    doc_col, doc_row = doc_index[:, None], doc_index[None, :]

    own_x = place * inner
    conv_own = jnp.concatenate(
        [
            lax.dynamic_slice_in_dim(conv_params, own_x, inner, axis=1),
            conv_params[:, INNER:],
        ],
        axis=1,
    )
    head_own = lax.dynamic_slice_in_dim(head_params, place * heads, heads, axis=1)
    gain_own = lax.dynamic_slice_in_dim(mixer_gain, own_x, inner, axis=0)

    conv_pad = jnp.pad(conv_own, ((0, 3), (0, 0)))
    rate_abs = jnp.exp(head_own[0])
    head_rows = jnp.pad(jnp.stack([rate_abs, head_own[1]]), ((0, 6), (0, LANES - heads)))
    col_rows = jnp.pad(
        jnp.stack([gain_own, jnp.repeat(head_own[2], HEAD_DIM)]), ((0, 6), (0, 0))
    )
    gain_rows = jnp.pad(norm_gains, ((0, 6), (0, 0)))

    square = ((length, length), f32)
    lane_rows = ((length, LANES), f32)
    lane_cols = ((LANES, length), f32)
    packed, dt_raw, full_y, res_part = vmem_call(
        forward_kernel,
        [
            jax.ShapeDtypeStruct((length, body), bf16),
            jax.ShapeDtypeStruct((length, LANES), f32),
            jax.ShapeDtypeStruct((length, inner), bf16),
            jax.ShapeDtypeStruct((length, D + LANES), bf16),
        ],
        [((length, D), bf16), square, square, lane_rows, lane_cols, ((length, inner), bf16),
         lane_rows],
        x_all, win, gain_rows, conv_pad, masks, head_rows, col_rows, doc_col, doc_row, wout,
    )
    pairs = pltpu.SemaphoreType.DMA
    payload = ((tok, D + LANES), bf16)
    hidden, mixer_res, two_own = remote_call(
        hidden_kernel, 0,
        [
            jax.ShapeDtypeStruct((tok, D), f32),
            jax.ShapeDtypeStruct((tok, D), f32),
            jax.ShapeDtypeStruct((tok, D + LANES), bf16),
        ],
        [((groups - 1, tok, D + LANES), bf16)],
        [pairs((groups - 1,)), pairs((groups - 1,))],
        res_part, tokens, gain_rows,
    )
    egu_came, ed_came, cot_other, two_own = lax.optimization_barrier(
        (egu_came, ed_came, cot_other, two_own)
    )
    egu = gathered(egu_kept, egu_came)
    ed = gathered(ed_kept, ed_came)
    gathered_shape = jax.ShapeDtypeStruct((groups, tok, D + LANES), bf16)
    got, other_two = remote_call(
        share_kernel, 1, [gathered_shape] * 2, [payload],
        [pairs((2 * groups - 1,)), pairs((2 * groups - 1,)), pairs((2,))],
        two_own,
    )
    got = got.reshape(length, -1)
    other_two = other_two.reshape(length, -1)
    scale_words = got[:, D:]
    cot_other = spread(cot_other, "expert").reshape(length, D)

    blocks = 2 * groups
    expert_at = (place * own_experts + half * held).reshape(1)
    two_rows = jnp.concatenate([got, other_two], axis=0)
    cot_two = jnp.concatenate([cot_all, cot_other], axis=0)
    router_lanes = jnp.pad(router, ((0, 0), (0, LANES - experts)))
    slot_rows = blocks * capacity

    def by_block(*shape):
        return pl.BlockSpec(shape, lambda b: (b,) + (0,) * (len(shape) - 1))

    def fixed(*shape):
        return pl.BlockSpec(shape, lambda b: (0,) * len(shape))

    slot_spec = pl.BlockSpec((held, capacity, D), lambda b: (0, b, 0))
    in_smem = pl.BlockSpec(memory_space=pltpu.SMEM)
    slot_shape = jax.ShapeDtypeStruct((held, slot_rows, D), bf16)
    slot_in, slot_top, slot_grad, weights, pick = grid_call(
        route_kernel, blocks,
        [by_block(tok, D + LANES), by_block(tok, D), by_block(tok, top), fixed(D, LANES), in_smem],
        [slot_spec] * 3 + [by_block(tok, LANES), by_block(1, tok, held * capacity)],
        [slot_shape] * 3
        + [
            jax.ShapeDtypeStruct((2 * length, LANES), f32),
            jax.ShapeDtypeStruct((blocks, tok, held * capacity), bf16),
        ],
        [],
        two_rows, cot_two, routes_two, router_lanes, expert_at,
    )
    shared_out, shared_back, grad_sgu, grad_sd = vmem_call(
        shared_kernel,
        [
            jax.ShapeDtypeStruct((length, D), bf16),
            jax.ShapeDtypeStruct((length, D), bf16),
            jax.ShapeDtypeStruct((D, 2 * own_ff), bf16),
            jax.ShapeDtypeStruct((own_ff, D), bf16),
        ],
        [((length, own_ff), bf16), ((length, 2 * own_ff), bf16)],
        got, cot_all, sgu, sd,
    )

    mates = copies // 2
    packed_rows = 2 * rows_egu + rows_ed * D // EXPERT_FF

    def by_expert(*shape):
        return pl.BlockSpec((1,) + shape, lambda e: (e,) + (0,) * len(shape))

    def weight_spec(rows, columns):
        return pl.BlockSpec((mates, 1, 2, rows, columns), lambda e: (0, e, 0, 0, 0))

    slot_out, slot_back, slot_q, expert_grads = grid_call(
        expert_kernel, held,
        [by_expert(slot_rows, D)] * 3
        + [weight_spec(rows_egu, 2 * EXPERT_FF), weight_spec(rows_ed, D)],
        [by_expert(slot_rows, D)] * 2
        + [
            by_expert(slot_rows, LANES),
            pl.BlockSpec((mates, 2, 1, packed_rows, EXPERT_FF), lambda e: (0, 0, e, 0, 0)),
        ],
        [slot_shape] * 2
        + [
            jax.ShapeDtypeStruct((held, slot_rows, LANES), f32),
            jax.ShapeDtypeStruct((mates, 2, held, packed_rows, EXPERT_FF), bf16),
        ],
        [((slot_rows, EXPERT_FF), bf16), ((slot_rows, 2 * EXPERT_FF), bf16)],
        slot_in, slot_top, slot_grad, egu, ed,
    )
    own_spec = pl.BlockSpec((tok, D), lambda b: (jnp.minimum(b, groups - 1), 0))
    out_parts, back_parts = grid_call(
        combine_kernel, blocks,
        [
            by_block(1, tok, held * capacity), by_block(tok, LANES), in_smem, slot_spec, slot_spec,
            pl.BlockSpec((held, capacity, LANES), lambda b: (0, b, 0)), own_spec, own_spec,
        ],
        [by_block(tok, D), by_block(tok, D + LANES)],
        [
            jax.ShapeDtypeStruct((2 * length, D), bf16),
            jax.ShapeDtypeStruct((2 * length, D + LANES), bf16),
        ],
        [],
        pick, weights, expert_at, slot_out, slot_back, slot_q, shared_out, shared_back,
    )

    weights_tok = lax.dynamic_slice_in_dim(weights, place * tok, tok, axis=0)
    hidden_all, grad_hidden, grad_logits, gain_two = remote_call(
        functools.partial(back_kernel, own_experts=own_experts), 2,
        [
            gathered_shape,
            jax.ShapeDtypeStruct((tok, D), f32),
            jax.ShapeDtypeStruct((tok, LANES), bf16),
            jax.ShapeDtypeStruct((8, D), f32),
        ],
        [((groups - 1, tok, D + LANES), bf16)] * 2 + [payload] * 3,
        [pairs((3 * groups - 2,)), pairs((3 * groups - 2,)), pairs(())],
        back_parts, hidden, mixer_res, cotangent, weights_tok, router_lanes, gain_rows,
    )
    hidden_all = hidden_all.reshape(length, -1)
    grad_gain_two = gain_two[0]
    grad_router = dot_tn(two_own[:, :D], grad_logits[:, :experts])

    out_parts, hidden_all = lax.optimization_barrier((out_parts, hidden_all))
    out_own, out_other = out_parts[:length], out_parts[length:]
    other_out = swap(out_other.reshape(groups, tok, D), "expert")
    other_out = to_partner(jnp.sum(other_out.astype(f32), axis=0).astype(bf16))
    own_out = swap(out_own.reshape(groups, tok, D), "expert")

    expert_mine = lax.psum_scatter(
        expert_grads.reshape(-1, EXPERT_FF), MATES, scatter_dimension=0, tiled=True
    ).reshape(expert_grads.shape[1:])

    gate_z = packed[:, :inner].astype(f32)
    mixer_act = (
        full_y.astype(f32) * jax.nn.silu(gate_z) * word_sum(scale_words) * gain_own
    ).astype(bf16)
    grad_wout = dot_tn(mixer_act, hidden_all[:, :D]).astype(bf16)
    wout_send = (
        grad_wout.reshape(per_pair, groups, rows_out, D)
        .transpose(1, 0, 2, 3)
        .reshape(groups, per_pair * rows_out, D)
    )
    wout_got = swap(wout_send, "expert").reshape(copies, rows_out, D)
    grad_proj, conv_grads, col_grads, head_grads = vmem_call(
        backward_kernel,
        [
            jax.ShapeDtypeStruct((length, body + LANES), bf16),
            jax.ShapeDtypeStruct((8, conv_cols), f32),
            jax.ShapeDtypeStruct((8, inner), f32),
            jax.ShapeDtypeStruct((8, LANES), f32),
        ],
        [square, square, lane_rows, lane_cols, square, lane_rows, lane_cols, lane_rows, lane_rows,
         ((length, LANES), bf16)],
        hidden_all, scale_words, wout, conv_pad, masks, head_rows, col_rows, doc_col, doc_row,
        packed, dt_raw, full_y,
    )
    conv_grads = conv_grads[: CONV + 1]
    grad_gain_mix = col_grads[0]
    grad_skip = jnp.sum(col_grads[1].reshape(heads, HEAD_DIM), axis=1)
    grad_log_rate = head_grads[0, :heads]
    grad_bias = head_grads[1, :heads]
    grad_proj, expert_mine = lax.optimization_barrier((grad_proj, expert_mine))
    inputs = x_all.astype(f32)
    normed_one = inputs * rms_scale(inputs)
    normed = (normed_one * norm_gains[0]).astype(bf16)
    grad_win = (
        dot_tn(normed, grad_proj)
        + jnp.pad(grad_router, ((0, 0), (body + heads, LANES - heads - experts)))
    ).astype(bf16)
    rows_sgu = groups * rows_in * 2 * own_ff // D
    second = jnp.concatenate(
        [wout_got, grad_sd.reshape(copies, rows_sd, D), sgu_rows(grad_sgu)], axis=1
    )
    second = jnp.pad(second, ((0, 0), (0, groups * rows_in - second.shape[1]), (0, 0)))
    dense = jnp.concatenate(
        [grad_win.reshape(copies, groups * rows_in, -1), second], axis=2
    )
    dense_mine = lax.psum_scatter(dense, DP, scatter_dimension=0, tiled=True)[0]
    one_part = dot_nt(grad_proj, win)
    grad_gain_one = jnp.sum(one_part * normed_one, axis=0)
    one_low = one_part.astype(bf16)
    one_low, expert_mine, own_out, other_out = lax.optimization_barrier(
        (one_low, expert_mine, own_out, other_out)
    )
    got = swap(one_low.reshape(groups, tok, D), "expert")
    output = (
        hidden + jnp.sum(own_out.astype(f32), axis=0) + other_out.astype(f32)
    ).astype(bf16)
    kept = lax.dynamic_index_in_dim(expert_mine, half, 0, False)
    came = to_partner(lax.dynamic_index_in_dim(expert_mine, 1 - half, 0, False))
    expert_sum = jnp.where(
        half == 0, jnp.concatenate([kept, came], 0), jnp.concatenate([came, kept], 0)
    )
    sum_egu = jnp.concatenate(
        [expert_sum[:, :rows_egu], expert_sum[:, rows_egu : 2 * rows_egu]], axis=2
    ).astype(f32)
    sum_ed = jnp.concatenate(
        [
            expert_sum[:, 2 * rows_egu + k * rows_ed : 2 * rows_egu + (k + 1) * rows_ed]
            for k in range(D // EXPERT_FF)
        ],
        axis=2,
    ).astype(f32)

    grad_norm_one = jnp.sum(got.astype(f32), axis=0)
    own_in = tokens.astype(f32)
    own_scale = rms_scale(own_in)
    grad_tokens = (
        grad_hidden + norm_back(grad_norm_one, own_in * own_scale, own_scale, norm_gains[0])
    ).astype(bf16)

    pieces = [
        conv_grads[:, :inner].reshape(-1),
        grad_gain_mix,
        grad_log_rate,
        grad_bias,
        grad_skip,
        conv_grads[:, inner:].reshape(-1),
        grad_gain_one,
        grad_gain_two,
    ]
    sizes = [piece.size for piece in pieces]
    total = sum(sizes)
    unit = copies * LANES
    small = jnp.pad(jnp.concatenate(pieces), (0, -total % unit)).reshape(copies, -1)
    small = jnp.sum(swap(small, DP), axis=0)
    small = spread(small, ("expert",) + DP).reshape(groups, -1)
    parts = []
    start = 0
    for size in sizes:
        parts.append(small[:, start : start + size])
        start += size
    sum_conv = jnp.concatenate(
        [
            parts[0].reshape(groups, CONV + 1, inner).transpose(1, 0, 2).reshape(CONV + 1, INNER),
            jnp.sum(parts[5], axis=0).reshape(CONV + 1, 2 * STATE),
        ],
        axis=1,
    )
    sum_mixer = parts[1].reshape(INNER)
    sum_head = jnp.stack([parts[2].reshape(HEADS), parts[3].reshape(HEADS), parts[4].reshape(HEADS)])
    sum_gains = jnp.stack([jnp.sum(parts[6], axis=0), jnp.sum(parts[7], axis=0)])

    win_mine = dense_mine[:, : body + LANES]
    second_mine = dense_mine[:, body + LANES :]
    sum_out = second_mine[:rows_out].astype(f32)
    sum_sd = second_mine[rows_out:rows_two].astype(f32)
    sgu_mine = jnp.concatenate(
        [
            second_mine[rows_two : rows_two + rows_sgu, k * 2 * own_ff : (k + 1) * 2 * own_ff]
            for k in range(D // (2 * own_ff))
        ],
        axis=0,
    )
    sum_sgu = (
        swap(sgu_mine.reshape(groups, rows_in, 2 * own_ff), "expert")
        .reshape(groups, rows_in, 2, copies, rows_sd)
        .transpose(1, 2, 3, 0, 4)
        .reshape(rows_in, 2 * SHARED_FF)
        .astype(f32)
    )
    win_got = swap(win_mine.reshape(groups, rows_in, -1), "expert").astype(f32)

    def laid(start, size):
        return win_got[:, :, start : start + size].transpose(1, 0, 2).reshape(rows_in, -1)

    sum_in = jnp.concatenate(
        [
            laid(0, inner),
            laid(inner, inner),
            jnp.sum(win_got[:, :, 2 * inner : body], axis=0),
            laid(body, heads),
        ],
        axis=1,
    )
    sum_router = jnp.sum(win_got[:, :, body + heads : body + heads + experts], axis=0)

    up_in = adam_step(w_in, w_in_first, w_in_second, sum_in)
    up_out = adam_step(w_out, w_out_first, w_out_second, sum_out)
    up_router = adam_step(w_router, w_router_first, w_router_second, sum_router)
    up_sgu = adam_step(w_shared_gu, w_shared_gu_first, w_shared_gu_second, sum_sgu)
    up_sd = adam_step(w_shared_down, w_shared_down_first, w_shared_down_second, sum_sd)
    up_egu = adam_step(w_expert_gu, w_expert_gu_first, w_expert_gu_second, sum_egu)
    up_ed = adam_step(w_expert_down, w_expert_down_first, w_expert_down_second, sum_ed)
    up_gains = adam_step(norm_gains, norm_gains_first, norm_gains_second, sum_gains)
    up_conv = adam_step(conv_params, conv_params_first, conv_params_second, sum_conv)
    up_head = adam_step(head_params, head_params_first, head_params_second, sum_head)
    up_mixer = adam_step(mixer_gain, mixer_gain_first, mixer_gain_second, sum_mixer)
    large = (up_in, up_out, up_router, up_sgu, up_sd, up_egu, up_ed)
    little = (up_gains, up_conv, up_head, up_mixer)
    return (
        (output, grad_tokens)
        + tuple(part for one in large for part in one[:4])
        + tuple(part for one in little for part in (one[0], one[4], one[2], one[3]))
    )


def solution(mesh):
    copies, groups = mesh.devices.shape
    split = Mesh(mesh.devices.reshape(2, copies // 4, 2, groups), ALL)
    rows = P(ALL, None)
    expert_rows = P("expert", DP, None)
    whole = P()
    return jax.shard_map(
        on_device,
        mesh=split,
        in_specs=(rows, rows, P(DP, None), rows)
        + (rows,) * 15
        + (expert_rows,) * 6
        + (whole,) * 12,
        out_specs=(rows, rows) + (rows,) * 20 + (expert_rows,) * 8 + (whole,) * 16,
        check_vma=False,
    )
```

time: 827 us -> 721 us (0.87)
  Pallas kernels: 0 us -> 225 us
  matrix products: 145 us -> 18 us
  local copies, waits for them, and re-layouts: 132 us -> 56.7 us
  waiting for transfers between devices: 293 us -> 222 us
  blocking collectives: 88.9 us -> 24.6 us
  starting transfers between devices: 58.3 us -> 74.5 us
  other arithmetic: 85.7 us -> 73.6 us
    pallas_call x0 -> x9, Pallas kernels: none -> 225 us  [the longest x3 126 us: remote_call(): pl.pallas_call(kernel, out_shape=out_shapes, in_specs=[spec] * len(operan...]
    reduce_scatter x6 -> x2, waiting for transfers between devices: 119 us -> 0.01 us  [the longest x1 0.01 us: on_device(): dense_mine = lax.psum_scatter(dense, DP, scatter_dimension=0, tiled=True)[0]]
    dot_general x22 -> x0, matrix products: 104 us -> none  [the longest x6 20.3 us: dot(): return jnp.dot(left, right, preferred_element_type=f32)]
    all_gather x2 -> x0, blocking collectives: 64.1 us -> none  [the longest x1 42.7 us: on_device(): lax.all_gather(small, ('expert', 'dp'), axis=0, tiled=True)]
    all_to_all x14 -> x12, waiting for transfers between devices: 122 us -> 168 us  [swap(): return lax.all_to_all(pieces, axis, split_axis=0, concat_axis=0, tiled=True)]
    all_gather x4, waiting for transfers between devices: 51.4 us -> 13.8 us  [the longest x2 8.78 us: gathered(): return lax.all_gather(both, MATES, axis=0, tiled=False)]
    ppermute x0 -> x6, waiting for transfers between devices: none -> 36.7 us  [to_partner(): return lax.ppermute(value, 'zhi', [(0, 1), (1, 0)])]
    concatenate x7 -> x0, local copies, waits for them, and re-layouts: 36.4 us -> none  [the longest x1 28.7 us: on_device(): jnp.concatenate([grad_win[:, :body + heads], grad_router, jnp.zeros((D, L...]
  transfers between devices with their start and end apart: 25 -> 25, of which waited for: 15 -> 16; matrix products, arithmetic and copies ran while one was open for 37% -> 16% of each run, Pallas kernels for 0% -> 32%
where the time goes in v2:
time: 721 us; the launch traced here: 710 us
  Pallas kernels  225 us (31%)
  waiting for transfers between devices  222 us (31%)
  starting transfers between devices  74.5 us (10%)
  other arithmetic  73.6 us (10%)
  local copies, waits for them, and re-layouts  56.7 us (8%)
  blocking collectives  24.6 us (3%)
  matrix products  18 us (2%)
  between operations  15.4 us (2%)
    all_to_all x12, waiting for transfers between devices, swap(): return lax.all_to_all(pieces, axis, split_axis=0, concat_axis=0, tiled=True)  168 us
    pallas_call x3, Pallas kernels, remote_call(): pl.pallas_call(kernel, out_shape=out_shapes, in_specs=[spec] * len(operan...  126 us
    pallas_call x3, Pallas kernels, vmem_call(): pl.pallas_call(kernel, out_shape=out_shapes, in_specs=[spec] * len(operan...  52.1 us
    all_to_all x12, starting transfers between devices, swap(): return lax.all_to_all(pieces, axis, split_axis=0, concat_axis=0, tiled=True)  51 us
    pallas_call x3, Pallas kernels, grid_call(): pl.pallas_call(kernel, grid=(steps,), out_shape=out_shapes, in_specs=in_s...  46.7 us
    ppermute x6, waiting for transfers between devices, to_partner(): return lax.ppermute(value, 'zhi', [(0, 1), (1, 0)])  36.7 us
    all_to_all x2, blocking collectives, swap(): return lax.all_to_all(pieces, axis, split_axis=0, concat_axis=0, tiled=True)  24.6 us
    add x7, other arithmetic, adam_step(): return (gradient, weight + moved, moment_one, moment_two, moved)  18 us
  transfers between devices with their start and end apart: 25, of which 16 were waited for; matrix products, arithmetic and copies ran while one was open for 16% of the time, Pallas kernels for 32%

profile of v2, /device:TPU:0, one launch (start us, length us, event | category | flops | bytes accessed | tf_op | source)
XLA Modules:
  0.0 709.7 jit_solution(4127967420929431220)
XLA Ops:
  11.2 16.0 %all_to_all.75 = bf16[4,48,1920]{2,1,0:T(8,128)(2,1)} all-to-all(bf16[4,48,1920]{2,1,0:T(8,128)(2,1)S(1)} %bitcast.142), channel_id=1, replica_groups=mesh['zhi'=2,'zlo'=2,'core'=2,'expert'=4] {'expert'}, dimensions={0} | all-to-all | bytes 1474560 | tf_op jit(solution)/shard_map/all_to_all | solution.py:52
  27.3 2.7 collective-permute-start
  29.9 2.0 collective-permute-done
  32.6 3.3 all-to-all-start.2
  36.9 3.6 all-to-all-done.2
  40.5 1.9 broadcast_in_dim.20
  42.5 3.8 all-to-all-start.3
  46.5 5.0 all-gather.15.cloned.1.call-done
  51.5 3.2 slice.261
  54.8 25.1 %all-to-all-done.3 = bf16[4,2,128,1536]{3,2,1,0:T(8,128)(2,1)S(1)} async-done(((bf16[4,2,128,1536]{3,2,1,0:T(8,128)(2,1)}), bf16[4,2,128,1536]{3,2,1,0:T(8,128)(2,1)S(1)}, u32[]{:S(2)}, u32[]{:S(2)}) %all-to-all-start.3) | async-done | bytes 3145760 | tf_op jit(solution)/shard_map/all_to_all | solution.py:52
  79.8 4.5 all-to-all-start.1
  84.4 2.4 convert_element_type.137
  86.8 3.3 convert_element_type.136
  93.4 2.0 fusion.58
  95.4 16.2 %all-to-all-done.1 = bf16[4,192,1536]{2,1,0:T(8,128)(2,1)} async-done(((bf16[4,192,1536]{2,1,0:T(8,128)(2,1)}), bf16[4,192,1536]{2,1,0:T(8,128)(2,1)}, u32[]{:S(2)}, u32[]{:S(2)}) %all-to-all-start.1) | async-done | bytes 2359328 | tf_op jit(solution)/shard_map/all_to_all | solution.py:52
  111.6 3.3 copy.324
  116.1 2.5 collective-permute-start.1
  119.9 2.5 collective-permute-start.3
  127.5 20.5 %shard_map.708 = (bf16[512,1792]{1,0:T(8,128)(2,1)}, f32[512,128]{1,0:T(8,128)}, bf16[512,768]{1,0:T(8,128)(2,1)}, bf16[512,1664]{1,0:T(8,128)(2,1)}) custom-call(bf16[512,1536]{1,0:T(8,128)(2,1)} %bitcast.123, bf16[1536,1920]{1,0:T(8,128)(2,1)} %all-gather.7.cloned.1.call-done.win_ref, f32[8,1536]{1,0:T(8,128)} %pad.34.gain_ref, ...), custom_call_target="tpu_custom_call" | custom-call | tf_op jit(solution)/shard_map/pallas_call | solution.py:692
  149.5 19.8 %shard_map.709 = (f32[128,1536]{1,0:T(8,128)S(1)}, f32[128,1536]{1,0:T(8,128)S(1)}, bf16[128,1664]{1,0:T(8,128)(2,1)S(1)}) custom-call(bf16[512,1664]{1,0:T(8,128)(2,1)S(1)} %copy-done.4, bf16[128,1536]{1,0:T(8,128)(2,1)S(1)} %copy-done, f32[8,1536]{1,0:T(8,128)S(1)} %copy-done.5), custom_call_target="tpu_custom_call" | custom-call | tf_op jit(solution)/shard_map/pallas_call | solution.py:678
  170.1 8.9 %collective-permute-done.2 = bf16[2,64,1536]{2,1,0:T(8,128)(2,1)S(1)} collective-permute-done((bf16[2,64,1536]{2,1,0:T(8,128)(2,1)}, bf16[2,64,1536]{2,1,0:T(8,128)(2,1)S(1)}, u32[]{:S(2)}, u32[]{:S(2)}) %collective-permute-start.2) | collective-permute-done | bytes 393248 | tf_op jit(solution)/shard_map/ppermute | solution.py:62
  179.0 7.3 %collective-permute-done.3 = bf16[128,1536]{1,0:T(8,128)(2,1)} collective-permute-done((bf16[128,1536]{1,0:T(8,128)(2,1)}, bf16[128,1536]{1,0:T(8,128)(2,1)}, u32[]{:S(2)}, u32[]{:S(2)}) %collective-permute-start.3) | collective-permute-done | bytes 393248 | tf_op jit(solution)/shard_map/ppermute | solution.py:62
  187.4 2.8 maximum_select_fusion.1
  192.8 8.6 %all_to_all.76 = bf16[4,48,512]{2,1,0:T(8,128)(2,1)} all-to-all(bf16[4,48,512]{2,1,0:T(8,128)(2,1)S(1)} %reshape.443), channel_id=1, replica_groups=mesh['zhi'=2,'zlo'=2,'core'=2,'expert'=4] {'expert'}, dimensions={0} | all-to-all | bytes 393216 | tf_op jit(solution)/shard_map/all_to_all | solution.py:52
  201.4 2.3 broadcast_in_dim.22
  203.7 4.3 all-to-all-start.4
  208.0 12.5 %reduce-scatter.3.cloned.1.call-start = ((), (), s32[]{:S(2)}) async-start(), calls=%async_computation.20 | async-start | bytes 11796480 | tf_op jit(solution)/shard_map/reduce_scatter | solution.py:999
  222.5 40.4 %shard_map.710 = (bf16[4,128,1664]{2,1,0:T(8,128)(2,1)S(1)}, bf16[4,128,1664]{2,1,0:T(8,128)(2,1)S(1)}) custom-call(bf16[128,1664]{1,0:T(8,128)(2,1)S(1)} %get-tuple-element.106.two_ref), custom_call_target="tpu_custom_call" | custom-call | tf_op jit(solution)/shard_map/pallas_call | solution.py:678
  262.9 2.2 pad_maximum_fusion.two_ref
  265.2 3.8 pad_maximum_fusion.1.cot_ref
  269.0 12.9 %shard_map.711 = (bf16[2,512,1536]{2,1,0:T(8,128)(2,1)}, bf16[2,512,1536]{2,1,0:T(8,128)(2,1)}, bf16[2,512,1536]{2,1,0:T(8,128)(2,1)}, f32[1024,128]{1,0:T(8,128)}, bf16[8,128,128]{2,1,0:T(8,128)(2,1)}) custom-call(bf16[1024,1664]{1,0:T(8,128)(2,1)} %pad_maximum_fusion.two_ref, bf16[1024,1536]{1,0:T(8,128)(2,1)} %pad_maximum_fusion.1.cot_ref, ...), custom_call_target="tpu_custom_call" | custom-call | tf_op jit(solution)/shard_map/pallas_call | solution.py:703
  281.9 8.8 %all-gather.9.cloned.1.call-done.gu_ref = bf16[4,2,2,192,1024]{4,3,2,1,0:T(8,128)(2,1)} async-done(((bf16[1,2,2,192,1024]{4,3,2,1,0:T(8,128)(2,1)}), bf16[4,2,2,192,1024]{4,3,2,1,0:T(8,128)(2,1)}) %all-gather.9.cloned.1.call-update) | async-done | bytes 6291472 | tf_op jit(solution)/shard_map/all_gather | solution.py:808
  290.7 22.9 %shard_map.712 = (bf16[2,512,1536]{2,1,0:T(8,128)(2,1)}, bf16[2,512,1536]{2,1,0:T(8,128)(2,1)}, f32[2,512,128]{2,1,0:T(8,128)}, bf16[4,2,2,576,512]{4,3,2,1,0:T(8,128)(2,1)}) custom-call(bf16[2,512,1536]{2,1,0:T(8,128)(2,1)} %get-tuple-element.113.in_ref, bf16[2,512,1536]{2,1,0:T(8,128)(2,1)} %get-tuple-element.114.top_ref, ...), custom_call_target="tpu_custom_call" | custom-call | tf_op jit(solution)/shard_map/pallas_call | solution.py:703
  313.6 2.1 slice.265
  315.7 3.4 all-gather.13.cloned.1.call-done.sgu_ref
  319.1 9.7 %shard_map.713 = (bf16[512,1536]{1,0:T(8,128)(2,1)}, bf16[512,1536]{1,0:T(8,128)(2,1)}, bf16[1536,512]{1,0:T(8,128)(2,1)}, bf16[256,1536]{1,0:T(8,128)(2,1)}) custom-call(bf16[512,1664]{1,0:T(8,128)(2,1)} %bitcast.115, bf16[512,1536]{1,0:T(8,128)(2,1)} %bitcast.128, bf16[1536,512]{1,0:T(8,128)(2,1)} %all-gather.13.cloned.1.call-done.sgu_ref, ...), custom_call_target="tpu_custom_call" | custom-call | tf_op jit(solution)/shard_map/pallas_call | solution.py:692
  331.0 11.0 %shard_map.714 = (bf16[1024,1536]{1,0:T(8,128)(2,1)}, bf16[1024,1664]{1,0:T(8,128)(2,1)}) custom-call(bf16[8,128,128]{2,1,0:T(8,128)(2,1)} %get-tuple-element.111.pick_ref, f32[1024,128]{1,0:T(8,128)} %get-tuple-element.112.weights_ref, s32[1]{0:T(128)} %bitcast.26.ids_ref, bf16[2,512,1536]{2,1,0:T(8,128)(2,1)} %get-tuple-element.118.out_ref, ...), custom_call_target="tpu_custom_call" | custom-call | tf_op jit(solution)/shard_map/pallas_call | solution.py:703
  342.0 65.5 %shard_map.715 = (bf16[4,128,1664]{2,1,0:T(8,128)(2,1)S(1)}, f32[128,1536]{1,0:T(8,128)S(1)}, bf16[128,128]{1,0:T(8,128)(2,1)S(1)}, f32[8,1536]{1,0:T(8,128)S(1)}) custom-call(bf16[1024,1664]{1,0:T(8,128)(2,1)} %get-tuple-element.124.back_ref, f32[128,1536]{1,0:T(8,128)S(1)} %get-tuple-element.101.hidden_ref, f32[128,1536]{1,0:T(8,128)S(1)} %copy-done.9, ...), custom_call_target="tpu_custom_call" | custom-call | tf_op jit(solution)/shard_map/pallas_call | solution.py:678
  410.8 4.8 all-to-all-start.9
  418.8 21.9 %shard_map.716 = (bf16[512,1920]{1,0:T(8,128)(2,1)}, f32[8,1024]{1,0:T(8,128)}, f32[8,768]{1,0:T(8,128)}, f32[8,128]{1,0:T(8,128)}) custom-call(bf16[512,1664]{1,0:T(8,128)(2,1)} %bitcast.119, bf16[512,128]{1,0:T(8,128)(2,1)} %slice.266.scale_ref, bf16[768,1536]{1,0:T(8,128)(2,1)} %bitcast.122, f32[8,1024]{1,0:T(8,128)} %select_maximum_fusion.conv_ref, ...), custom_call_target="tpu_custom_call" | custom-call | tf_op jit(solution)/shard_map/pallas_call | solution.py:692
  441.9 7.2 %add_convert_fusion = bf16[1536,1920]{1,0:T(8,128)(2,1)} fusion(f32[1536,16]{1,0:T(8,128)} %fusion.34, bf16[512,1920]{1,0:T(8,128)(2,1)} %get-tuple-element.133, bf16[512,1536]{1,0:T(8,128)(2,1)S(1)} %bitcast.125, f32[1536]{0:T(1024)S(1)} %slice_reduce_fusion.6, f32[512]{0:T(512)S(1)} %add_rsqrt_fusion), kind=kOutput, calls=%fused_computation | convolution fusion | flops 3028942848 | bytes 9543680 | tf_op jit(solution)/shard_map/dot_general | solution.py:48
  449.1 13.5 %maximum_maximum_fusion = bf16[8,192,3456]{2,1,0:T(8,128)(2,1)} fusion(bf16[8,64,512]{2,1,0:T(8,128)(2,1)} %get-tuple-element.530, bf16[8,64,512]{2,1,0:T(8,128)(2,1)} %get-tuple-element.529, bf16[8,64,512]{2,1,0:T(8,128)(2,1)} %get-tuple-element.528, bf16[8,32,1536]{2,1,0:T(8,128)(2,1)} %bitcast.158, bf16[8,96,1536]{2,1,0:T(8,128)(2,1)} %bitcast.45, ...), kind=kLoop, calls=%fused_computation.1 | loop fusion | flops 63700992 | bytes 21233664 | tf_op jit(solution)/shard_map/concatenate | solution.py:1045
  462.5 3.7 fusion.57
  466.3 4.7 all-to-all-start.7
  472.8 18.2 %all-to-all-done.7 = bf16[4,128,1536]{2,1,0:T(8,128)(2,1)} async-done(((bf16[4,128,1536]{2,1,0:T(8,128)(2,1)}), bf16[4,128,1536]{2,1,0:T(8,128)(2,1)}, u32[]{:S(2)}, u32[]{:S(2)}) %all-to-all-start.7) | async-done | bytes 1572896 | tf_op jit(solution)/shard_map/all_to_all | solution.py:52
  491.0 4.4 all-to-all-start.6
  496.1 2.5 reduce_sum.139
  498.6 2.6 collective-permute-start.4
  501.3 8.0 %fusion.3 = (f32[1536]{0:T(1024)S(1)}, bf16[512,1536]{1,0:T(8,128)(2,1)}) fusion(bf16[512,1536]{1,0:T(8,128)(2,1)S(1)} %bitcast.126, f32[512]{0:T(512)S(1)} %add_rsqrt_fusion, bf16[512,1920]{1,0:T(8,128)(2,1)} %get-tuple-element.133, bf16[1536,1920]{1,0:T(8,128)(2,1)} %all-gather.7.cloned.1.call-done.win_ref), kind=kOutput, calls=%fused_computation.10 | convolution fusion | flops 3023829504 | bytes 11018240 | tf_op jit(solution)/shard_map/dot_general | solution.py:44
  510.0 3.8 all-to-all-done.6
  513.7 4.4 all-to-all-start.12
  518.2 18.5 %collective-permute-done.4 = bf16[128,1536]{1,0:T(8,128)(2,1)S(1)} collective-permute-done((bf16[128,1536]{1,0:T(8,128)(2,1)}, bf16[128,1536]{1,0:T(8,128)(2,1)S(1)}, u32[]{:S(2)}, u32[]{:S(2)}) %collective-permute-start.4) | collective-permute-done | bytes 393248 | tf_op jit(solution)/shard_map/ppermute | solution.py:62
  539.1 2.9 dynamic-slice_bitcast_fusion.1
  542.8 5.5 all-to-all-start.13
  550.2 81.2 %all-to-all-done.13 = f32[32,1,1152]{2,1,0:T(1,128)S(1)} async-done(((f32[32,1,1152]{2,1,0:T(1,128)}), f32[32,1,1152]{2,1,0:T(1,128)S(1)}, u32[]{:S(2)}, u32[]{:S(2)}) %all-to-all-start.13) | async-done | bytes 147488 | tf_op jit(solution)/shard_map/all_to_all | solution.py:52
  631.4 3.7 all-to-all-start.8
  641.4 13.9 %all-to-all-done.8 = bf16[4,128,1536]{2,1,0:T(8,128)(2,1)S(1)} async-done(((bf16[4,128,1536]{2,1,0:T(8,128)(2,1)}), bf16[4,128,1536]{2,1,0:T(8,128)(2,1)S(1)}, u32[]{:S(2)}, u32[]{:S(2)}) %all-to-all-start.8) | async-done | bytes 1572896 | tf_op jit(solution)/shard_map/all_to_all | solution.py:52
  660.6 3.6 multiply_add_fusion.2
  666.6 5.1 multiply_add_fusion
  673.5 3.4 all-to-all-start.11
  676.9 2.6 multiply_add_fusion.6
  682.0 4.2 all-to-all-start.10
  690.6 4.9 all-to-all-done.10
  698.8 3.8 multiply_add_fusion.4
  (272 shorter events, 68.3 us)
Async XLA Ops:
  7.2 3.1 copy-start.14
  7.2 44.3 %all-gather.15.cloned.1.call-start = ((), (), s32[]{:S(2)}) async-start(), calls=%async_computation.22 | async-start | bytes 3538944 | tf_op jit(solution)/shard_map/all_gather | solution.py:779
  10.2 104.7 %all-gather.7.cloned.1.call-start = ((), (), s32[]{:S(2)}) async-start(), calls=%async_computation.16 | async-start | bytes 6635520 | tf_op jit(solution)/shard_map/all_gather | solution.py:770
  10.9 16.4 %copy-start.57 = (s32[128,6]{0,1:T(8,128)S(1)}, s32[128,6]{0,1:T(8,128)}, u32[]{:S(2)}) copy-start(s32[128,6]{0,1:T(8,128)} %param.40) | copy-start | bytes 9220
  10.9 24.9 %copy-start = (bf16[128,1536]{1,0:T(8,128)(2,1)S(1)}, bf16[128,1536]{1,0:T(8,128)(2,1)}, u32[]{:S(2)}) copy-start(bf16[128,1536]{1,0:T(8,128)(2,1)} %tokens_ref.1) | copy-start | bytes 1179652
  27.3 4.7 collective-permute-start
  32.6 8.0 %all-to-all-start.2 = ((s32[4,2,128,6]{2,1,3,0:T(2,128)}), s32[4,2,128,6]{2,1,3,0:T(2,128)S(1)}, u32[]{:S(2)}, u32[]{:S(2)}) async-start(s32[4,2,128,6]{2,1,3,0:T(2,128)} %broadcast_in_dim.19), calls=%async_computation.2 | async-start | bytes 49152 | tf_op jit(solution)/shard_map/all_to_all | solution.py:52
  42.5 3.8 copy-start.59
  42.5 37.3 %all-to-all-start.3 = ((bf16[4,2,128,1536]{3,2,1,0:T(8,128)(2,1)}), bf16[4,2,128,1536]{3,2,1,0:T(8,128)(2,1)S(1)}, u32[]{:S(2)}, u32[]{:S(2)}) async-start(bf16[4,2,128,1536]{3,2,1,0:T(8,128)(2,1)} %broadcast_in_dim.20), calls=%async_computation.3 | async-start | bytes 6291456 | tf_op jit(solution)/shard_map/all_to_all | solution.py:52
  79.8 31.8 %all-to-all-start.1 = ((bf16[4,192,1536]{2,1,0:T(8,128)(2,1)}), bf16[4,192,1536]{2,1,0:T(8,128)(2,1)}, u32[]{:S(2)}, u32[]{:S(2)}) async-start(bf16[4,192,1536]{2,1,0:T(8,128)(2,1)} %bitcast.131), calls=%async_computation.1 | async-start | bytes 4718592 | tf_op jit(solution)/shard_map/all_to_all | solution.py:52
  84.3 197.6 %all-gather.11.cloned.1.call-start = ((), (), s32[]{:S(2)}) async-start(), calls=%async_computation.18 | async-start | bytes 3932160 | tf_op jit(solution)/shard_map/all_gather | solution.py:808
  86.8 3.3 copy-start.55
  90.9 32.1 %copy-start.39 = (s32[512]{0:T(512)}, s32[512]{0:T(512)S(1)}, u32[]{:S(2)}) copy-start(s32[512]{0:T(512)S(1)} %broadcast_add_fusion) | copy-start | bytes 6148
  111.6 3.4 copy-start.12
  115.0 3.6 copy-start.56
  115.0 3.6 copy-start.16
  116.0 8.7 %copy-start.46 = (f32[512,4]{0,1:T(4,128)S(1)}, f32[512,4]{0,1:T(4,128)}, u32[]{:S(2)}) copy-start(f32[512,4]{0,1:T(4,128)} %pad_maximum_fusion.8) | copy-start | bytes 24580
  116.0 8.8 %copy-start.41 = (f32[2,1536]{1,0:T(2,128)S(1)}, f32[2,1536]{1,0:T(2,128)}, u32[]{:S(2)}) copy-start(f32[2,1536]{1,0:T(2,128)} %param.62) | copy-start | bytes 36868
  116.0 10.2 %copy-start.38 = (f32[5,3328]{1,0:T(8,128)S(1)}, f32[5,3328]{1,0:T(8,128)}, u32[]{:S(2)}) copy-start(f32[5,3328]{1,0:T(8,128)} %param.65) | copy-start | bytes 199684
  116.0 10.8 %slice-start = ((f32[5,3328]{1,0:T(8,128)}), f32[5,256]{1,0:T(8,128)S(1)}, s32[]{:S(2)}) async-start(f32[5,3328]{1,0:T(8,128)} %param.65), calls=%async_computation.23 | async-start | bytes 16384 | tf_op jit(solution)/shard_map/slice | solution.py:835
  116.1 70.3 %collective-permute-start.1 = (bf16[2,192,1024]{2,1,0:T(8,128)(2,1)}, bf16[2,192,1024]{2,1,0:T(8,128)(2,1)}, u32[]{:S(2)}, u32[]{:S(2)}) collective-permute-start(bf16[2,192,1024]{2,1,0:T(8,128)(2,1)} %get-tuple-element.532), channel_id=1, source_target_pairs={{0,16},{16,0},{1,17},{17,1},{2,18},{18,2},{3,19},{19,3},{4,20},{20... | collective-permute-start | bytes 2359304 | tf_op jit(solution)/shard_map/ppermute | solution.py:62
  119.4 59.6 %collective-permute-start.2 = (bf16[2,64,1536]{2,1,0:T(8,128)(2,1)}, bf16[2,64,1536]{2,1,0:T(8,128)(2,1)S(1)}, u32[]{:S(2)}, u32[]{:S(2)}) collective-permute-start(bf16[2,64,1536]{2,1,0:T(8,128)(2,1)} %get-tuple-element.539), channel_id=1, source_target_pairs={{0,16},{16,0},{1,17},{17,1},{2,18},{18,2},{3,19},{19,3},{4,20},{20... | collective-permute-start | bytes 1179656 | tf_op jit(solution)/shard_map/ppermute | solution.py:62
  119.9 66.4 %collective-permute-start.3 = (bf16[128,1536]{1,0:T(8,128)(2,1)}, bf16[128,1536]{1,0:T(8,128)(2,1)}, u32[]{:S(2)}, u32[]{:S(2)}) collective-permute-start(bf16[128,1536]{1,0:T(8,128)(2,1)} %cot_ref.1), channel_id=1, source_target_pairs={{0,16},{16,0},{1,17},{17,1},{2,18},{18,2},{3,19},{19,3},{4,20},{20... | collective-permute-start | bytes 1179656 | tf_op jit(solution)/shard_map/ppermute | solution.py:62
  127.5 20.5 %copy-start.5 = (f32[8,1536]{1,0:T(8,128)S(1)}, f32[8,1536]{1,0:T(8,128)}, u32[]{:S(2)}) copy-start(f32[8,1536]{1,0:T(8,128)} %pad.34.gain_ref) | copy-start | bytes 147460
  187.3 103.4 %all-gather.9.cloned.1.call-start = ((), (), s32[]{:S(2)}) async-start(), calls=%async_computation.17 | async-start | bytes 7864320 | tf_op jit(solution)/shard_map/all_gather | solution.py:808
  190.1 129.0 %all-gather.13.cloned.1.call-start = ((), (), s32[]{:S(2)}) async-start(), calls=%async_computation.19 | async-start | bytes 1769472 | tf_op jit(solution)/shard_map/all_gather | solution.py:793
  203.7 61.5 %all-to-all-start.4 = ((bf16[4,128,1536]{2,1,0:T(8,128)(2,1)}), bf16[4,128,1536]{2,1,0:T(8,128)(2,1)}, u32[]{:S(2)}, u32[]{:S(2)}) async-start(bf16[4,128,1536]{2,1,0:T(8,128)(2,1)} %broadcast_in_dim.22), calls=%async_computation.4 | async-start | bytes 3145728 | tf_op jit(solution)/shard_map/all_to_all | solution.py:52
  208.0 233.9 %reduce-scatter.3.cloned.1.call-start = ((), (), s32[]{:S(2)}) async-start(), calls=%async_computation.20 | async-start | bytes 11796480 | tf_op jit(solution)/shard_map/reduce_scatter | solution.py:999
  330.9 11.0 %copy-start.2 = (bf16[1536,128]{1,0:T(8,128)(2,1)S(1)}, bf16[1536,128]{1,0:T(8,128)(2,1)}, u32[]{:S(2)}) copy-start(bf16[1536,128]{1,0:T(8,128)(2,1)} %pad.39.router_ref) | copy-start | bytes 1179652
  330.9 11.0 %copy-start.9 = (f32[128,1536]{1,0:T(8,128)S(1)}, f32[128,1536]{1,0:T(8,128)}, u32[]{:S(2)}) copy-start(f32[128,1536]{1,0:T(8,128)} %copy-done.8) | copy-start | bytes 2359300
  341.9 65.6 %copy-start.20 = (bf16[512,1792]{1,0:T(8,128)(2,1)S(1)}, bf16[512,1792]{1,0:T(8,128)(2,1)}, u32[]{:S(2)}) copy-start(bf16[512,1792]{1,0:T(8,128)(2,1)} %get-tuple-element.128.packed_ref) | copy-start | bytes 5505028
  341.9 65.6 %copy-start.29 = (bf16[512,768]{1,0:T(8,128)(2,1)S(1)}, bf16[512,768]{1,0:T(8,128)(2,1)}, u32[]{:S(2)}) copy-start(bf16[512,768]{1,0:T(8,128)(2,1)} %get-tuple-element.130.y_ref) | copy-start | bytes 2359300
  410.8 4.8 copy-start.42
  410.8 4.8 copy-start.10
  410.8 38.3 %all-to-all-start.9 = ((bf16[4,192,1536]{2,1,0:T(8,128)(2,1)}), bf16[4,192,1536]{2,1,0:T(8,128)(2,1)}, u32[]{:S(2)}, u32[]{:S(2)}) async-start(bf16[4,192,1536]{2,1,0:T(8,128)(2,1)} %bitcast.132), calls=%async_computation.10 | async-start | bytes 4718592 | tf_op jit(solution)/shard_map/all_to_all | solution.py:52
  415.5 256.2 %reduce-scatter.5.cloned.1.call-start = ((), (), s32[]{:S(2)}) async-start(), calls=%async_computation.21 | async-start | bytes 11943936 | tf_op jit(solution)/shard_map/reduce_scatter | solution.py:1048
  466.3 5.4 copy-start.47
  466.3 24.7 %all-to-all-start.7 = ((bf16[4,128,1536]{2,1,0:T(8,128)(2,1)}), bf16[4,128,1536]{2,1,0:T(8,128)(2,1)}, u32[]{:S(2)}, u32[]{:S(2)}) async-start(bf16[4,128,1536]{2,1,0:T(8,128)(2,1)} %bitcast.135), calls=%async_computation.8 | async-start | bytes 3145728 | tf_op jit(solution)/shard_map/all_to_all | solution.py:52
  491.0 22.8 %all-to-all-start.6 = ((bf16[4,128,1536]{2,1,0:T(8,128)(2,1)}), bf16[4,128,1536]{2,1,0:T(8,128)(2,1)}, u32[]{:S(2)}, u32[]{:S(2)}) async-start(bf16[4,128,1536]{2,1,0:T(8,128)(2,1)} %bitcast.134), calls=%async_computation.7 | async-start | bytes 3145728 | tf_op jit(solution)/shard_map/all_to_all | solution.py:52
  498.6 38.0 %collective-permute-start.4 = (bf16[128,1536]{1,0:T(8,128)(2,1)}, bf16[128,1536]{1,0:T(8,128)(2,1)S(1)}, u32[]{:S(2)}, u32[]{:S(2)}) collective-permute-start(bf16[128,1536]{1,0:T(8,128)(2,1)} %reduce_sum.139), channel_id=1, source_target_pairs={{0,16},{16,0},{1,17},{17,1},{2,18},{18,2},{3,19},{19,3},{4,20},{20... | collective-permute-start | bytes 1179656 | tf_op jit(solution)/shard_map/ppermute | solution.py:62
  513.7 28.3 %all-to-all-start.12 = ((f32[8,1,1152]{2,1,0:T(1,128)}), f32[8,1,1152]{2,1,0:T(1,128)S(1)}, u32[]{:S(2)}, u32[]{:S(2)}) async-start(f32[8,1,1152]{2,1,0:T(1,128)} %bitcast.63), calls=%async_computation.14 | async-start | bytes 73728 | tf_op jit(solution)/shard_map/all_to_all | solution.py:52
  542.0 113.8 %collective-permute-start.5 = (bf16[2,576,512]{2,1,0:T(8,128)(2,1)}, bf16[2,576,512]{2,1,0:T(8,128)(2,1)}, u32[]{:S(2)}, u32[]{:S(2)}) collective-permute-start(bf16[2,576,512]{2,1,0:T(8,128)(2,1)} %get-tuple-element.527), channel_id=1, source_target_pairs={{0,16},{16,0},{1,17},{17,1},{2,18},{18,2},{3,19},{19,3},{4,20},{20... | collective-permute-start | bytes 3538952 | tf_op jit(solution)/shard_map/ppermute | solution.py:62
  542.8 88.6 %all-to-all-start.13 = ((f32[32,1,1152]{2,1,0:T(1,128)}), f32[32,1,1152]{2,1,0:T(1,128)S(1)}, u32[]{:S(2)}, u32[]{:S(2)}) async-start(f32[32,1,1152]{2,1,0:T(1,128)} %broadcast_in_dim.23), calls=%async_computation.15 | async-start | bytes 294912 | tf_op jit(solution)/shard_map/all_to_all | solution.py:52
  631.4 23.8 %all-to-all-start.8 = ((bf16[4,128,1536]{2,1,0:T(8,128)(2,1)}), bf16[4,128,1536]{2,1,0:T(8,128)(2,1)S(1)}, u32[]{:S(2)}, u32[]{:S(2)}) async-start(bf16[4,128,1536]{2,1,0:T(8,128)(2,1)} %bitcast.149), calls=%async_computation.9 | async-start | bytes 3145728 | tf_op jit(solution)/shard_map/all_to_all | solution.py:52
  635.2 2.9 copy-start.49
  635.2 2.9 copy-start.52
  635.2 5.6 copy-start.50
  635.2 5.5 copy-start.51
  635.8 19.7 %copy-start.58 = (f32[128]{0:T(128)S(1)}, f32[128]{0:T(128)}, u32[]{:S(2)}) copy-start(f32[128]{0:T(128)} %add_rsqrt_fusion.1) | copy-start | bytes 1540
  637.9 17.8 %copy-start.43 = (f32[3072]{0:T(1024)}, f32[3072]{0:T(1024)S(1)}, u32[]{:S(2)}) copy-start(f32[3072]{0:T(1024)S(1)} %reshape.469) | copy-start | bytes 36868
  660.6 3.6 copy-start.11
  660.6 5.1 copy-start.17
  660.6 6.0 copy-start.18
  666.6 10.3 %copy-start.32 = (f32[96,1536]{1,0:T(8,128)S(1)}, f32[96,1536]{1,0:T(8,128)}, u32[]{:S(2)}) copy-start(f32[96,1536]{1,0:T(8,128)} %param.46) | copy-start | bytes 1769476
  671.7 5.1 copy-start.19
  671.7 5.1 copy-start.31
  673.5 8.5 %all-to-all-start.11 = ((bf16[4,48,512]{2,1,0:T(8,128)(2,1)}), bf16[4,48,512]{2,1,0:T(8,128)(2,1)S(1)}, u32[]{:S(2)}, u32[]{:S(2)}) async-start(bf16[4,48,512]{2,1,0:T(8,128)(2,1)} %bitcast.56), calls=%async_computation.13 | async-start | bytes 393216 | tf_op jit(solution)/shard_map/all_to_all | solution.py:52
  676.9 2.6 copy-start.27
  679.5 6.7 copy-start.30
  679.5 6.7 copy-start.36
  679.5 6.7 copy-start.37
  682.0 13.5 %all-to-all-start.10 = ((bf16[4,48,1920]{2,1,0:T(8,128)(2,1)}), bf16[4,48,1920]{2,1,0:T(8,128)(2,1)}, u32[]{:S(2)}, u32[]{:S(2)}) async-start(bf16[4,48,1920]{2,1,0:T(8,128)(2,1)} %bitcast.52), calls=%async_computation.12 | async-start | bytes 1474560 | tf_op jit(solution)/shard_map/all_to_all | solution.py:52
  689.5 7.3 %copy-start.24 = (f32[48,2048]{1,0:T(8,128)}, f32[48,2048]{1,0:T(8,128)S(1)}, u32[]{:S(2)}) copy-start(f32[48,2048]{1,0:T(8,128)S(1)} %copy.352) | copy-start | bytes 1179652
  697.1 5.5 copy-start.48
  (22 other events, 31.1 us)
Sparse Core Ops, SparseCore 0:
  10.4 41.1 all-gather.14
  53.2 60.2 all-gather.6
  187.4 34.3 all-gather.10
  223.8 66.8 all-gather.8
  292.2 26.8 all-gather.12
  321.3 93.6 reduce-scatter.2
  462.7 156.7 reduce-scatter.4

commit v3 on v2

--- a/solution.py
+++ b/solution.py
@@ -20,6 +20,7 @@
 INNER = 3072
 CONV_DIM = 3328
 LANES = 128
+CHUNK = 384
 
 DP = ("zhi", "zlo", "core")
 MATES = ("zlo", "core")
@@ -185,8 +186,24 @@
 
 
 def forward_kernel(x_ref, win_ref, gain_ref, conv_ref, masks_ref, head_ref, cols_ref, doc_col_ref,
-                   doc_row_ref, wout_ref, packed_ref, dt_ref, y_ref, out_ref,
-                   normed_ref, neg_ref, scores_ref, cum_ref, cum_t_ref, act_ref, square_ref):
+                   doc_row_ref, wout_ref, gu_ref, gu_sent_ref, cot_ref, cot_came_ref,
+                   packed_ref, dt_ref, y_ref, out_ref, gu_all_ref, gu_came_ref, cot_two_ref,
+                   normed_ref, neg_ref, scores_ref, cum_ref, cum_t_ref, act_ref, square_ref,
+                   send_sems, recv_sems, mate_send, mate_recv, mate_local, local_sems):
+    greet(group_ids() + near_ids())
+    count, me, _ = peers()
+    sems = (send_sems, recv_sems)
+    over = remote(gu_sent_ref, gu_came_ref, sems, 0, partner_id())
+    weights = MateSpread(gu_ref, gu_all_ref, (mate_send, mate_recv), 0, mate_local)
+    cots = [
+        pltpu.make_async_copy(cot_ref, cot_two_ref.at[0], local_sems.at[0]),
+        pltpu.make_async_copy(cot_came_ref, cot_two_ref.at[1, me], local_sems.at[1]),
+    ]
+    cots += spread_copies(cot_came_ref, cot_two_ref.at[1], sems, 1)
+    over.start()
+    weights.start()
+    for copy in cots:
+        copy.start()
     length = x_ref.shape[0]
     inner = wout_ref.shape[0]
     body = packed_ref.shape[1]
@@ -244,6 +261,11 @@
 
     squares = jnp.sum(square_ref[...], axis=1, keepdims=True)
     out_ref[:, D:] = word_lanes(squares)
+    weights.forward()
+    for copy in cots:
+        copy.wait()
+    over.wait()
+    weights.finish()
 
 
 def word_lanes(column):
@@ -258,13 +280,55 @@
 
 
 def backward_kernel(hid_ref, scale_ref, wout_ref, conv_ref, masks_ref, head_ref, cols_ref,
-                    doc_col_ref, doc_row_ref, packed_ref, dt_ref, y_ref,
-                    proj_ref, conv_grad_ref, cols_grad_ref, head_grad_ref,
+                    doc_col_ref, doc_row_ref, packed_ref, dt_ref, y_ref, sums_ref, came_one_ref, out_ref,
+                    proj_ref, conv_grad_ref, cols_grad_ref, head_grad_ref, total_ref, wout_send_ref,
+                    out_own_ref, out_send_ref,
                     neg_ref, scores_ref, cum_ref, cum_t_ref, grad_scores_ref, row_ref, col_ref,
-                    step_ref, scaled_ref, low_ref):
+                    step_ref, scaled_ref, low_ref, wout_grad_ref, theirs_ref, out_got_ref, out_mine_ref, send_sem, recv_sem, out_send, out_recv,
+                    out_local):
+    greet(group_ids() + [partner_id()])
+    tok = out_own_ref.shape[0]
+    count = lax.axis_size("expert")
+    out_sems = (out_send, out_recv)
+    rows_all = out_ref.shape[0] // 2
+    out_copies = reduce_copies(out_ref, out_got_ref.at[0], out_sems, 0, tok, rows_all)
+    out_copies += reduce_copies(out_ref, out_got_ref.at[1], out_sems, count - 1, tok, 0)
+    mine = pl.ds(pl.multiple_of(lax.axis_index("expert") * tok, tok), tok)
+    yours = pl.ds(pl.multiple_of(rows_all + lax.axis_index("expert") * tok, tok), tok)
+    out_copies += [
+        pltpu.make_async_copy(out_ref.at[yours], out_mine_ref.at[0], out_local.at[0]),
+        pltpu.make_async_copy(out_ref.at[mine], out_mine_ref.at[1], out_local.at[1]),
+    ]
+    for copy in out_copies:
+        copy.start()
+    half = lax.axis_index("zhi")
+    held = sums_ref.shape[0]
+    across = pltpu.make_async_remote_copy(
+        src_ref=sums_ref.at[1, 1 - half], dst_ref=theirs_ref, send_sem=send_sem,
+        recv_sem=recv_sem, device_id=partner_id(), device_id_type=pl.DeviceIdType.MESH,
+    )
+    across.start()
     length = dt_ref.shape[0]
     inner = wout_ref.shape[0]
     body = packed_ref.shape[1]
+    scale_mix = word_sum(scale_ref[...])
+
+    @pl.loop(0, inner // LANES)
+    def _(pair):
+        at, _ = pair_slices(pair, inner)
+        gated = y_ref[:, at].astype(f32) * jax.nn.silu(packed_ref[:, at].astype(f32))
+        act = (gated * scale_mix * cols_ref[0:1, at]).astype(bf16)
+        wout_grad_ref[at, :] = dot_tn(act, hid_ref[:, :D]).astype(bf16)
+
+    owners, rows_out, _ = wout_send_ref.shape
+    real = inner // owners
+    for k in range(owners):
+        wout_send_ref[k, :real, :] = wout_grad_ref[k * real : (k + 1) * real, :]
+        if real < rows_out:
+            wout_send_ref[k, real:, :] = jnp.zeros((rows_out - real, D), bf16)
+    for e in range(held):
+        total_ref[half * held + e] = sums_ref[e, half]
+    total_ref[(1 - half) * held] = came_one_ref[...]
     masks = masks_ref[...]
     pre_step, dt_step, log_decay, exact, b_out, c_out, b_low, c_low = scan_setup(
         dt_ref, packed_ref, conv_ref, masks, head_ref, doc_col_ref[...], doc_row_ref[...], inner,
@@ -277,7 +341,6 @@
     conv_grad_ref[...] = jnp.zeros_like(conv_grad_ref)
     cols_grad_ref[...] = jnp.zeros_like(cols_grad_ref)
     head_grad_ref[...] = jnp.zeros_like(head_grad_ref)
-    scale_mix = word_sum(scale_ref[...])
     row_mean = word_sum(hid_ref[:, D:])
     lanes_all = lax.broadcasted_iota(jnp.int32, (length, LANES), 1)
     lanes = lax.broadcasted_iota(jnp.int32, (LANES, LANES), 1)
@@ -358,17 +421,29 @@
     head_grad_ref[0:1] = jnp.sum(grad_decay * log_decay, axis=0, keepdims=True)
     head_grad_ref[1:2] = jnp.sum(grad_pre, axis=0, keepdims=True)
     proj_ref[:, body:] = grad_pre.astype(bf16)
+    for copy in out_copies:
+        copy.wait()
+    totals = []
+    for side in range(2):
+        total = out_mine_ref[side].astype(f32)
+        for number in range(count - 1):
+            total = total + out_got_ref[side, number].astype(f32)
+        totals.append(total)
+    out_send_ref[...] = totals[0].astype(bf16)
+    out_own_ref[...] = totals[1]
+    across.wait()
+    total_ref[(1 - half) * held + 1] = theirs_ref[...]
 
 
 def route_kernel(two_ref, cot_ref, routes_ref, router_ref, ids_ref,
-                 in_ref, top_ref, grad_ref, weights_ref, pick_ref):
+                 in_ref, top_ref, grad_ref, weights_ref, pick_ref, *, top_count, heads):
     tok = two_ref.shape[0]
     held, capacity, _ = in_ref.shape
     rows = two_ref[:, :D]
-    logits = dot(rows, router_ref[...])
+    logits = pltpu.roll(dot(rows, router_ref[...]), LANES - heads, 1)
     lanes = lax.broadcasted_iota(jnp.int32, (tok, LANES), 1)
     named = lanes < 0
-    for k in range(routes_ref.shape[1]):
+    for k in range(top_count):
         named = named | (lanes == routes_ref[:, k : k + 1])
     top_logit = jnp.max(jnp.where(named, logits, -1e30), axis=1, keepdims=True)
     raised = jnp.where(named, jnp.exp(jnp.where(named, logits - top_logit, 0.0)), 0.0)
@@ -394,67 +469,58 @@
     pick_ref[0] = jnp.concatenate(picks, axis=1)
 
 
-def shared_kernel(two_ref, cot_ref, sgu_ref, sd_ref, out_ref, back_ref, grad_gu_ref, grad_down_ref,
-                  mid_ref, act_ref):
-    width = sd_ref.shape[0]
-    gate = dot(two_ref[:, :D], sgu_ref[:, :width])
-    up = dot(two_ref[:, :D], sgu_ref[:, width:])
-    silu = jax.nn.silu(gate)
-    mid_ref[...] = (silu * up).astype(bf16)
-    grad_mid = dot_nt(cot_ref[...], sd_ref[...])
-    act_ref[:, :width] = (grad_mid * up * silu_slope(gate)).astype(bf16)
-    act_ref[:, width:] = (grad_mid * silu).astype(bf16)
-
-    @pl.loop(0, D // 256)
-    def _(part):
-        at = pl.ds(pl.multiple_of(part * 256, 256), 256)
-        out_ref[:, at] = dot(mid_ref[...], sd_ref[:, at]).astype(bf16)
-        back_ref[:, at] = dot_nt(act_ref[...], sgu_ref[at, :]).astype(bf16)
-        grad_gu_ref[at, :] = dot_tn(two_ref[:, at], act_ref[...]).astype(bf16)
-        grad_down_ref[:, at] = dot_tn(mid_ref[...], cot_ref[:, at]).astype(bf16)
-
-
-def expert_kernel(in_ref, top_ref, grad_ref, gu_ref, down_ref, out_ref, back_ref, q_ref, sums_ref,
-                  mid_ref, act_ref):
-    mates, _, halves, rows_gu, _ = gu_ref.shape
-    rows_down = down_ref.shape[3]
-    shards = [(h, m) for h in range(halves) for m in range(mates)]
-
-    def gu(at, which=shards):
-        return jnp.concatenate([gu_ref[m, 0, h, :, at] for h, m in which], axis=0)
-
-    def down(at):
-        return jnp.concatenate([down_ref[m, 0, h, :, at] for h, m in shards], axis=0)
-
-    for part in range(EXPERT_FF // 256):
-        at = slice(part * 256, (part + 1) * 256)
-        up_at = slice(EXPERT_FF + part * 256, EXPERT_FF + (part + 1) * 256)
-        gate = dot(in_ref[0], gu(at))
-        up = dot(in_ref[0], gu(up_at))
+def expert_kernel(in_ref, top_ref, grad_ref, half_ref, gu_near_ref, gu_far_ref, down_near_ref,
+                  down_far_ref, out_ref, back_ref, q_ref, sums_ref, mid_ref, act_ref):
+    mates, _, rows_gu, _ = gu_near_ref.shape
+    rows_down = down_near_ref.shape[2]
+    shards = [(h, m) for h in range(2) for m in range(mates)]
+    half = half_ref[0]
+    sides = (
+        (half, gu_near_ref, down_near_ref),
+        (1 - half, gu_far_ref, down_far_ref),
+    )
+
+    def joined(ref, at, which=range(mates)):
+        return jnp.concatenate([ref[m, 0, :, at] for m in which], axis=0)
+
+    def block(place, size, offset=0):
+        return pl.ds(pl.multiple_of(offset + place * size, LANES), size)
+
+    wide = D // 2
+    tall = EXPERT_FF // 2
+    for place, _, down in sides:
+        at = block(place, tall)
+        up_at = block(place, tall, EXPERT_FF)
+        gate = sum(
+            dot(in_ref[0, :, block(side, wide)], joined(gu, at)) for side, gu, _ in sides
+        )
+        up = sum(
+            dot(in_ref[0, :, block(side, wide)], joined(gu, up_at)) for side, gu, _ in sides
+        )
         silu = jax.nn.silu(gate)
         mid_ref[:, at] = (silu * up).astype(bf16)
-        each = 256 // rows_down
-        rows = jnp.concatenate(
-            [down_ref[m, 0, h, :, :] for h, m in shards[part * each : (part + 1) * each]], axis=0
-        )
-        grad_mid = dot_nt(grad_ref[0], rows)
+        grad_mid = dot_nt(grad_ref[0], joined(down, slice(None)))
         act_ref[:, at] = (grad_mid * up * silu_slope(gate)).astype(bf16)
         act_ref[:, up_at] = (grad_mid * silu).astype(bf16)
     step = 384
     each = step // rows_gu
+    for side, gu, _ in sides:
+        for part in range(wide // step):
+            rows = joined(gu, slice(None), range(part * each, (part + 1) * each))
+            at = pl.ds(pl.multiple_of(side * wide + part * step, LANES), step)
+            back_ref[0, :, at] = dot_nt(act_ref[...], rows).astype(bf16)
     q = jnp.zeros((in_ref.shape[1], 1), f32)
     for part in range(D // step):
         at = slice(part * step, (part + 1) * step)
-        rows = dot(mid_ref[...], down(at))
+        rows = sum(dot(mid_ref[:, block(side, tall)], joined(down, at)) for side, _, down in sides)
         out_ref[0, :, at] = rows.astype(bf16)
         q = q + jnp.sum(rows * top_ref[0, :, at].astype(f32), axis=1, keepdims=True)
         chosen = shards[part * each : (part + 1) * each]
-        back_ref[0, :, at] = dot_nt(act_ref[...], gu(slice(None), chosen)).astype(bf16)
         for number in range(2):
             half_at = slice(number * EXPERT_FF, (number + 1) * EXPERT_FF)
             total = dot_tn(in_ref[0, :, at], act_ref[:, half_at]).astype(bf16)
             for k, (h, m) in enumerate(chosen):
-                sums_ref[m, h, 0, number * rows_gu : (number + 1) * rows_gu, :] = total[
+                sums_ref[m, 0, h, number * rows_gu : (number + 1) * rows_gu, :] = total[
                     k * rows_gu : (k + 1) * rows_gu
                 ]
     q_ref[0] = jnp.broadcast_to(q, q_ref.shape[1:])
@@ -463,7 +529,7 @@
         total = total.astype(bf16)
         start = 2 * rows_gu + part * rows_down
         for k, (h, m) in enumerate(shards):
-            sums_ref[m, h, 0, start : start + rows_down, :] = total[
+            sums_ref[m, 0, h, start : start + rows_down, :] = total[
                 k * rows_down : (k + 1) * rows_down
             ]
 
@@ -498,19 +564,30 @@
     return count, me, [lax.rem(me + step, count) for step in range(1, count)]
 
 
-def greet(with_partner):
-    count, me, others = peers()
+def group_ids():
+    return [{"expert": other} for other in peers()[2]]
+
+
+def partner_id():
+    return {"zhi": 1 - lax.axis_index("zhi")}
+
+
+def core_id():
+    return {"core": 1 - lax.axis_index("core")}
+
+
+def mate_ids():
+    count, me = lax.axis_size("zlo"), lax.axis_index("zlo")
+    return [lax.rem(me + step, count) for step in range(1, count)]
+
+
+def greet(targets):
     barrier = pltpu.get_barrier_semaphore()
-    for other in others:
+    for target in targets:
         pl.semaphore_signal(
-            barrier, inc=1, device_id={"expert": other}, device_id_type=pl.DeviceIdType.MESH
+            barrier, inc=1, device_id=target, device_id_type=pl.DeviceIdType.MESH
         )
-    if with_partner:
-        pl.semaphore_signal(
-            barrier, inc=1, device_id={"zhi": 1 - lax.axis_index("zhi")},
-            device_id_type=pl.DeviceIdType.MESH,
-        )
-    pl.semaphore_wait(barrier, count - 1 + (1 if with_partner else 0))
+    pl.semaphore_wait(barrier, len(targets))
 
 
 def remote(src, dst, sems, number, target):
@@ -547,14 +624,279 @@
     return total
 
 
-def hidden_kernel(part_ref, tokens_ref, gain_ref, hidden_ref, res_ref, two_ref,
-                  got_ref, send_sems, recv_sems):
+class MateSpread:
+    def __init__(self, rows, full, sems, base, local_sem):
+        planes = mate_ids()
+        core, me = lax.axis_index("core"), lax.axis_index("zlo")
+        slot = me * 2 + core
+        self.over = [
+            remote(rows, full.at[slot], sems, base + number, {"zlo": mate})
+            for number, mate in enumerate(planes)
+        ]
+        count = len(planes)
+        self.beside = [remote(rows, full.at[slot], sems, base + count, core_id())]
+        size = count + 1
+        self.onward = [
+            remote(
+                full.at[lax.rem(me + size - 1 - number, size) * 2 + core],
+                full.at[lax.rem(me + size - 1 - number, size) * 2 + core],
+                sems, base + count + 1 + number, core_id(),
+            )
+            for number in range(count)
+        ]
+        self.own = pltpu.make_async_copy(rows, full.at[slot], local_sem)
+
+    def start(self):
+        for copy in self.over + self.beside + [self.own]:
+            copy.start()
+
+    def forward(self):
+        for copy, onward in zip(self.over, self.onward):
+            copy.wait()
+            onward.start()
+
+    def finish(self):
+        for copy in self.beside + self.onward + [self.own]:
+            copy.wait()
+
+
+def mate_sems(planes):
+    return 2 * planes - 1
+
+
+def near_ids():
+    return [partner_id(), core_id()] + [{"zlo": mate} for mate in mate_ids()]
+
+
+def plane_place():
+    planes = lax.axis_size("zlo")
+    return lax.axis_index("zhi") * planes + lax.axis_index("zlo"), 2 * planes
+
+
+def plane_id(plane):
+    planes = lax.axis_size("zlo")
+    return {"zhi": plane // planes, "zlo": lax.rem(plane, planes)}
+
+
+def line_sems(count):
+    return [
+        pltpu.SemaphoreType.DMA((count - 1,)), pltpu.SemaphoreType.DMA((count - 1,)),
+        pltpu.SemaphoreType.DMA((count - 1,)), pltpu.SemaphoreType.DMA((count - 1,)),
+        pltpu.SemaphoreType.DMA((2 * count - 1,)), pltpu.SemaphoreType.DMA((2 * count - 1,)),
+    ]
+
+
+class LineGather:
+    def __init__(self, full, sems):
+        self.full = full
+        self.up, self.down, self.side = sems[0:2], sems[2:4], sems[4:6]
+        self.core = lax.axis_index("core")
+        self.at, self.count = plane_place()
+
+    def block(self, plane):
+        return self.full.at[plane * 2 + self.core]
+
+    def move(self, plane, sems, number, target):
+        return remote(self.block(plane), self.block(plane), sems, number, target)
+
+    def upward(self, step):
+        return self.move(self.at - step, self.up, step, plane_id(self.at + 1))
+
+    def downward(self, step):
+        return self.move(self.at + step, self.down, step, plane_id(self.at - 1))
+
+    def sends_up(self, step):
+        return (self.at < self.count - 1) & (self.at >= step)
+
+    def sends_down(self, step):
+        return (self.at > 0) & (self.at + step < self.count)
+
+    def gets_up(self, step):
+        return self.at >= step + 1
+
+    def gets_down(self, step):
+        return self.at + step + 1 < self.count
+
+    def beside(self, plane, number):
+        return self.move(plane, self.side, number, core_id())
+
+    def start(self):
+        pl.when(self.sends_up(0))(lambda: self.upward(0).start())
+        pl.when(self.sends_down(0))(lambda: self.downward(0).start())
+        self.beside(self.at, 0).start()
+
+    def step(self, step):
+        def from_below():
+            self.move(self.at - step - 1, self.up, step, plane_id(self.at)).wait_recv()
+            self.beside(self.at - step - 1, 1 + step).start()
+
+        def from_above():
+            self.move(self.at + step + 1, self.down, step, plane_id(self.at)).wait_recv()
+            self.beside(self.at + step + 1, self.count + step).start()
+
+        pl.when(self.gets_up(step))(from_below)
+        if step + 1 < self.count - 1:
+            pl.when(self.sends_up(step + 1))(lambda: self.upward(step + 1).start())
+        pl.when(self.gets_down(step))(from_above)
+        if step + 1 < self.count - 1:
+            pl.when(self.sends_down(step + 1))(lambda: self.downward(step + 1).start())
+
+    def finish(self):
+        self.beside(self.at, 0).wait()
+        for step in range(self.count - 1):
+            pl.when(self.sends_up(step))(lambda step=step: self.upward(step).wait_send())
+            pl.when(self.sends_down(step))(lambda step=step: self.downward(step).wait_send())
+            pl.when(self.gets_up(step))(
+                lambda step=step: self.beside(self.at - step - 1, 1 + step).wait()
+            )
+            pl.when(self.gets_down(step))(
+                lambda step=step: self.beside(self.at + step + 1, self.count + step).wait()
+            )
+
+
+def start_kernel(lengths_ref, x_ref, cot_ref, routes_ref, win_ref, sgu_ref, wout_ref, sd_ref,
+                 gu_ref, down_ref,
+                 x_all_ref, cot_all_ref, cot_came_ref, routes_two_ref, win_all_ref, sgu_all_ref, wout_own_ref,
+                 sd_own_ref, masks_ref, doc_col_ref, doc_row_ref, gu_kept_ref, gu_sent_ref,
+                 down_kept_ref, down_sent_ref,
+                 wout_all_ref, sd_all_ref, routes_came_ref, send_sems, recv_sems,
+                 out_send, out_recv, near_send, near_recv, local_sems, *line):
+    count, me, others = peers()
+    at, planes = plane_place()
+    half = lax.axis_index("zhi")
+    sems = (send_sems, recv_sems)
+    near = (near_send, near_recv)
+    barrier = pltpu.get_barrier_semaphore()
+
+    def tell(target):
+        pl.semaphore_signal(
+            barrier, inc=1, device_id=target, device_id_type=pl.DeviceIdType.MESH
+        )
+
+    for target in group_ids() + [partner_id(), core_id()]:
+        tell(target)
+    pl.when(at > 0)(lambda: tell(plane_id(at - 1)))
+    pl.when(at < planes - 1)(lambda: tell(plane_id(at + 1)))
+    ends = (at > 0).astype(jnp.int32) + (at < planes - 1).astype(jnp.int32)
+    pl.semaphore_wait(barrier, count + 1 + ends)
+
+    slot = at * 2 + lax.axis_index("core")
+    peer_count = len(others)
+
+    def pieces(src, dst, base, local):
+        copies = [
+            remote(src.at[other], dst.at[slot, me], sems, base + number, {"expert": other})
+            for number, other in enumerate(others)
+        ]
+        return copies + [pltpu.make_async_copy(src.at[me], dst.at[slot, me], local)]
+
+    def shared_rows(src, dst, base, local):
+        return spread_copies(src, dst, sems, base) + [
+            pltpu.make_async_copy(src, dst.at[me], local)
+        ]
+
+    def started(copies):
+        for copy in copies:
+            copy.start()
+        return copies
+
+    def ended(copies):
+        for copy in copies:
+            copy.wait()
+
+    lines = [
+        LineGather(full, line[6 * k : 6 * k + 6])
+        for k, full in enumerate((win_all_ref, wout_all_ref, sgu_all_ref, sd_all_ref))
+    ]
+    win_copies = started(pieces(win_ref, win_all_ref, 0, local_sems.at[0]))
+    keep = started([
+        pltpu.make_async_copy(wout_ref, wout_all_ref.at[slot], local_sems.at[1]),
+        pltpu.make_async_copy(sd_ref, sd_all_ref.at[slot], local_sems.at[2]),
+    ])
+    ended(keep)
+    lines[1].start()
+    lines[3].start()
+    sgu_copies = started(pieces(sgu_ref, sgu_all_ref, peer_count, local_sems.at[3]))
+    routes_over = started([remote(routes_ref, routes_came_ref, near, 1, partner_id())])
+    ended(win_copies)
+    lines[0].start()
+    wide = started(
+        shared_rows(x_ref, x_all_ref, 2 * peer_count, local_sems.at[4])
+        + shared_rows(routes_ref, routes_two_ref.at[0], 3 * peer_count, local_sems.at[5])
+    )
+    for step in range(planes - 1):
+        lines[1].step(step)
+        lines[3].step(step)
+    lines[1].finish()
+    lines[3].finish()
+    rows = wout_own_ref.shape[0]
+    out_copies = []
+    for j in range(rows):
+        for k, (full, own) in enumerate(
+            ((wout_all_ref, wout_own_ref), (sd_all_ref, sd_own_ref))
+        ):
+            base = (2 * j + k) * peer_count
+            for number, other in enumerate(others):
+                out_copies.append(remote(
+                    full.at[other * rows + j], own.at[j, me], (out_send, out_recv),
+                    base + number, {"expert": other},
+                ))
+            out_copies.append(pltpu.make_async_copy(
+                full.at[me * rows + j], own.at[j, me], local_sems.at[9 + 2 * j + k]
+            ))
+    started(out_copies)
+    lines[0].step(0)
+    ended(sgu_copies)
+    lines[2].start()
+    cot_over = started([remote(cot_ref, cot_came_ref, near, 0, partner_id())])
+    wide += started(shared_rows(cot_ref, cot_all_ref, 4 * peer_count, local_sems.at[6]))
+
+    length = masks_ref.shape[0]
+    place = lax.broadcasted_iota(jnp.int32, (length, LANES), 0)
+    lane = lax.broadcasted_iota(jnp.int32, (length, LANES), 1)
+    across = lax.broadcasted_iota(jnp.int32, (1, length), 1)
+    doc, earlier, doc_row = place * 0 - 1, place * 0 - 1, across * 0 - 1
+    start = 0
+    for k in range(lengths_ref.shape[1]):
+        doc = doc + (place >= start).astype(jnp.int32)
+        earlier = earlier + (place - lane >= start).astype(jnp.int32)
+        doc_row = doc_row + (across >= start).astype(jnp.int32)
+        start = start + lengths_ref[0, k]
+    masks_ref[...] = (doc == earlier).astype(f32)
+    doc_col_ref[...] = doc[:, :1]
+    doc_row_ref[...] = doc_row
+    held = gu_kept_ref.shape[0]
+    for e in range(held):
+        gu_kept_ref[e] = gu_ref[half * held + e].astype(bf16)
+        gu_sent_ref[e] = gu_ref[(1 - half) * held + e].astype(bf16)
+        down_kept_ref[e] = down_ref[half * held + e].astype(bf16)
+        down_sent_ref[e] = down_ref[(1 - half) * held + e].astype(bf16)
+
+    ended(routes_over)
+    wide += started(
+        shared_rows(routes_came_ref, routes_two_ref.at[1], 5 * peer_count, local_sems.at[7])
+    )
+    for step in range(1, planes - 1):
+        lines[0].step(step)
+        lines[2].step(step - 1)
+    lines[2].step(planes - 2)
+    lines[0].finish()
+    lines[2].finish()
+    ended(wide + out_copies + cot_over)
+
+
+def hidden_kernel(part_ref, tokens_ref, gain_ref, down_ref, down_sent_ref,
+                  hidden_ref, res_ref, two_ref, down_all_ref, down_came_ref,
+                  got_ref, send_sems, recv_sems, mate_send, mate_recv, mate_local):
     tok = tokens_ref.shape[0]
     sems = (send_sems, recv_sems)
-    greet(False)
+    greet(group_ids() + near_ids())
     copies = reduce_copies(part_ref, got_ref, sems, 0, tok, 0)
-    for copy in copies:
+    over = remote(down_sent_ref, down_came_ref, sems, len(copies), partner_id())
+    weights = MateSpread(down_ref, down_all_ref, (mate_send, mate_recv), 0, mate_local)
+    for copy in copies + [over]:
         copy.start()
+    weights.start()
     for copy in copies:
         copy.wait()
     squares = word_sum(reduced(part_ref, got_ref, tok, 0, slice(D, D + LANES)))
@@ -566,29 +908,81 @@
     scale = lax.rsqrt(jnp.mean(hidden * hidden, axis=1, keepdims=True) + norm_eps)
     two_ref[:, :D] = (hidden * scale * gain_ref[1:2]).astype(bf16)
     two_ref[:, D:] = word_lanes(scale_mix)
-
-
-def share_kernel(two_ref, own_ref, other_ref, came_ref, send_sems, recv_sems, local_sems):
+    weights.forward()
+    over.wait()
+    weights.finish()
+
+
+def share_kernel(two_ref, gu_ref, down_ref, cot_ref, sgu_ref, sd_ref,
+                 two_all_ref, gu_all_ref, down_all_ref, out_ref, back_ref, grad_gu_ref,
+                 grad_down_ref, came_ref, rows_ref, mid_ref, act_ref,
+                 send_sems, recv_sems, mate_send, mate_recv, local_sems):
     count, me, _ = peers()
     sems = (send_sems, recv_sems)
-    greet(True)
-    over = remote(two_ref, came_ref, sems, 0, {"zhi": 1 - lax.axis_index("zhi")})
+    mate = (mate_send, mate_recv)
+    own_ref, other_ref = two_all_ref.at[0], two_all_ref.at[1]
+    greet(group_ids() + near_ids())
+    over = remote(two_ref, came_ref, sems, 0, partner_id())
     over.start()
     first = spread_copies(two_ref, own_ref, sems, 1)
     for copy in first:
         copy.start()
     mine = pltpu.make_async_copy(two_ref, own_ref.at[me], local_sems.at[0])
     mine.start()
+    step = (mate_send.shape[0]) // 2
+    gu_weights = MateSpread(gu_ref, gu_all_ref, mate, 0, local_sems.at[1])
+    down_weights = MateSpread(down_ref, down_all_ref, mate, step, local_sems.at[2])
+    gu_weights.start()
+    down_weights.start()
     over.wait()
     second = spread_copies(came_ref, other_ref, sems, count)
     for copy in second:
         copy.start()
-    theirs = pltpu.make_async_copy(came_ref, other_ref.at[me], local_sems.at[1])
+    theirs = pltpu.make_async_copy(came_ref, other_ref.at[me], local_sems.at[3])
     theirs.start()
-    for copy in first + second:
+    for copy in first:
         copy.wait()
     mine.wait()
+
+    length, width = rows_ref.shape[0], sd_ref.shape[0]
+    tok = two_ref.shape[0]
+    for g in range(count):
+        rows_ref[g * tok : (g + 1) * tok, :] = two_all_ref[0, g, :, :D]
+    gate = dot(rows_ref[...], sgu_ref[:, :width])
+    up = dot(rows_ref[...], sgu_ref[:, width:])
+    silu = jax.nn.silu(gate)
+    mid_ref[...] = (silu * up).astype(bf16)
+    grad_mid = dot_nt(cot_ref[:length, :], sd_ref[...])
+    act_ref[:, :width] = (grad_mid * up * silu_slope(gate)).astype(bf16)
+    act_ref[:, width:] = (grad_mid * silu).astype(bf16)
+    gu_weights.forward()
+
+    @pl.loop(0, D // 256)
+    def _(part):
+        at = pl.ds(pl.multiple_of(part * 256, 256), 256)
+        out_ref[:, at] = dot(mid_ref[...], sd_ref[:, at]).astype(bf16)
+        back_ref[:, at] = dot_nt(act_ref[...], sgu_ref[at, :]).astype(bf16)
+
+    owners, rows_down, _ = grad_down_ref.shape
+    real = width // owners
+    total = dot_tn(mid_ref[...], cot_ref[:length, :]).astype(bf16)
+    for k in range(owners):
+        grad_down_ref[k, :real, :] = total[k * real : (k + 1) * real]
+        if real < rows_down:
+            grad_down_ref[k, real:, :] = jnp.zeros((rows_down - real, D), bf16)
+    each = D // owners
+    wide = max(each, 384)
+    for part in range(D // wide):
+        total = dot_tn(rows_ref[:, part * wide : (part + 1) * wide], act_ref[...]).astype(bf16)
+        for k in range(wide // each):
+            owner = part * (wide // each) + k
+            grad_gu_ref[owner // 2, owner % 2] = total[k * each : (k + 1) * each]
+    for copy in second:
+        copy.wait()
     theirs.wait()
+    down_weights.forward()
+    gu_weights.finish()
+    down_weights.finish()
 
 
 def q_lanes(sources, held, own_experts, half):
@@ -604,10 +998,20 @@
     return total
 
 
-def back_kernel(back_ref, hidden_ref, res_ref, cot_ref, weights_ref, router_ref, gain_ref,
-                all_ref, grad_hidden_ref, grad_logits_ref, gain_grad_ref,
-                got_other_ref, got_own_ref, send_ref, came_ref, low_ref, send_sems, recv_sems,
-                local_sem, *, own_experts):
+def sum_plane(sums_ref, part_ref, slots_ref, expert):
+    me = lax.axis_index("zlo")
+    for h in range(sums_ref.shape[1]):
+        total = part_ref[me, expert, h].astype(f32)
+        for number in range(slots_ref.shape[0]):
+            total = total + slots_ref[number, expert, h].astype(f32)
+        sums_ref[expert, h] = total.astype(bf16)
+
+
+def back_kernel(back_ref, hidden_ref, res_ref, cot_ref, weights_ref, router_ref, gain_ref, grads_ref,
+                all_ref, grad_hidden_ref, grad_logits_ref, gain_grad_ref, sums_ref, theirs_ref,
+                got_other_ref, got_own_ref, send_ref, came_ref, low_ref, slots_ref, core_ref,
+                send_sems, recv_sems, plane_send, plane_recv, core_send, core_recv, local_sem,
+                *, own_experts, heads):
     tok = cot_ref.shape[0]
     length = back_ref.shape[0] // 2
     held = own_experts // 2
@@ -615,11 +1019,45 @@
     half = lax.axis_index("zhi")
     sems = (send_sems, recv_sems)
     words_at = slice(D, D + LANES)
-    greet(True)
+    mates = mate_ids()
+    greet(group_ids() + near_ids())
+    core = lax.axis_index("core")
+    planes_here = core_ref.shape[0]
+    core_copies = [
+        [
+            remote(
+                grads_ref.at[z, 1 - core, expert], core_ref.at[z, expert], (core_send, core_recv),
+                expert * planes_here + z, core_id(),
+            )
+            for z in range(planes_here)
+        ]
+        for expert in range(held)
+    ]
+    plane_sems = (plane_send, plane_recv)
+    planes = [
+        [
+            remote(
+                core_ref.at[mate, expert], slots_ref.at[number, expert], plane_sems,
+                expert * len(mates) + number, {"zlo": mate},
+            )
+            for number, mate in enumerate(mates)
+        ]
+        for expert in range(held)
+    ]
     first = reduce_copies(back_ref, got_other_ref, sems, 0, tok, length)
     second = reduce_copies(back_ref, got_own_ref, sems, count - 1, tok, 0)
-    for copy in first + second:
+    for copy in first + core_copies[0] + core_copies[1]:
         copy.start()
+    for expert in range(held):
+        for z, copy in enumerate(core_copies[expert]):
+            copy.wait()
+            for h in range(2):
+                core_ref[z, expert, h] = (
+                    core_ref[z, expert, h].astype(f32) + grads_ref[z, core, expert, h].astype(f32)
+                ).astype(bf16)
+        if expert == 0:
+            for copy in planes[0]:
+                copy.start()
 
     def q_of(start, slots):
         mine = back_ref[pl.ds(pl.multiple_of(start + me * tok, tok), tok), words_at]
@@ -641,17 +1079,29 @@
     over = remote(send_ref, came_ref, sems, 2 * (count - 1), {"zhi": 1 - half})
     over.start()
     for copy in second:
+        copy.start()
+    for copy in planes[0]:
+        copy.wait()
+    for copy in planes[1]:
+        copy.start()
+    sum_plane(sums_ref, core_ref, slots_ref, 0)
+    across = remote(
+        sums_ref.at[0, 1 - half], theirs_ref, plane_sems, held * len(mates), partner_id()
+    )
+    for copy in second:
         copy.wait()
     q_own = q_of(0, got_own_ref)
     total = reduced(back_ref, got_own_ref, tok, 0, slice(0, D))
     over.wait()
+    across.start()
     came = came_ref[:, D:].astype(f32)
     came = came + pltpu.roll(came, LANES - shift, 1) + pltpu.roll(came, LANES - 2 * shift, 1)
     q = q_own + jnp.where(lanes < shift, came, 0.0)
     weights = weights_ref[...]
     grad_logits = weights * (q - jnp.sum(weights * q, axis=1, keepdims=True))
     grad_logits_ref[...] = grad_logits.astype(bf16)
-    total = total + came_ref[:, :D].astype(f32) + dot_nt(grad_logits_ref[...], router_ref[...])
+    placed_logits = pltpu.roll(grad_logits, heads, 1).astype(bf16)
+    total = total + came_ref[:, :D].astype(f32) + dot_nt(placed_logits, router_ref[...])
     hidden = hidden_ref[...]
     scale = lax.rsqrt(jnp.mean(hidden * hidden, axis=1, keepdims=True) + norm_eps)
     unit = hidden * scale
@@ -668,21 +1118,339 @@
         copy.start()
     mine = pltpu.make_async_copy(low_ref, all_ref.at[me], local_sem)
     mine.start()
+    for copy in planes[1]:
+        copy.wait()
+    sum_plane(sums_ref, core_ref, slots_ref, 1)
     for copy in third:
         copy.wait()
     mine.wait()
-
-
-def remote_call(kernel, number, out_shapes, scratch, sems, *operands):
+    across.wait()
+
+
+def dense_kernel(x_ref, tokens_ref, win_ref, gain_ref, proj_ref, two_ref, logits_ref, sgu_ref,
+                 wout_ref, down_ref, grad_hidden_ref, out_own_ref, out_send_ref, hidden_ref,
+                 conv_ref, cols_ref,
+                 head_ref, gain_two_ref,
+                 got_ref, own_out_ref, own_down_ref, tokens_grad_ref, output_ref, all_small_ref,
+                 normed_ref, first_ref, second_ref, core_ref, slots_ref, plane_ref, came_ref,
+                 send_ref, one_ref, one_got_ref, out_came_ref, scale_ref, step_ref, step_came_ref, core_send, core_recv, plane_send,
+                 plane_recv, half_send, half_recv, row_send, row_recv, one_send, one_recv, out_send,
+                 out_recv, small_send, small_recv, fold_send, fold_recv, local_sems, fold_sems,
+                 own_sems, *, shared_chunks, heads):
+    length = x_ref.shape[0]
+    tok = tokens_ref.shape[0]
+    chunks_one = first_ref.shape[0]
+    chunks = core_ref.shape[0]
+    own_rows = first_ref.shape[3]
+    rows_in = send_ref.shape[2]
+    core, half, zlo = lax.axis_index("core"), lax.axis_index("zhi"), lax.axis_index("zlo")
+    mates = mate_ids()
+    count, me, others = peers()
+    planes = core_ref.shape[1] // 2
+    greet(group_ids() + near_ids())
+
+    def source(chunk):
+        if chunk < chunks_one:
+            return first_ref.at[chunk]
+        start = (chunk - chunks_one) * CHUNK
+        return second_ref.at[:, :, :, start : start + CHUNK]
+
+    wide_out = D * wout_ref.shape[1] // own_rows
+    wide_down = D * down_ref.shape[1] // own_rows
+    start = wide_out + wide_down
+    beside = pltpu.make_async_copy(
+        sgu_ref, second_ref.at[:, :, :, start : start + sgu_ref.shape[3]], own_sems.at[0]
+    )
+    beside.start()
+    each = wout_ref.shape[0] // count
+    fold_copies = []
+    number = 0
+    local = 0
+    for full, width, offset in ((wout_ref, wide_out, 0), (down_ref, wide_down, wide_out)):
+        rows = full.shape[1]
+        for j in range(each):
+            for fold in range(D // width):
+                columns = slice(fold * width, (fold + 1) * width)
+                place = pl.ds(fold * rows, rows)
+                owner = me * each + j
+                target = second_ref.at[
+                    owner // 2, lax.rem(owner, 2), place, offset : offset + width
+                ]
+                for other in others:
+                    fold_copies.append(remote(
+                        full.at[j * count + other, :, columns], target, (fold_send, fold_recv),
+                        number, {"expert": other},
+                    ))
+                    number += 1
+                fold_copies.append(pltpu.make_async_copy(
+                    full.at[j * count + me, :, columns], target, fold_sems.at[local]
+                ))
+                local += 1
+    for copy in fold_copies:
+        copy.start()
+
+    core_copies, plane_copies, half_copies, row_copies = {}, {}, {}, {}
+
+    def send_core(chunk):
+        copies = [
+            pltpu.make_async_remote_copy(
+                src_ref=source(chunk).at[:, 1 - core],
+                dst_ref=core_ref.at[chunk], send_sem=core_send.at[chunk],
+                recv_sem=core_recv.at[chunk], device_id=core_id(),
+                device_id_type=pl.DeviceIdType.MESH,
+            )
+        ]
+        for copy in copies:
+            copy.start()
+        core_copies[chunk] = copies
+
+    def send_plane(chunk):
+        for copy in core_copies[chunk]:
+            copy.wait()
+        for k in range(2 * planes):
+            core_ref[chunk, k] = (
+                source(chunk)[k, core].astype(f32) + core_ref[chunk, k].astype(f32)
+            ).astype(bf16)
+        copies = [
+            remote(
+                core_ref.at[chunk, pl.ds(h * planes + mate, 1)],
+                slots_ref.at[chunk, number, pl.ds(h, 1)],
+                (plane_send, plane_recv), (chunk * len(mates) + number) * 2 + h, {"zlo": mate},
+            )
+            for number, mate in enumerate(mates)
+            for h in range(2)
+        ]
+        for copy in copies:
+            copy.start()
+        plane_copies[chunk] = copies
+
+    def send_half(chunk):
+        for copy in plane_copies[chunk]:
+            copy.wait()
+        for h in range(2):
+            total = core_ref[chunk, h * planes + zlo].astype(f32)
+            for number in range(len(mates)):
+                total = total + slots_ref[chunk, number, h].astype(f32)
+            plane_ref[chunk, h] = total.astype(bf16)
+        copy = remote(
+            plane_ref.at[chunk, 1 - half], came_ref.at[chunk], (half_send, half_recv), chunk,
+            partner_id(),
+        )
+        copy.start()
+        half_copies[chunk] = copy
+
+    def send_rows(chunk):
+        half_copies[chunk].wait()
+        total = plane_ref[chunk, half].astype(f32) + came_ref[chunk].astype(f32)
+        for block in range(CHUNK // LANES):
+            at = (chunk - chunks_one) * CHUNK + block * LANES
+            columns = total[:, block * LANES : (block + 1) * LANES]
+            if 0 <= at < wide_out:
+                put(own_out_ref, columns, wide_out, at)
+            elif wide_out <= at < wide_out + wide_down:
+                put(own_down_ref, columns, wide_down, at - wide_out)
+        if chunk not in shared_chunks:
+            return
+        spot = shared_chunks.index(chunk)
+        columns = slice(spot * CHUNK, (spot + 1) * CHUNK)
+        low = total.astype(bf16)
+        for place in range(count):
+            send_ref[spot, place] = low[place * rows_in : (place + 1) * rows_in]
+        copies = [
+            remote(
+                send_ref.at[spot, other], got_ref.at[me, :, columns], (row_send, row_recv),
+                chunk * (count - 1) + number, {"expert": other},
+            )
+            for number, other in enumerate(others)
+        ]
+        mine = pltpu.make_async_copy(
+            send_ref.at[spot, me], got_ref.at[me, :, columns], local_sems.at[chunk]
+        )
+        for copy in copies + [mine]:
+            copy.start()
+        row_copies[chunk] = copies + [mine]
+
+    def put(ref, columns, width, at):
+        rows = ref.shape[0]
+        for fold in range(D // width):
+            ref[:, fold * width + at : fold * width + at + LANES] = columns[
+                fold * rows : (fold + 1) * rows
+            ]
+
+    alone = [chunk for chunk in range(chunks_one, chunks)
+             if (chunk - chunks_one) * CHUNK >= wide_out + wide_down]
+    mixed = [chunk for chunk in range(chunks_one, chunks) if chunk not in alone]
+    order = alone + list(range(chunks_one)) + mixed
+    ready = set()
+
+    @pl.loop(0, length // LANES)
+    def _(part):
+        rows = pl.ds(pl.multiple_of(part * LANES, LANES), LANES)
+        block = x_ref[rows, :].astype(f32)
+        scale = lax.rsqrt(jnp.mean(block * block, axis=1, keepdims=True) + norm_eps)
+        normed_ref[rows, :] = (block * scale * gain_ref[0:1]).astype(bf16)
+        scale_ref[rows, :] = scale
+
+    out_over = remote(out_send_ref, out_came_ref, (out_send, out_recv), 0, partner_id())
+
+    def produce(chunk):
+        if chunk in ready:
+            return
+        ready.add(chunk)
+        if chunk in alone:
+            beside.wait()
+        elif chunk in mixed:
+            if not any(one in ready for one in mixed if one != chunk):
+                for copy in fold_copies:
+                    copy.wait()
+                if not alone:
+                    beside.wait()
+            for one in mixed:
+                ready.add(one)
+                send_core(one)
+            return
+        else:
+            at = slice(chunk * CHUNK, (chunk + 1) * CHUNK)
+            total = dot_tn(normed_ref[...], proj_ref[:, at])
+            if chunk == chunks_one - 1:
+                logits = pltpu.roll(logits_ref[...].astype(f32), heads, 1).astype(bf16)
+                router = dot_tn(two_ref[:, :D], logits)
+                total = total + jnp.concatenate(
+                    [jnp.zeros((D, CHUNK - LANES), f32), router], axis=1
+                )
+            low = total.astype(bf16)
+            for k in range(D // own_rows):
+                first_ref[chunk, k // 2, k % 2] = low[k * own_rows : (k + 1) * own_rows]
+        send_core(chunk)
+
+    begin = conv_ref.shape[1]
+    step_ref[0, :, :begin] = conv_ref[...]
+    step_ref[0, :, begin : begin + cols_ref.shape[1]] = cols_ref[...]
+    begin += cols_ref.shape[1]
+    step_ref[0, :, begin : begin + LANES] = head_ref[...]
+    begin += LANES
+    step_ref[0, :, begin : begin + D] = gain_two_ref[...]
+    begin += D
+
+    def input_part(part):
+        at = slice(part * CHUNK, (part + 1) * CHUNK)
+        one = dot_nt(proj_ref[...], win_ref[at, :])
+        gains = jnp.sum(one * (x_ref[:, at].astype(f32) * scale_ref[...]), axis=0, keepdims=True)
+        step_ref[0, :, begin + part * CHUNK : begin + (part + 1) * CHUNK] = jnp.broadcast_to(
+            gains, (8, CHUNK)
+        )
+        one_ref[:, at] = one.astype(bf16)
+
+    one_copies = reduce_copies(one_ref, one_got_ref, (one_send, one_recv), 0, tok, 0)
+
+    small_sems = (small_send, small_recv)
+    rounds = [[core_id()], [{"zlo": mate} for mate in mates], [partner_id()]]
+    bases = [sum(len(targets) for targets in rounds[:level]) for level in range(4)]
+    small_copies = [
+        [
+            remote(
+                step_ref.at[level], step_came_ref.at[bases[level] + k], small_sems,
+                bases[level] + k, target,
+            )
+            for k, target in enumerate(targets)
+        ]
+        for level, targets in enumerate(rounds)
+    ]
+    small_copies.append([
+        remote(
+            step_ref.at[3], all_small_ref.at[me], small_sems, bases[3] + number, {"expert": other}
+        )
+        for number, other in enumerate(others)
+    ])
+    small_copies[3].append(
+        pltpu.make_async_copy(step_ref.at[3], all_small_ref.at[me], own_sems.at[1])
+    )
+
+    def small_start(level):
+        for copy in small_copies[level]:
+            copy.start()
+
+    def small_sum(level):
+        total = step_ref[level]
+        for k, copy in enumerate(small_copies[level]):
+            copy.wait()
+            total = total + step_came_ref[bases[level] + k]
+        step_ref[level + 1] = total
+
+    amount = len(order)
+    parts = D // CHUNK
+    produce(order[0])
+    for tick in range(amount + 4):
+        if tick + 1 < amount:
+            produce(order[tick + 1])
+        if tick < amount:
+            send_plane(order[tick])
+        if tick == 2:
+            out_over.start()
+        if 2 <= tick < amount + 2:
+            send_half(order[tick - 2])
+        if 4 <= tick:
+            send_rows(order[tick - 4])
+        if amount - parts <= tick < amount:
+            input_part(tick - (amount - parts))
+        if tick == amount - 1:
+            for copy in one_copies:
+                copy.start()
+            small_start(0)
+        if amount <= tick < amount + 3:
+            small_sum(tick - amount)
+            small_start(tick - amount + 1)
+    for copy in one_copies:
+        copy.wait()
+    total = reduced(one_ref, one_got_ref, tok, 0, slice(0, D))
+    block = tokens_ref[...].astype(f32)
+    scale = lax.rsqrt(jnp.mean(block * block, axis=1, keepdims=True) + norm_eps)
+    tokens_grad_ref[...] = (
+        grad_hidden_ref[...] + norm_back(total, block * scale, scale, gain_ref[0:1])
+    ).astype(bf16)
+    out_over.wait()
+    output_ref[...] = (
+        hidden_ref[...] + out_own_ref[...] + out_came_ref[...].astype(f32)
+    ).astype(bf16)
+    for copy in small_copies[3]:
+        copy.wait()
+    for copies in row_copies.values():
+        for copy in copies:
+            copy.wait()
+
+
+def kernel_room(shapes):
+    total = 0
+    for shape, dtype in shapes:
+        size = jnp.dtype(dtype).itemsize
+        rows = shape[-2] if len(shape) > 1 else 1
+        padded = -(-rows // 16) * 16 * -(-shape[-1] // LANES) * LANES
+        total += math.prod(shape[:-2]) * padded * size
+    rows = max([0] + [shape[0] for shape, _ in shapes if len(shape) == 2 and shape[0] == shape[1]])
+    total += 20 * rows * rows + 5 * 1024 * 1024
+    return min(max(total, 54 * 1024 * 1024), 62 * 1024 * 1024)
+
+
+def remote_call(kernel, number, out_shapes, scratch, sems, *operands, outside=()):
     spec = pl.BlockSpec(memory_space=pltpu.VMEM)
+    scalars = pl.BlockSpec(memory_space=pltpu.SMEM)
+    anywhere = pl.BlockSpec(memory_space=pl.ANY)
+    inside = [one for k, one in enumerate(operands) if k not in outside]
     return pl.pallas_call(
         kernel,
         out_shape=out_shapes,
-        in_specs=[spec] * len(operands),
+        in_specs=[
+            anywhere if k in outside
+            else scalars if one.dtype == jnp.int32 and one.size < LANES else spec
+            for k, one in enumerate(operands)
+        ],
         out_specs=[spec] * len(out_shapes),
         scratch_shapes=[pltpu.VMEM(shape, dtype) for shape, dtype in scratch] + sems,
         compiler_params=pltpu.CompilerParams(
-            collective_id=number, has_side_effects=True, vmem_limit_bytes=48 * 1024 * 1024
+            collective_id=number, has_side_effects=True,
+            vmem_limit_bytes=kernel_room(
+                [(one.shape, one.dtype) for one in inside + out_shapes] + scratch
+            ),
         ),
     )(*operands)
 
@@ -709,13 +1477,6 @@
         scratch_shapes=[pltpu.VMEM(shape, dtype) for shape, dtype in scratch],
         compiler_params=pltpu.CompilerParams(vmem_limit_bytes=56 * 1024 * 1024),
     )(*operands)
-
-
-def sgu_rows(grad):
-    copies = lax.axis_size("zhi") * lax.axis_size("zlo") * lax.axis_size("core")
-    wide = D // grad.shape[1]
-    pieces = grad.reshape(copies, wide, -1, grad.shape[1])
-    return jnp.concatenate([pieces[:, k] for k in range(wide)], axis=2)
 
 
 def on_device(
@@ -765,68 +1526,59 @@
     win_pieces = jnp.concatenate(
         [z_cols, x_cols, bc_cols, dt_cols, router_cols, fill], axis=2
     ).transpose(1, 0, 2)
-    win_rows = swap(win_pieces, "expert").reshape(groups * rows_in, -1)
-    down_own = jnp.concatenate([w_out.astype(bf16), w_shared_down.astype(bf16)], axis=0)
-    win = lax.all_gather(win_rows, DP, axis=0, tiled=True)
-    router = win[:, body + heads : body + heads + experts]
-    both_all = spread(jnp.stack([tokens, cotangent]), "expert").transpose(1, 0, 2, 3)
-    x_all = both_all[0].reshape(length, D)
-    cot_all = both_all[1].reshape(length, D)
-    routes_two = spread(jnp.stack([routes, to_partner(routes)]), "expert")
-    routes_two = routes_two.transpose(1, 0, 2, 3).reshape(2 * length, top)
-
-    rows_two = rows_out + rows_sd
-    down_rows = lax.all_gather(down_own, DP, axis=0, tiled=False)
-    sd = down_rows[:, rows_out:].reshape(own_ff, D)
-    wout = (
-        swap(down_rows[:, :rows_out].reshape(groups, per_pair * rows_out, D), "expert")
-        .reshape(groups, per_pair, rows_out, D)
-        .transpose(1, 0, 2, 3)
-        .reshape(inner, D)
-    )
     sgu_pieces = (
         w_shared_gu.astype(bf16)
-        .reshape(rows_in, 2, copies, groups, rows_sd)
-        .transpose(3, 0, 1, 2, 4)
+        .reshape(rows_in, 2, groups, own_ff)
+        .transpose(2, 0, 1, 3)
         .reshape(groups, rows_in, 2 * own_ff)
     )
-    sgu = lax.all_gather(
-        swap(sgu_pieces, "expert").reshape(groups * rows_in, 2 * own_ff), DP, axis=0, tiled=True
-    )
-
+    pairs = pltpu.SemaphoreType.DMA
+    route_pad = jnp.pad(routes, ((0, 0), (0, LANES - top)))
+    row_shape = jax.ShapeDtypeStruct((groups, tok, D), bf16)
+    route_shape = jax.ShapeDtypeStruct((groups, tok, LANES), jnp.int32)
     half = lax.axis_index("zhi")
     held = own_experts // 2
     rows_egu, rows_ed = w_expert_gu.shape[1], w_expert_down.shape[1]
-
-    def halves(shard):
-        kept = lax.dynamic_slice_in_dim(shard, half * held, held, axis=0)
-        sent = lax.dynamic_slice_in_dim(shard, (1 - half) * held, held, axis=0)
-        return kept, sent
-
-    def gathered(kept, came):
-        both = jnp.where(half == 0, jnp.stack([kept, came], 1), jnp.stack([came, kept], 1))
-        return lax.all_gather(both, MATES, axis=0, tiled=False)
-
-    egu_own, ed_own = w_expert_gu.astype(bf16), w_expert_down.astype(bf16)
-    win, wout, routes_two, x_all, egu_own, ed_own, cot_own = lax.optimization_barrier(
-        (win, wout, routes_two, x_all, egu_own, ed_own, cotangent)
-    )
-    cot_other = to_partner(cot_own)
-    egu_kept, egu_sent = halves(egu_own)
-    ed_kept, ed_sent = halves(ed_own)
-    egu_came = to_partner(egu_sent)
-    ed_came = to_partner(ed_sent)
-
-    positions = jnp.arange(length, dtype=jnp.int32)
-    starts = jnp.cumsum(lengths[0]) - lengths[0]
-    doc_index = jnp.sum((starts[None, :] <= positions[:, None]).astype(jnp.int32), axis=1) - 1
-    earlier_doc = [
-        jnp.concatenate([jnp.full((offset,), -1, jnp.int32), doc_index[: length - offset]])
-        for offset in range(CONV)
-    ]
-    masks = jnp.stack([(earlier == doc_index).astype(f32) for earlier in earlier_doc], axis=1)
-    masks = jnp.pad(masks, ((0, 0), (0, LANES - CONV)))
-    doc_col, doc_row = doc_index[:, None], doc_index[None, :]
+    gu_held = jax.ShapeDtypeStruct((held, rows_egu, 2 * EXPERT_FF), bf16)
+    ed_held = jax.ShapeDtypeStruct((held, rows_ed, D), bf16)
+    (
+        x_all, cot_all, cot_came, routes_two, win, sgu, wout, sd, masks, doc_col, doc_row,
+        egu_kept, egu_sent, ed_kept, ed_sent,
+    ) = remote_call(
+        start_kernel, 7,
+        [
+            jax.ShapeDtypeStruct((groups, tok, D), bf16),
+            jax.ShapeDtypeStruct((groups, tok, D), bf16),
+            jax.ShapeDtypeStruct((tok, D), bf16),
+            jax.ShapeDtypeStruct((2, groups, tok, LANES), jnp.int32),
+            jax.ShapeDtypeStruct((copies,) + win_pieces.shape, bf16),
+            jax.ShapeDtypeStruct((copies,) + sgu_pieces.shape, bf16),
+            jax.ShapeDtypeStruct((per_pair, groups, rows_out, D), bf16),
+            jax.ShapeDtypeStruct((per_pair, groups, rows_sd, D), bf16),
+            jax.ShapeDtypeStruct((length, LANES), f32),
+            jax.ShapeDtypeStruct((length, 1), jnp.int32),
+            jax.ShapeDtypeStruct((1, length), jnp.int32),
+            gu_held, gu_held, ed_held, ed_held,
+        ],
+        [
+            ((copies, rows_out, D), bf16), ((copies, rows_sd, D), bf16), ((tok, LANES), jnp.int32),
+        ],
+        [pairs((7 * (groups - 1),))] * 2
+        + [pairs((2 * per_pair * (groups - 1),))] * 2
+        + [pairs((2,))] * 2
+        + [pairs((9 + 2 * per_pair,))]
+        + line_sems(copies // 2) * 4,
+        lengths, tokens, cotangent, route_pad, win_pieces, sgu_pieces,
+        w_out.astype(bf16), w_shared_down.astype(bf16), w_expert_gu, w_expert_down,
+    )
+    x_all = x_all.reshape(length, D)
+    routes_two = routes_two.reshape(2 * length, LANES)
+    win = win.reshape(D, -1)
+    sgu = sgu.reshape(D, -1)
+    wout = wout.reshape(inner, D)
+    sd = sd.reshape(own_ff, D)
+    router = win[:, body:]
+
 
     own_x = place * inner
     conv_own = jnp.concatenate(
@@ -850,52 +1602,68 @@
     square = ((length, length), f32)
     lane_rows = ((length, LANES), f32)
     lane_cols = ((LANES, length), f32)
-    packed, dt_raw, full_y, res_part = vmem_call(
-        forward_kernel,
+    planes_half = copies // 4
+    mates = copies // 2
+    spread_sems = [pairs((mate_sems(planes_half),))] * 2
+    gu_all = jax.ShapeDtypeStruct((mates,) + egu_kept.shape, bf16)
+    ed_all = jax.ShapeDtypeStruct((mates,) + ed_kept.shape, bf16)
+    packed, dt_raw, full_y, res_part, gu_near, gu_came, cot_two = remote_call(
+        forward_kernel, 3,
         [
             jax.ShapeDtypeStruct((length, body), bf16),
             jax.ShapeDtypeStruct((length, LANES), f32),
             jax.ShapeDtypeStruct((length, inner), bf16),
             jax.ShapeDtypeStruct((length, D + LANES), bf16),
+            gu_all,
+            gu_held,
+            jax.ShapeDtypeStruct((2, groups, tok, D), bf16),
         ],
         [((length, D), bf16), square, square, lane_rows, lane_cols, ((length, inner), bf16),
          lane_rows],
+        [pairs((groups,))] * 2 + spread_sems + [pairs(()), pairs((2,))],
         x_all, win, gain_rows, conv_pad, masks, head_rows, col_rows, doc_col, doc_row, wout,
-    )
-    pairs = pltpu.SemaphoreType.DMA
-    payload = ((tok, D + LANES), bf16)
-    hidden, mixer_res, two_own = remote_call(
+        egu_kept, egu_sent, cot_all, cot_came, outside=(12, 13),
+    )
+    cot_two = cot_two.reshape(2 * length, D)
+    hidden, mixer_res, two_own, ed_near, ed_came = remote_call(
         hidden_kernel, 0,
         [
             jax.ShapeDtypeStruct((tok, D), f32),
             jax.ShapeDtypeStruct((tok, D), f32),
             jax.ShapeDtypeStruct((tok, D + LANES), bf16),
+            ed_all,
+            ed_held,
         ],
         [((groups - 1, tok, D + LANES), bf16)],
-        [pairs((groups - 1,)), pairs((groups - 1,))],
-        res_part, tokens, gain_rows,
-    )
-    egu_came, ed_came, cot_other, two_own = lax.optimization_barrier(
-        (egu_came, ed_came, cot_other, two_own)
-    )
-    egu = gathered(egu_kept, egu_came)
-    ed = gathered(ed_kept, ed_came)
+        [pairs((groups,))] * 2 + spread_sems + [pairs(())],
+        res_part, tokens, gain_rows, ed_kept, ed_sent,
+    )
     gathered_shape = jax.ShapeDtypeStruct((groups, tok, D + LANES), bf16)
-    got, other_two = remote_call(
-        share_kernel, 1, [gathered_shape] * 2, [payload],
-        [pairs((2 * groups - 1,)), pairs((2 * groups - 1,)), pairs((2,))],
-        two_own,
-    )
-    got = got.reshape(length, -1)
-    other_two = other_two.reshape(length, -1)
-    scale_words = got[:, D:]
-    cot_other = spread(cot_other, "expert").reshape(length, D)
+    own_rows = groups * rows_in
+    payload = ((tok, D + LANES), bf16)
+    tile = 16
+    down_rows = -(-rows_sd // tile) * tile
+    two_rows, gu_far, ed_far, shared_out, shared_back, grad_sgu, grad_sd = remote_call(
+        share_kernel, 1,
+        [
+            jax.ShapeDtypeStruct((2, groups, tok, D + LANES), bf16), gu_all, ed_all,
+            jax.ShapeDtypeStruct((length, D), bf16),
+            jax.ShapeDtypeStruct((length, D), bf16),
+            jax.ShapeDtypeStruct((copies // 2, 2, own_rows, 2 * own_ff), bf16),
+            jax.ShapeDtypeStruct((copies, down_rows, D), bf16),
+        ],
+        [
+            payload, ((length, D), bf16),
+            ((length, own_ff), bf16), ((length, 2 * own_ff), bf16),
+        ],
+        [pairs((2 * groups - 1,))] * 2 + [pairs((2 * mate_sems(planes_half),))] * 2 + [pairs((4,))],
+        two_own, gu_came, ed_came, cot_two, sgu, sd,
+    )
+    scale_words = two_rows[0, :, :, D:].reshape(length, LANES)
+    two_rows = two_rows.reshape(2 * length, D + LANES)
 
     blocks = 2 * groups
     expert_at = (place * own_experts + half * held).reshape(1)
-    two_rows = jnp.concatenate([got, other_two], axis=0)
-    cot_two = jnp.concatenate([cot_all, cot_other], axis=0)
-    router_lanes = jnp.pad(router, ((0, 0), (0, LANES - experts)))
     slot_rows = blocks * capacity
 
     def by_block(*shape):
@@ -908,8 +1676,8 @@
     in_smem = pl.BlockSpec(memory_space=pltpu.SMEM)
     slot_shape = jax.ShapeDtypeStruct((held, slot_rows, D), bf16)
     slot_in, slot_top, slot_grad, weights, pick = grid_call(
-        route_kernel, blocks,
-        [by_block(tok, D + LANES), by_block(tok, D), by_block(tok, top), fixed(D, LANES), in_smem],
+        functools.partial(route_kernel, top_count=top, heads=heads), blocks,
+        [by_block(tok, D + LANES), by_block(tok, D), by_block(tok, LANES), fixed(D, LANES), in_smem],
         [slot_spec] * 3 + [by_block(tok, LANES), by_block(1, tok, held * capacity)],
         [slot_shape] * 3
         + [
@@ -917,45 +1685,34 @@
             jax.ShapeDtypeStruct((blocks, tok, held * capacity), bf16),
         ],
         [],
-        two_rows, cot_two, routes_two, router_lanes, expert_at,
-    )
-    shared_out, shared_back, grad_sgu, grad_sd = vmem_call(
-        shared_kernel,
-        [
-            jax.ShapeDtypeStruct((length, D), bf16),
-            jax.ShapeDtypeStruct((length, D), bf16),
-            jax.ShapeDtypeStruct((D, 2 * own_ff), bf16),
-            jax.ShapeDtypeStruct((own_ff, D), bf16),
-        ],
-        [((length, own_ff), bf16), ((length, 2 * own_ff), bf16)],
-        got, cot_all, sgu, sd,
-    )
-
-    mates = copies // 2
+        two_rows, cot_two, routes_two, router, expert_at,
+    )
     packed_rows = 2 * rows_egu + rows_ed * D // EXPERT_FF
 
     def by_expert(*shape):
         return pl.BlockSpec((1,) + shape, lambda e: (e,) + (0,) * len(shape))
 
     def weight_spec(rows, columns):
-        return pl.BlockSpec((mates, 1, 2, rows, columns), lambda e: (0, e, 0, 0, 0))
+        return pl.BlockSpec((mates, 1, rows, columns), lambda e: (0, e, 0, 0))
 
     slot_out, slot_back, slot_q, expert_grads = grid_call(
         expert_kernel, held,
         [by_expert(slot_rows, D)] * 3
-        + [weight_spec(rows_egu, 2 * EXPERT_FF), weight_spec(rows_ed, D)],
+        + [in_smem]
+        + [weight_spec(rows_egu, 2 * EXPERT_FF)] * 2
+        + [weight_spec(rows_ed, D)] * 2,
         [by_expert(slot_rows, D)] * 2
         + [
             by_expert(slot_rows, LANES),
-            pl.BlockSpec((mates, 2, 1, packed_rows, EXPERT_FF), lambda e: (0, 0, e, 0, 0)),
+            pl.BlockSpec((mates, 1, 2, packed_rows, EXPERT_FF), lambda e: (0, e, 0, 0, 0)),
         ],
         [slot_shape] * 2
         + [
             jax.ShapeDtypeStruct((held, slot_rows, LANES), f32),
-            jax.ShapeDtypeStruct((mates, 2, held, packed_rows, EXPERT_FF), bf16),
+            jax.ShapeDtypeStruct((mates, held, 2, packed_rows, EXPERT_FF), bf16),
         ],
         [((slot_rows, EXPERT_FF), bf16), ((slot_rows, 2 * EXPERT_FF), bf16)],
-        slot_in, slot_top, slot_grad, egu, ed,
+        slot_in, slot_top, slot_grad, half.reshape(1), gu_near, gu_far, ed_near, ed_far,
     )
     own_spec = pl.BlockSpec((tok, D), lambda b: (jnp.minimum(b, groups - 1), 0))
     out_parts, back_parts = grid_call(
@@ -974,92 +1731,103 @@
     )
 
     weights_tok = lax.dynamic_slice_in_dim(weights, place * tok, tok, axis=0)
-    hidden_all, grad_hidden, grad_logits, gain_two = remote_call(
-        functools.partial(back_kernel, own_experts=own_experts), 2,
+    gathered_shape = jax.ShapeDtypeStruct((groups, tok, D + LANES), bf16)
+    hidden_all, grad_hidden, grad_logits, gain_two, expert_sums, came_one = remote_call(
+        functools.partial(back_kernel, own_experts=own_experts, heads=heads), 2,
         [
             gathered_shape,
             jax.ShapeDtypeStruct((tok, D), f32),
             jax.ShapeDtypeStruct((tok, LANES), bf16),
             jax.ShapeDtypeStruct((8, D), f32),
-        ],
-        [((groups - 1, tok, D + LANES), bf16)] * 2 + [payload] * 3,
-        [pairs((3 * groups - 2,)), pairs((3 * groups - 2,)), pairs(())],
-        back_parts, hidden, mixer_res, cotangent, weights_tok, router_lanes, gain_rows,
+            jax.ShapeDtypeStruct((held, 2, packed_rows, EXPERT_FF), bf16),
+            jax.ShapeDtypeStruct((packed_rows, EXPERT_FF), bf16),
+        ],
+        [((groups - 1, tok, D + LANES), bf16)] * 2
+        + [payload] * 3
+        + [
+            ((planes_half - 1, held, 2, packed_rows, EXPERT_FF), bf16),
+            ((planes_half, held, 2, packed_rows, EXPERT_FF), bf16),
+        ],
+        [
+            pairs((3 * groups - 2,)), pairs((3 * groups - 2,)),
+            pairs((held * (planes_half - 1) + 1,)), pairs((held * (planes_half - 1) + 1,)),
+            pairs((held * planes_half,)), pairs((held * planes_half,)),
+            pairs(()),
+        ],
+        back_parts, hidden, mixer_res, cotangent, weights_tok, router, gain_rows,
+        expert_grads.reshape((planes_half, 2) + expert_grads.shape[1:]),
     )
     hidden_all = hidden_all.reshape(length, -1)
     grad_gain_two = gain_two[0]
-    grad_router = dot_tn(two_own[:, :D], grad_logits[:, :experts])
-
-    out_parts, hidden_all = lax.optimization_barrier((out_parts, hidden_all))
-    out_own, out_other = out_parts[:length], out_parts[length:]
-    other_out = swap(out_other.reshape(groups, tok, D), "expert")
-    other_out = to_partner(jnp.sum(other_out.astype(f32), axis=0).astype(bf16))
-    own_out = swap(out_own.reshape(groups, tok, D), "expert")
-
-    expert_mine = lax.psum_scatter(
-        expert_grads.reshape(-1, EXPERT_FF), MATES, scatter_dimension=0, tiled=True
-    ).reshape(expert_grads.shape[1:])
-
-    gate_z = packed[:, :inner].astype(f32)
-    mixer_act = (
-        full_y.astype(f32) * jax.nn.silu(gate_z) * word_sum(scale_words) * gain_own
-    ).astype(bf16)
-    grad_wout = dot_tn(mixer_act, hidden_all[:, :D]).astype(bf16)
-    wout_send = (
-        grad_wout.reshape(per_pair, groups, rows_out, D)
-        .transpose(1, 0, 2, 3)
-        .reshape(groups, per_pair * rows_out, D)
-    )
-    wout_got = swap(wout_send, "expert").reshape(copies, rows_out, D)
-    grad_proj, conv_grads, col_grads, head_grads = vmem_call(
-        backward_kernel,
+
+    out_rows = -(-rows_out // tile) * tile
+    (
+        grad_proj, conv_grads, col_grads, head_grads, expert_sum, grad_wout, out_own, out_other,
+    ) = remote_call(
+        backward_kernel, 5,
         [
             jax.ShapeDtypeStruct((length, body + LANES), bf16),
             jax.ShapeDtypeStruct((8, conv_cols), f32),
             jax.ShapeDtypeStruct((8, inner), f32),
             jax.ShapeDtypeStruct((8, LANES), f32),
+            jax.ShapeDtypeStruct((own_experts, packed_rows, EXPERT_FF), bf16),
+            jax.ShapeDtypeStruct((copies, out_rows, D), bf16),
+            jax.ShapeDtypeStruct((tok, D), f32),
+            jax.ShapeDtypeStruct((tok, D), bf16),
         ],
         [square, square, lane_rows, lane_cols, square, lane_rows, lane_cols, lane_rows, lane_rows,
-         ((length, LANES), bf16)],
+         ((length, LANES), bf16), ((inner, D), bf16), ((packed_rows, EXPERT_FF), bf16),
+         ((2, groups - 1, tok, D), bf16), ((2, tok, D), bf16)],
+        [pairs(()), pairs(()), pairs((2 * groups - 2,)), pairs((2 * groups - 2,)), pairs((2,))],
         hidden_all, scale_words, wout, conv_pad, masks, head_rows, col_rows, doc_col, doc_row,
-        packed, dt_raw, full_y,
-    )
-    conv_grads = conv_grads[: CONV + 1]
-    grad_gain_mix = col_grads[0]
-    grad_skip = jnp.sum(col_grads[1].reshape(heads, HEAD_DIM), axis=1)
-    grad_log_rate = head_grads[0, :heads]
-    grad_bias = head_grads[1, :heads]
-    grad_proj, expert_mine = lax.optimization_barrier((grad_proj, expert_mine))
-    inputs = x_all.astype(f32)
-    normed_one = inputs * rms_scale(inputs)
-    normed = (normed_one * norm_gains[0]).astype(bf16)
-    grad_win = (
-        dot_tn(normed, grad_proj)
-        + jnp.pad(grad_router, ((0, 0), (body + heads, LANES - heads - experts)))
-    ).astype(bf16)
-    rows_sgu = groups * rows_in * 2 * own_ff // D
-    second = jnp.concatenate(
-        [wout_got, grad_sd.reshape(copies, rows_sd, D), sgu_rows(grad_sgu)], axis=1
-    )
-    second = jnp.pad(second, ((0, 0), (0, groups * rows_in - second.shape[1]), (0, 0)))
-    dense = jnp.concatenate(
-        [grad_win.reshape(copies, groups * rows_in, -1), second], axis=2
-    )
-    dense_mine = lax.psum_scatter(dense, DP, scatter_dimension=0, tiled=True)[0]
-    one_part = dot_nt(grad_proj, win)
-    grad_gain_one = jnp.sum(one_part * normed_one, axis=0)
-    one_low = one_part.astype(bf16)
-    one_low, expert_mine, own_out, other_out = lax.optimization_barrier(
-        (one_low, expert_mine, own_out, other_out)
-    )
-    got = swap(one_low.reshape(groups, tok, D), "expert")
-    output = (
-        hidden + jnp.sum(own_out.astype(f32), axis=0) + other_out.astype(f32)
-    ).astype(bf16)
-    kept = lax.dynamic_index_in_dim(expert_mine, half, 0, False)
-    came = to_partner(lax.dynamic_index_in_dim(expert_mine, 1 - half, 0, False))
-    expert_sum = jnp.where(
-        half == 0, jnp.concatenate([kept, came], 0), jnp.concatenate([came, kept], 0)
+        packed, dt_raw, full_y, expert_sums, came_one, out_parts, outside=(14,),
+    )
+    wide_out = D * out_rows // own_rows
+    wide_down = D * down_rows // own_rows
+    chunks_one = (body + LANES) // CHUNK
+    chunks_two = -(-(wide_out + wide_down + 2 * own_ff) // CHUNK)
+    chunks = chunks_one + chunks_two
+    first_shared = chunks_one + (wide_out + wide_down) // CHUNK
+    shared_chunks = list(range(chunks_one)) + list(range(first_shared, chunks))
+    shared_wide = len(shared_chunks) * CHUNK
+    small_wide = conv_cols + inner + LANES + 2 * D
+    folds = own_rows // out_rows + own_rows // down_rows
+    dense_sems = [pairs((chunks,))] * 2 + [pairs((2 * chunks * (planes_half - 1),))] * 2
+    dense_sems += [pairs((chunks,))] * 2 + [pairs((chunks * (groups - 1),))] * 2
+    dense_sems += [pairs((groups - 1,))] * 2 + [pairs((1,))] * 2
+    dense_sems += [pairs((planes_half + groups,))] * 2
+    dense_sems += [pairs((per_pair * folds * (groups - 1),))] * 2
+    dense_sems += [pairs((chunks,)), pairs((per_pair * folds,)), pairs((2,))]
+    got_rows, sum_out, sum_sd, grad_tokens, output, small = remote_call(
+        functools.partial(dense_kernel, shared_chunks=shared_chunks, heads=heads), 6,
+        [
+            jax.ShapeDtypeStruct((groups, rows_in, shared_wide), bf16),
+            jax.ShapeDtypeStruct((out_rows, D), f32),
+            jax.ShapeDtypeStruct((down_rows, D), f32),
+            jax.ShapeDtypeStruct((tok, D), bf16),
+            jax.ShapeDtypeStruct((tok, D), bf16),
+            jax.ShapeDtypeStruct((groups, 8, small_wide), f32),
+        ],
+        [
+            ((length, D), bf16),
+            ((chunks_one, copies // 2, 2, own_rows, CHUNK), bf16),
+            ((copies // 2, 2, own_rows, chunks_two * CHUNK), bf16),
+            ((chunks, copies // 2, own_rows, CHUNK), bf16),
+            ((chunks, planes_half - 1, 2, own_rows, CHUNK), bf16),
+            ((chunks, 2, own_rows, CHUNK), bf16),
+            ((chunks, own_rows, CHUNK), bf16),
+            ((len(shared_chunks), groups, rows_in, CHUNK), bf16),
+            ((length, D), bf16),
+            ((groups - 1, tok, D), bf16),
+            ((tok, D), bf16),
+            ((length, 1), f32),
+            ((4, 8, small_wide), f32),
+            ((planes_half + 1, 8, small_wide), f32),
+        ],
+        dense_sems,
+        x_all, tokens, win, gain_rows, grad_proj, two_own, grad_logits, grad_sgu, grad_wout,
+        grad_sd, grad_hidden, out_own, out_other, hidden, conv_grads, col_grads, head_grads, gain_two,
+        outside=(7, 8, 9),
     )
     sum_egu = jnp.concatenate(
         [expert_sum[:, :rows_egu], expert_sum[:, rows_egu : 2 * rows_egu]], axis=2
@@ -1072,82 +1840,50 @@
         axis=2,
     ).astype(f32)
 
-    grad_norm_one = jnp.sum(got.astype(f32), axis=0)
-    own_in = tokens.astype(f32)
-    own_scale = rms_scale(own_in)
-    grad_tokens = (
-        grad_hidden + norm_back(grad_norm_one, own_in * own_scale, own_scale, norm_gains[0])
-    ).astype(bf16)
-
-    pieces = [
-        conv_grads[:, :inner].reshape(-1),
-        grad_gain_mix,
-        grad_log_rate,
-        grad_bias,
-        grad_skip,
-        conv_grads[:, inner:].reshape(-1),
-        grad_gain_one,
-        grad_gain_two,
-    ]
-    sizes = [piece.size for piece in pieces]
-    total = sum(sizes)
-    unit = copies * LANES
-    small = jnp.pad(jnp.concatenate(pieces), (0, -total % unit)).reshape(copies, -1)
-    small = jnp.sum(swap(small, DP), axis=0)
-    small = spread(small, ("expert",) + DP).reshape(groups, -1)
-    parts = []
-    start = 0
-    for size in sizes:
-        parts.append(small[:, start : start + size])
-        start += size
     sum_conv = jnp.concatenate(
         [
-            parts[0].reshape(groups, CONV + 1, inner).transpose(1, 0, 2).reshape(CONV + 1, INNER),
-            jnp.sum(parts[5], axis=0).reshape(CONV + 1, 2 * STATE),
+            small[:, : CONV + 1, :inner].transpose(1, 0, 2).reshape(CONV + 1, INNER),
+            jnp.sum(small[:, : CONV + 1, inner:conv_cols], axis=0),
         ],
         axis=1,
     )
-    sum_mixer = parts[1].reshape(INNER)
-    sum_head = jnp.stack([parts[2].reshape(HEADS), parts[3].reshape(HEADS), parts[4].reshape(HEADS)])
-    sum_gains = jnp.stack([jnp.sum(parts[6], axis=0), jnp.sum(parts[7], axis=0)])
-
-    win_mine = dense_mine[:, : body + LANES]
-    second_mine = dense_mine[:, body + LANES :]
-    sum_out = second_mine[:rows_out].astype(f32)
-    sum_sd = second_mine[rows_out:rows_two].astype(f32)
-    sgu_mine = jnp.concatenate(
-        [
-            second_mine[rows_two : rows_two + rows_sgu, k * 2 * own_ff : (k + 1) * 2 * own_ff]
-            for k in range(D // (2 * own_ff))
-        ],
-        axis=0,
-    )
-    sum_sgu = (
-        swap(sgu_mine.reshape(groups, rows_in, 2 * own_ff), "expert")
-        .reshape(groups, rows_in, 2, copies, rows_sd)
-        .transpose(1, 2, 3, 0, 4)
-        .reshape(rows_in, 2 * SHARED_FF)
-        .astype(f32)
-    )
-    win_got = swap(win_mine.reshape(groups, rows_in, -1), "expert").astype(f32)
-
-    def laid(start, size):
-        return win_got[:, :, start : start + size].transpose(1, 0, 2).reshape(rows_in, -1)
-
+    start = conv_cols
+    sum_mixer = small[:, 0, start : start + inner].reshape(INNER)
+    sum_skip = jnp.sum(
+        small[:, 1, start : start + inner].reshape(groups, heads, HEAD_DIM), axis=2
+    ).reshape(HEADS)
+    start = start + inner
+    sum_head = jnp.stack(
+        [small[:, k, start : start + heads].reshape(HEADS) for k in range(2)] + [sum_skip]
+    )
+    start = start + LANES
+    gain_sums = jnp.sum(small[:, 0, start:], axis=0)
+    sum_gains = jnp.stack([gain_sums[D:], gain_sums[:D]])
+
+    def laid(source, start, size):
+        return source[:, :, start : start + size].transpose(1, 0, 2).reshape(rows_in, -1)
+
+    win_got = got_rows.astype(f32)
     sum_in = jnp.concatenate(
         [
-            laid(0, inner),
-            laid(inner, inner),
+            laid(win_got, 0, inner),
+            laid(win_got, inner, inner),
             jnp.sum(win_got[:, :, 2 * inner : body], axis=0),
-            laid(body, heads),
+            laid(win_got, body, heads),
         ],
         axis=1,
     )
     sum_router = jnp.sum(win_got[:, :, body + heads : body + heads + experts], axis=0)
-
-    up_in = adam_step(w_in, w_in_first, w_in_second, sum_in)
+    start = body + LANES + (wide_out + wide_down) % CHUNK
+    sum_sgu = (
+        win_got[:, :, start : start + 2 * own_ff]
+        .reshape(groups, rows_in, 2, own_ff)
+        .transpose(1, 2, 0, 3)
+        .reshape(rows_in, 2 * SHARED_FF)
+    )
+    sum_out = sum_out[:rows_out]
+    sum_sd = sum_sd[:rows_sd]
     up_out = adam_step(w_out, w_out_first, w_out_second, sum_out)
-    up_router = adam_step(w_router, w_router_first, w_router_second, sum_router)
     up_sgu = adam_step(w_shared_gu, w_shared_gu_first, w_shared_gu_second, sum_sgu)
     up_sd = adam_step(w_shared_down, w_shared_down_first, w_shared_down_second, sum_sd)
     up_egu = adam_step(w_expert_gu, w_expert_gu_first, w_expert_gu_second, sum_egu)
@@ -1156,6 +1892,9 @@
     up_conv = adam_step(conv_params, conv_params_first, conv_params_second, sum_conv)
     up_head = adam_step(head_params, head_params_first, head_params_second, sum_head)
     up_mixer = adam_step(mixer_gain, mixer_gain_first, mixer_gain_second, sum_mixer)
+
+    up_in = adam_step(w_in, w_in_first, w_in_second, sum_in)
+    up_router = adam_step(w_router, w_router_first, w_router_second, sum_router)
     large = (up_in, up_out, up_router, up_sgu, up_sd, up_egu, up_ed)
     little = (up_gains, up_conv, up_head, up_mixer)
     return (

time: 721 us -> 638 us (0.88)
  Pallas kernels: 225 us -> 562 us
  waiting for transfers between devices: 222 us -> 0 us
  starting transfers between devices: 74.5 us -> 0 us
  other arithmetic: 73.6 us -> 27.9 us
  blocking collectives: 24.6 us -> 0 us
  local copies, waits for them, and re-layouts: 56.7 us -> 36.8 us
  matrix products: 18 us -> 0 us
  between operations: 15.4 us -> 1.62 us
    pallas_call x6 -> x7, Pallas kernels: 178 us -> 514 us  [remote_call(): pl.pallas_call(kernel, out_shape=out_shapes, in_specs=[anywhere if k in o...]
    all_to_all x12 -> x0, waiting for transfers between devices: 168 us -> none  [swap(): return lax.all_to_all(pieces, axis, split_axis=0, concat_axis=0, tiled=True)]
    all_to_all x12 -> x0, starting transfers between devices: 51 us -> none  [swap(): return lax.all_to_all(pieces, axis, split_axis=0, concat_axis=0, tiled=True)]
    ppermute x6 -> x0, waiting for transfers between devices: 36.7 us -> none  [to_partner(): return lax.ppermute(value, 'zhi', [(0, 1), (1, 0)])]
    all_to_all x2 -> x0, blocking collectives: 24.6 us -> none  [swap(): return lax.all_to_all(pieces, axis, split_axis=0, concat_axis=0, tiled=True)]
    concatenate x5 -> x0, other arithmetic: 21 us -> none  [the longest x1 13.5 us: on_device(): jnp.concatenate([grad_win.reshape(copies, groups * rows_in, -1), second],...]
    dot_general x4 -> x0, matrix products: 18 us -> none  [the longest x3 10 us: dot_tn(): lax.dot_general(left, right, (((0,), (0,)), ((), ())), preferred_element_...]
    all_gather x5 -> x0, waiting for transfers between devices: 17.3 us -> none  [the longest x2 8.78 us: gathered(): return lax.all_gather(both, MATES, axis=0, tiled=False)]
  transfers between devices with their start and end apart: 25 -> 0, of which waited for: 16 -> 0; matrix products, arithmetic and copies ran while one was open for 16% -> 0% of each run, Pallas kernels for 32% -> 0%
where the time goes in v3:
time: 638 us; the launch traced here: 628 us
  Pallas kernels  562 us (88%)
  local copies, waits for them, and re-layouts  36.8 us (6%)
  other arithmetic  27.9 us (4%)
    pallas_call x7, Pallas kernels, remote_call(): pl.pallas_call(kernel, out_shape=out_shapes, in_specs=[anywhere if k in o...  514 us
    pallas_call x3, Pallas kernels, grid_call(): pl.pallas_call(kernel, grid=(steps,), out_shape=out_shapes, in_specs=in_s...  48 us
    add x7, other arithmetic, adam_step(): return (gradient, weight + moved, moment_one, moment_two, moved)  16.5 us

profile of v3, /device:TPU:0, one launch (start us, length us, event | category | flops | bytes accessed | tf_op | source)
XLA Modules:
  0.0 628.0 jit_solution(7667837847479560232)
XLA Ops:
  0.7 0.8 constant_dynamic-slice_fusion.1
  1.5 0.8 dynamic_slice.14
  2.3 0.6 select_maximum_fusion.2.head_ref
  2.9 0.7 convert_element_type.33
  3.9 0.7 slice.94
  4.6 0.6 select_maximum_fusion.1.cols_ref
  5.2 0.7 constant_dynamic-slice_fusion.2
  5.9 0.6 select_maximum_fusion.conv_ref
  6.6 1.3 pad.21.gain_ref
  7.9 0.9 copy.119
  8.8 0.6 pad.20.routes_ref
  9.4 1.6 convert_element_type.36.sd_ref
  11.0 1.0 convert_element_type.34
  12.3 0.8 reshape.167.sgu_ref
  13.1 0.7 convert_element_type.35.wout_ref
  14.3 1.0 concatenate.18
  15.4 118.4 %shard_map.708 = (bf16[4,128,1536]{2,1,0:T(8,128)(2,1)}, bf16[4,128,1536]{2,1,0:T(8,128)(2,1)}, bf16[128,1536]{1,0:T(8,128)(2,1)}, s32[2,4,128,128]{3,2,1,0:T(8,...) custom-call(s32[1,3]{1,0:T(1,128)} %lengths_ref.1, ...), custom_call_target="tpu_custom_call" | custom-call | tf_op jit(solution)/shard_map/pallas_call | solution.py:1439
  133.8 1.8 slice.124.router_ref
  135.6 46.6 %shard_map.709 = (bf16[512,1792]{1,0:T(8,128)(2,1)}, f32[512,128]{1,0:T(8,128)}, bf16[512,768]{1,0:T(8,128)(2,1)}, bf16[512,1664]{1,0:T(8,128)(2,1)}, bf16[4,2,1...) custom-call(bf16[512,1536]{1,0:T(8,128)(2,1)} %bitcast.52, ...), custom_call_target="tpu_custom_call" | custom-call | tf_op jit(solution)/shard_map/pallas_call | solution.py:1439
  182.2 29.1 %shard_map.710 = (f32[128,1536]{1,0:T(8,128)}, f32[128,1536]{1,0:T(8,128)}, bf16[128,1664]{1,0:T(8,128)(2,1)}, bf16[4,2,64,1536]{3,2,1,0:T(8,128)(2,1)}, bf16[2,64,1536]{2,1,0:T(8,128)(2,1)}) custom-call(bf16[512,1664]{1,0:T(8,128)(2,1)} %get-tuple-element.121.part_ref, bf16[128,1536]{1,0:T(8,128)(2,1)} %tokens_ref.3, f32[8,1536]{1,0:T(8,128)} %pad.21.gain_ref, ...), custom_call_target="tpu_custom_call" | custom-call | tf_op jit(solution)/shard_map/pallas_call | solution.py:1439
  211.3 52.3 %shard_map.711 = (bf16[2,4,128,1664]{3,2,1,0:T(8,128)(2,1)}, bf16[4,2,192,1024]{3,2,1,0:T(8,128)(2,1)}, bf16[4,2,64,1536]{3,2,1,0:T(8,128)(2,1)}, bf16[512,1536]...) custom-call(bf16[128,1664]{1,0:T(8,128)(2,1)} %get-tuple-element.124.t, ...), custom_call_target="tpu_custom_call" | custom-call | tf_op jit(solution)/shard_map/pallas_call | solution.py:1439
  263.6 1.6 slice.99
  265.1 12.9 %shard_map.712 = (bf16[2,512,1536]{2,1,0:T(8,128)(2,1)}, bf16[2,512,1536]{2,1,0:T(8,128)(2,1)}, bf16[2,512,1536]{2,1,0:T(8,128)(2,1)}, f32[1024,128]{1,0:T(8,128)}, bf16[8,128,128]{2,1,0:T(8,128)(2,1)}) custom-call(bf16[1024,1664]{1,0:T(8,128)(2,1)} %bitcast.54, bf16[1024,1536]{1,0:T(8,128)(2,1)} %bitcast.48, s32[1024,128]{1,0:T(8,128)} %bitcast.66, ...), custom_call_target="tpu_custom_call" | custom-call | tf_op jit(solution)/shard_map/pallas_call | solution.py:1471
  278.0 1.5 constant_dynamic-slice_fusion.weights_ref
  279.5 24.4 %shard_map.713 = (bf16[2,512,1536]{2,1,0:T(8,128)(2,1)}, bf16[2,512,1536]{2,1,0:T(8,128)(2,1)}, f32[2,512,128]{2,1,0:T(8,128)}, bf16[4,2,2,576,512]{4,3,2,1,0:T(8,128)(2,1)}) custom-call(bf16[2,512,1536]{2,1,0:T(8,128)(2,1)} %get-tuple-element.134.in_ref, bf16[2,512,1536]{2,1,0:T(8,128)(2,1)} %get-tuple-element.135.top_ref, ...), custom_call_target="tpu_custom_call" | custom-call | tf_op jit(solution)/shard_map/pallas_call | solution.py:1471
  303.9 10.8 %shard_map.714 = (bf16[1024,1536]{1,0:T(8,128)(2,1)}, bf16[1024,1664]{1,0:T(8,128)(2,1)}) custom-call(bf16[8,128,128]{2,1,0:T(8,128)(2,1)} %get-tuple-element.132.pick_ref, f32[1024,128]{1,0:T(8,128)} %get-tuple-element.133.weights_ref, s32[1]{0:T(128)} %bitcast.11.ids_ref, bf16[2,512,1536]{2,1,0:T(8,128)(2,1)} %get-tuple-element.141.out_ref, ...), custom_call_target="tpu_custom_call" | custom-call | tf_op jit(solution)/shard_map/pallas_call | solution.py:1471
  314.6 88.7 %shard_map.715 = (bf16[4,128,1664]{2,1,0:T(8,128)(2,1)}, f32[128,1536]{1,0:T(8,128)}, bf16[128,128]{1,0:T(8,128)(2,1)}, f32[8,1536]{1,0:T(8,128)}, bf16[2,2,576,...) custom-call(bf16[1024,1664]{1,0:T(8,128)(2,1)} %get-tuple-element.146.back_ref, f32[128,1536]{1,0:T(8,128)} %get-tuple-element.147.hidden_ref, ...), custom_call_target="tpu_custom_call" | custom-call | tf_op jit(solution)/shard_map/pallas_call | solution.py:1439
  403.4 46.2 %shard_map.716 = (bf16[512,1920]{1,0:T(8,128)(2,1)}, f32[8,1024]{1,0:T(8,128)}, f32[8,768]{1,0:T(8,128)}, f32[8,128]{1,0:T(8,128)}, bf16[4,576,512]{2,1,0:T(8,12...) custom-call(bf16[512,1664]{1,0:T(8,128)(2,1)} %bitcast.58, ...), custom_call_target="tpu_custom_call" | custom-call | tf_op jit(solution)/shard_map/pallas_call | solution.py:1439
  449.8 132.2 %shard_map.717 = (bf16[4,48,2688]{2,1,0:T(8,128)(2,1)}, f32[96,1536]{1,0:T(8,128)}, f32[32,1536]{1,0:T(8,128)}, bf16[128,1536]{1,0:T(8,128)(2,1)}, bf16[128,1536]{1,0:T(8,128)(2,1)}, /*index=5*/f32[4,8,4992]{2,1,0:T(8,128)}) custom-call(bf16[512,1536]{1,0:T(8,128)(2,1)} %bitcast.53, bf16[128,1536]{1,0:T(8,128)(2,1)} %tokens_ref.3, ...), custom_call_target="tpu_custom_call" | custom-call | tf_op jit(solution)/shard_map/pallas_call | solution.py:1439
  582.0 0.8 slice_reduce_fusion.6
  583.0 0.8 slice_reduce_fusion.3
  583.8 1.0 slice_reduce_fusion.2
  584.9 1.0 fusion.24
  585.9 0.9 slice.114
  587.1 0.6 add_multiply_fusion.3
  587.7 0.7 add_multiply_fusion.2
  588.4 0.6 add_multiply_fusion.1
  589.0 0.8 add_multiply_fusion
  589.8 1.0 slice.130
  591.4 0.9 reshape.184
  592.4 0.9 multiply_add_fusion.10
  593.3 2.0 fusion.22
  595.3 1.2 fusion.23
  597.7 1.3 multiply_add_fusion.15
  599.0 0.6 slice_reduce_fusion
  599.7 0.6 slice_bitcast_fusion.2
  600.3 1.1 slice_bitcast_fusion.1
  601.4 1.1 copy.128
  602.6 1.2 copy.137
  603.8 1.1 copy.138
  605.0 1.5 multiply_add_fusion.6
  606.8 1.2 multiply_add_fusion.8
  608.0 0.7 copy-done.17
  608.7 2.8 multiply_add_fusion.4
  612.1 0.7 copy-done.15
  613.0 3.6 multiply_add_fusion.2
  616.7 0.8 copy-done.4
  617.5 1.0 copy-done.5
  618.6 0.9 copy-done.6
  619.5 5.1 multiply_add_fusion
  624.6 0.7 copy.147
  625.4 0.7 copy.148
  626.1 0.8 copy.149
  626.9 0.7 copy.150
  (122 shorter events, 4.4 us)
Async XLA Ops:
  0.7 12.4 %copy-start.8 = (f32[96,1536]{1,0:T(8,128)S(1)}, f32[96,1536]{1,0:T(8,128)}, u32[]{:S(2)}) copy-start(f32[96,1536]{1,0:T(8,128)} %param.44) | copy-start | bytes 1769476
  7.9 6.0 copy-start.2
  449.6 137.4 %copy-start.44 = (f32[3,48]{1,0:T(4,128)S(1)}, f32[3,48]{1,0:T(4,128)}, u32[]{:S(2)}) copy-start(f32[3,48]{1,0:T(4,128)} %param.68) | copy-start | bytes 1732
  449.6 137.4 %copy-start.45 = (f32[3,48]{1,0:T(4,128)S(1)}, f32[3,48]{1,0:T(4,128)}, u32[]{:S(2)}) copy-start(f32[3,48]{1,0:T(4,128)} %param.69) | copy-start | bytes 1732
  449.7 137.4 %copy-start.46 = (f32[3,48]{1,0:T(4,128)S(1)}, f32[3,48]{1,0:T(4,128)}, u32[]{:S(2)}) copy-start(f32[3,48]{1,0:T(4,128)} %param.70) | copy-start | bytes 1732
  449.7 138.0 %copy-start.35 = (f32[2,1536]{1,0:T(2,128)S(1)}, f32[2,1536]{1,0:T(2,128)}, u32[]{:S(2)}) copy-start(f32[2,1536]{1,0:T(2,128)} %param.62) | copy-start | bytes 36868
  449.7 138.0 %copy-start.40 = (f32[2,1536]{1,0:T(2,128)S(1)}, f32[2,1536]{1,0:T(2,128)}, u32[]{:S(2)}) copy-start(f32[2,1536]{1,0:T(2,128)} %param.63) | copy-start | bytes 36868
  449.7 138.0 %copy-start.41 = (f32[2,1536]{1,0:T(2,128)S(1)}, f32[2,1536]{1,0:T(2,128)}, u32[]{:S(2)}) copy-start(f32[2,1536]{1,0:T(2,128)} %param.64) | copy-start | bytes 36868
  449.7 138.7 %copy-start.39 = (f32[3072]{0:T(1024)S(1)}, f32[3072]{0:T(1024)}, u32[]{:S(2)}) copy-start(f32[3072]{0:T(1024)} %param.71) | copy-start | bytes 36868
  449.7 138.7 %copy-start.42 = (f32[3072]{0:T(1024)S(1)}, f32[3072]{0:T(1024)}, u32[]{:S(2)}) copy-start(f32[3072]{0:T(1024)} %param.72) | copy-start | bytes 36868
  449.7 138.6 %copy-start.43 = (f32[3072]{0:T(1024)S(1)}, f32[3072]{0:T(1024)}, u32[]{:S(2)}) copy-start(f32[3072]{0:T(1024)} %param.73) | copy-start | bytes 36868
  449.7 139.3 %copy-start.32 = (f32[5,3328]{1,0:T(8,128)S(1)}, f32[5,3328]{1,0:T(8,128)}, u32[]{:S(2)}) copy-start(f32[5,3328]{1,0:T(8,128)} %param.65) | copy-start | bytes 199684
  449.8 139.3 %copy-start.33 = (f32[5,3328]{1,0:T(8,128)S(1)}, f32[5,3328]{1,0:T(8,128)}, u32[]{:S(2)}) copy-start(f32[5,3328]{1,0:T(8,128)} %param.66) | copy-start | bytes 199684
  449.8 139.2 %copy-start.34 = (f32[5,3328]{1,0:T(8,128)S(1)}, f32[5,3328]{1,0:T(8,128)}, u32[]{:S(2)}) copy-start(f32[5,3328]{1,0:T(8,128)} %param.67) | copy-start | bytes 199684
  585.9 5.5 copy-start.36
  589.8 2.5 copy-start.21
  589.8 2.5 copy-start.22
  589.8 2.5 copy-start.30
  589.8 2.5 copy-start.31
  592.4 2.9 copy-start.7
  595.3 1.7 copy-start.11
  597.0 0.7 copy-start.37
  597.7 6.1 copy-start.38
  601.4 3.5 copy-start.9
  601.4 3.5 copy-start.10
  601.4 3.5 copy-start.23
  602.6 2.4 copy-start.24
  605.0 1.6 copy-start.12
  605.0 1.6 copy-start.13
  605.0 1.6 copy-start.27
  605.0 1.8 copy-start.28
  606.6 1.5 copy-start.16
  606.6 2.1 copy-start.17
  606.6 2.1 copy-start.29
  608.7 2.9 copy-start.1
  608.7 3.4 copy-start.14
  608.7 4.2 copy-start.15
  608.7 4.2 copy-start.18
  608.7 4.2 copy-start.19
  608.7 4.3 copy-start.20
  613.0 3.7 copy-start
  613.0 3.7 copy-start.3
  613.0 4.5 copy-start.4
  613.0 5.5 copy-start.5
  613.0 6.4 %copy-start.6 = (f32[4,192,1024]{2,1,0:T(8,128)S(1)}, f32[4,192,1024]{2,1,0:T(8,128)}, u32[]{:S(2)}) copy-start(f32[4,192,1024]{2,1,0:T(8,128)} %param.58) | copy-start | bytes 9437188
  619.5 5.2 copy-start.26
  619.5 5.9 copy-start.25

commit v4 on v3

--- a/solution.py
+++ b/solution.py
@@ -282,23 +282,18 @@
 def backward_kernel(hid_ref, scale_ref, wout_ref, conv_ref, masks_ref, head_ref, cols_ref,
                     doc_col_ref, doc_row_ref, packed_ref, dt_ref, y_ref, sums_ref, came_one_ref, out_ref,
                     proj_ref, conv_grad_ref, cols_grad_ref, head_grad_ref, total_ref, wout_send_ref,
-                    out_own_ref, out_send_ref,
+                    out_send_ref,
                     neg_ref, scores_ref, cum_ref, cum_t_ref, grad_scores_ref, row_ref, col_ref,
                     step_ref, scaled_ref, low_ref, wout_grad_ref, theirs_ref, out_got_ref, out_mine_ref, send_sem, recv_sem, out_send, out_recv,
                     out_local):
     greet(group_ids() + [partner_id()])
-    tok = out_own_ref.shape[0]
+    tok = out_send_ref.shape[0]
     count = lax.axis_size("expert")
     out_sems = (out_send, out_recv)
     rows_all = out_ref.shape[0] // 2
-    out_copies = reduce_copies(out_ref, out_got_ref.at[0], out_sems, 0, tok, rows_all)
-    out_copies += reduce_copies(out_ref, out_got_ref.at[1], out_sems, count - 1, tok, 0)
-    mine = pl.ds(pl.multiple_of(lax.axis_index("expert") * tok, tok), tok)
+    out_copies = reduce_copies(out_ref, out_got_ref, out_sems, 0, tok, rows_all)
     yours = pl.ds(pl.multiple_of(rows_all + lax.axis_index("expert") * tok, tok), tok)
-    out_copies += [
-        pltpu.make_async_copy(out_ref.at[yours], out_mine_ref.at[0], out_local.at[0]),
-        pltpu.make_async_copy(out_ref.at[mine], out_mine_ref.at[1], out_local.at[1]),
-    ]
+    out_copies.append(pltpu.make_async_copy(out_ref.at[yours], out_mine_ref, out_local))
     for copy in out_copies:
         copy.start()
     half = lax.axis_index("zhi")
@@ -423,14 +418,10 @@
     proj_ref[:, body:] = grad_pre.astype(bf16)
     for copy in out_copies:
         copy.wait()
-    totals = []
-    for side in range(2):
-        total = out_mine_ref[side].astype(f32)
-        for number in range(count - 1):
-            total = total + out_got_ref[side, number].astype(f32)
-        totals.append(total)
-    out_send_ref[...] = totals[0].astype(bf16)
-    out_own_ref[...] = totals[1]
+    total = out_mine_ref[...].astype(f32)
+    for number in range(count - 1):
+        total = total + out_got_ref[number].astype(f32)
+    out_send_ref[...] = total.astype(bf16)
     across.wait()
     total_ref[(1 - half) * held + 1] = theirs_ref[...]
 
@@ -754,13 +745,14 @@
             )
 
 
-def start_kernel(lengths_ref, x_ref, cot_ref, routes_ref, win_ref, sgu_ref, wout_ref, sd_ref,
-                 gu_ref, down_ref,
-                 x_all_ref, cot_all_ref, cot_came_ref, routes_two_ref, win_all_ref, sgu_all_ref, wout_own_ref,
-                 sd_own_ref, masks_ref, doc_col_ref, doc_row_ref, gu_kept_ref, gu_sent_ref,
-                 down_kept_ref, down_sent_ref,
-                 wout_all_ref, sd_all_ref, routes_came_ref, send_sems, recv_sems,
-                 out_send, out_recv, near_send, near_recv, local_sems, *line):
+def start_kernel(lengths_ref, x_ref, cot_ref, routes_ref, w_in_ref, w_router_ref, w_sgu_ref, w_out_ref,
+                 w_sd_ref, gu_ref, down_ref, conv_ref, head_ref, mixer_ref,
+                 x_all_ref, cot_all_ref, cot_came_ref, routes_two_ref, win_all_ref, sgu_all_ref,
+                 wout_own_ref, sd_own_ref, masks_ref, doc_col_ref, doc_row_ref, gu_kept_ref,
+                 gu_sent_ref, down_kept_ref, down_sent_ref, conv_own_ref, head_own_ref, cols_ref,
+                 wout_all_ref, sd_all_ref, routes_came_ref, win_ref, sgu_ref, wout_ref, sd_ref,
+                 tail_ref, send_sems, recv_sems, out_send, out_recv, near_send, near_recv,
+                 local_sems, *line):
     count, me, others = peers()
     at, planes = plane_place()
     half = lax.axis_index("zhi")
@@ -808,7 +800,34 @@
         LineGather(full, line[6 * k : 6 * k + 6])
         for k, full in enumerate((win_all_ref, wout_all_ref, sgu_all_ref, sd_all_ref))
     ]
+    inner = INNER // count
+    heads = HEADS // count
+    own_ff = SHARED_FF // count
+    body = 2 * inner + 2 * STATE
+    tail_ref[...] = jnp.zeros_like(tail_ref)
+    tail_ref[0, :, :HEADS] = w_in_ref[:, 2 * INNER + 2 * STATE :]
+    tail_ref[1, :, : w_router_ref.shape[1]] = w_router_ref[...]
+    lanes_in = lax.broadcasted_iota(jnp.int32, tail_ref.shape[1:], 1)
+    routers = pltpu.roll(tail_ref[1], heads, 1)
+    for g in range(count):
+        win_ref[g, :, :inner] = w_in_ref[:, g * inner : (g + 1) * inner].astype(bf16)
+        win_ref[g, :, inner : 2 * inner] = w_in_ref[
+            :, INNER + g * inner : INNER + (g + 1) * inner
+        ].astype(bf16)
+        win_ref[g, :, 2 * inner : body] = w_in_ref[:, 2 * INNER : 2 * INNER + 2 * STATE].astype(
+            bf16
+        )
+        steps = pltpu.roll(tail_ref[0], LANES - g * heads, 1) if g else tail_ref[0]
+        win_ref[g, :, body:] = jnp.where(lanes_in < heads, steps, routers).astype(bf16)
     win_copies = started(pieces(win_ref, win_all_ref, 0, local_sems.at[0]))
+    wout_ref[...] = w_out_ref[...].astype(bf16)
+    sd_ref[...] = w_sd_ref[...].astype(bf16)
+    for g in range(count):
+        for k in range(2):
+            start = k * SHARED_FF + g * own_ff
+            sgu_ref[g, :, k * own_ff : (k + 1) * own_ff] = w_sgu_ref[
+                :, start : start + own_ff
+            ].astype(bf16)
     keep = started([
         pltpu.make_async_copy(wout_ref, wout_all_ref.at[slot], local_sems.at[1]),
         pltpu.make_async_copy(sd_ref, sd_all_ref.at[slot], local_sems.at[2]),
@@ -822,6 +841,7 @@
     lines[0].start()
     wide = started(
         shared_rows(x_ref, x_all_ref, 2 * peer_count, local_sems.at[4])
+        + shared_rows(cot_ref, cot_all_ref, 4 * peer_count, local_sems.at[6])
         + shared_rows(routes_ref, routes_two_ref.at[0], 3 * peer_count, local_sems.at[5])
     )
     for step in range(planes - 1):
@@ -849,8 +869,29 @@
     ended(sgu_copies)
     lines[2].start()
     cot_over = started([remote(cot_ref, cot_came_ref, near, 0, partner_id())])
-    wide += started(shared_rows(cot_ref, cot_all_ref, 4 * peer_count, local_sems.at[6]))
-
+
+    at_inner = pl.ds(pl.multiple_of(me * inner, LANES), inner)
+    conv_own_ref[...] = jnp.zeros_like(conv_own_ref)
+    conv_own_ref[: CONV + 1, :inner] = conv_ref[:, at_inner]
+    conv_own_ref[: CONV + 1, inner:] = conv_ref[:, INNER:]
+    tail_ref[0] = jnp.zeros_like(tail_ref[0])
+    tail_ref[0, :3, :HEADS] = head_ref[...]
+    mine = tail_ref[0, :8, :]
+    for g in range(1, count):
+        moved = pltpu.roll(tail_ref[0, :8, :], LANES - g * heads, 1)
+        mine = jnp.where(me == g, moved, mine)
+    lane_eight = lax.broadcasted_iota(jnp.int32, mine.shape, 1)
+    row_eight = lax.broadcasted_iota(jnp.int32, mine.shape, 0)
+    mine = jnp.where((lane_eight < heads) & (row_eight < 3), mine, 0.0)
+    head_own_ref[...] = jnp.where(
+        (row_eight == 0) & (lane_eight < heads), jnp.exp(mine), mine
+    )
+    cols_ref[...] = jnp.zeros_like(cols_ref)
+    cols_ref[0:1, :] = mixer_ref[:, at_inner]
+    for pair in range(inner // LANES):
+        cols_ref[1:2, pair * LANES : (pair + 1) * LANES] = dot_words_left(
+            mine, head_lanes(pair)
+        )[2:3]
     length = masks_ref.shape[0]
     place = lax.broadcasted_iota(jnp.int32, (length, LANES), 0)
     lane = lax.broadcasted_iota(jnp.int32, (length, LANES), 1)
@@ -1009,9 +1050,9 @@
 
 def back_kernel(back_ref, hidden_ref, res_ref, cot_ref, weights_ref, router_ref, gain_ref, grads_ref,
                 all_ref, grad_hidden_ref, grad_logits_ref, gain_grad_ref, sums_ref, theirs_ref,
-                got_other_ref, got_own_ref, send_ref, came_ref, low_ref, slots_ref, core_ref,
-                send_sems, recv_sems, plane_send, plane_recv, core_send, core_recv, local_sem,
-                *, own_experts, heads):
+                got_other_ref, got_own_ref, send_ref, came_ref, low_ref, slots_ref, core_ref, mine_ref,
+                send_sems, recv_sems, plane_send, plane_recv, core_send, core_recv, mine_sems,
+                local_sem, *, own_experts, heads):
     tok = cot_ref.shape[0]
     length = back_ref.shape[0] // 2
     held = own_experts // 2
@@ -1046,14 +1087,20 @@
     ]
     first = reduce_copies(back_ref, got_other_ref, sems, 0, tok, length)
     second = reduce_copies(back_ref, got_own_ref, sems, count - 1, tok, 0)
-    for copy in first + core_copies[0] + core_copies[1]:
+    loads = [
+        pltpu.make_async_copy(grads_ref.at[z, core], mine_ref.at[z], mine_sems.at[z])
+        for z in range(planes_here)
+    ]
+    for copy in loads + first + core_copies[0] + core_copies[1]:
         copy.start()
+    for copy in loads:
+        copy.wait()
     for expert in range(held):
         for z, copy in enumerate(core_copies[expert]):
             copy.wait()
             for h in range(2):
                 core_ref[z, expert, h] = (
-                    core_ref[z, expert, h].astype(f32) + grads_ref[z, core, expert, h].astype(f32)
+                    core_ref[z, expert, h].astype(f32) + mine_ref[z, expert, h].astype(f32)
                 ).astype(bf16)
         if expert == 0:
             for copy in planes[0]:
@@ -1128,12 +1175,13 @@
 
 
 def dense_kernel(x_ref, tokens_ref, win_ref, gain_ref, proj_ref, two_ref, logits_ref, sgu_ref,
-                 wout_ref, down_ref, grad_hidden_ref, out_own_ref, out_send_ref, hidden_ref,
+                 wout_ref, down_ref, grad_hidden_ref, out_ref, out_send_ref, hidden_ref,
                  conv_ref, cols_ref,
                  head_ref, gain_two_ref,
                  got_ref, own_out_ref, own_down_ref, tokens_grad_ref, output_ref, all_small_ref,
                  normed_ref, first_ref, second_ref, core_ref, slots_ref, plane_ref, came_ref,
-                 send_ref, one_ref, one_got_ref, out_came_ref, scale_ref, step_ref, step_came_ref, core_send, core_recv, plane_send,
+                 send_ref, one_ref, one_got_ref, out_came_ref, out_got_ref, out_mine_ref, scale_ref,
+                 step_ref, step_came_ref, core_send, core_recv, plane_send,
                  plane_recv, half_send, half_recv, row_send, row_recv, one_send, one_recv, out_send,
                  out_recv, small_send, small_recv, fold_send, fold_recv, local_sems, fold_sems,
                  own_sems, *, shared_chunks, heads):
@@ -1291,7 +1339,12 @@
         normed_ref[rows, :] = (block * scale * gain_ref[0:1]).astype(bf16)
         scale_ref[rows, :] = scale
 
-    out_over = remote(out_send_ref, out_came_ref, (out_send, out_recv), 0, partner_id())
+    out_sems = (out_send, out_recv)
+    out_over = remote(out_send_ref, out_came_ref, out_sems, 0, partner_id())
+    out_copies = reduce_copies(out_ref, out_got_ref, out_sems, 1, tok, 0)
+    out_copies.append(pltpu.make_async_copy(
+        out_ref.at[pl.ds(pl.multiple_of(me * tok, tok), tok)], out_mine_ref, own_sems.at[2]
+    ))
 
     def produce(chunk):
         if chunk in ready:
@@ -1329,16 +1382,15 @@
     begin += cols_ref.shape[1]
     step_ref[0, :, begin : begin + LANES] = head_ref[...]
     begin += LANES
-    step_ref[0, :, begin : begin + D] = gain_two_ref[...]
-    begin += D
+    for k in range(D // CHUNK):
+        step_ref[0, k : k + 1, begin:] = gain_two_ref[0:1, k * CHUNK : (k + 1) * CHUNK]
 
     def input_part(part):
         at = slice(part * CHUNK, (part + 1) * CHUNK)
         one = dot_nt(proj_ref[...], win_ref[at, :])
         gains = jnp.sum(one * (x_ref[:, at].astype(f32) * scale_ref[...]), axis=0, keepdims=True)
-        step_ref[0, :, begin + part * CHUNK : begin + (part + 1) * CHUNK] = jnp.broadcast_to(
-            gains, (8, CHUNK)
-        )
+        row = D // CHUNK + part
+        step_ref[0, row : row + 1, begin:] = gains
         one_ref[:, at] = one.astype(bf16)
 
     one_copies = reduce_copies(one_ref, one_got_ref, (one_send, one_recv), 0, tok, 0)
@@ -1379,6 +1431,7 @@
 
     amount = len(order)
     parts = D // CHUNK
+    small_every = max(1, (amount + 4 - parts) // 3)
     produce(order[0])
     for tick in range(amount + 4):
         if tick + 1 < amount:
@@ -1387,19 +1440,23 @@
             send_plane(order[tick])
         if tick == 2:
             out_over.start()
+        if tick == parts:
+            for copy in out_copies:
+                copy.start()
         if 2 <= tick < amount + 2:
             send_half(order[tick - 2])
         if 4 <= tick:
             send_rows(order[tick - 4])
-        if amount - parts <= tick < amount:
-            input_part(tick - (amount - parts))
-        if tick == amount - 1:
+        if tick < parts:
+            input_part(tick)
+        if tick == parts - 1:
             for copy in one_copies:
                 copy.start()
             small_start(0)
-        if amount <= tick < amount + 3:
-            small_sum(tick - amount)
-            small_start(tick - amount + 1)
+        level = (tick - parts) // small_every
+        if tick >= parts and (tick - parts) % small_every == small_every - 1 and level < 3:
+            small_sum(level)
+            small_start(level + 1)
     for copy in one_copies:
         copy.wait()
     total = reduced(one_ref, one_got_ref, tok, 0, slice(0, D))
@@ -1408,10 +1465,12 @@
     tokens_grad_ref[...] = (
         grad_hidden_ref[...] + norm_back(total, block * scale, scale, gain_ref[0:1])
     ).astype(bf16)
-    out_over.wait()
-    output_ref[...] = (
-        hidden_ref[...] + out_own_ref[...] + out_came_ref[...].astype(f32)
-    ).astype(bf16)
+    for copy in out_copies + [out_over]:
+        copy.wait()
+    total = hidden_ref[...] + out_came_ref[...].astype(f32) + out_mine_ref[...].astype(f32)
+    for number in range(count - 1):
+        total = total + out_got_ref[number].astype(f32)
+    output_ref[...] = total.astype(bf16)
     for copy in small_copies[3]:
         copy.wait()
     for copies in row_copies.values():
@@ -1428,14 +1487,15 @@
         total += math.prod(shape[:-2]) * padded * size
     rows = max([0] + [shape[0] for shape, _ in shapes if len(shape) == 2 and shape[0] == shape[1]])
     total += 20 * rows * rows + 5 * 1024 * 1024
-    return min(max(total, 54 * 1024 * 1024), 62 * 1024 * 1024)
-
-
-def remote_call(kernel, number, out_shapes, scratch, sems, *operands, outside=()):
+    return min(max(total, 47 * 1024 * 1024), 62 * 1024 * 1024)
+
+
+def remote_call(kernel, number, out_shapes, scratch, sems, *operands, outside=(), left=()):
     spec = pl.BlockSpec(memory_space=pltpu.VMEM)
     scalars = pl.BlockSpec(memory_space=pltpu.SMEM)
     anywhere = pl.BlockSpec(memory_space=pl.ANY)
     inside = [one for k, one in enumerate(operands) if k not in outside]
+    inside += [one for k, one in enumerate(out_shapes) if k not in left]
     return pl.pallas_call(
         kernel,
         out_shape=out_shapes,
@@ -1444,12 +1504,12 @@
             else scalars if one.dtype == jnp.int32 and one.size < LANES else spec
             for k, one in enumerate(operands)
         ],
-        out_specs=[spec] * len(out_shapes),
+        out_specs=[anywhere if k in left else spec for k in range(len(out_shapes))],
         scratch_shapes=[pltpu.VMEM(shape, dtype) for shape, dtype in scratch] + sems,
         compiler_params=pltpu.CompilerParams(
             collective_id=number, has_side_effects=True,
             vmem_limit_bytes=kernel_room(
-                [(one.shape, one.dtype) for one in inside + out_shapes] + scratch
+                [(one.shape, one.dtype) for one in inside] + scratch
             ),
         ),
     )(*operands)
@@ -1477,6 +1537,48 @@
         scratch_shapes=[pltpu.VMEM(shape, dtype) for shape, dtype in scratch],
         compiler_params=pltpu.CompilerParams(vmem_limit_bytes=56 * 1024 * 1024),
     )(*operands)
+
+
+def update_kernel(got_ref, sum_out_ref, sum_down_ref, *refs, inner, own_ff, heads):
+    groups, _, _ = got_ref.shape
+    names = 4
+    given = [refs[3 * k : 3 * k + 3] for k in range(names)]
+    made = [refs[3 * names + 4 * k : 3 * names + 4 * k + 4] for k in range(names)]
+    router_ref = refs[7 * names]
+
+    def step(which, at, gradient):
+        weight, first, second = (ref[:, at] for ref in given[which])
+        parts = adam_step(weight, first, second, gradient)[:4]
+        for ref, part in zip(made[which], parts):
+            ref[:, at] = part
+
+    def piece(place, start, size):
+        return got_ref[place, :, start : start + size].astype(f32)
+
+    body = 2 * inner + 2 * STATE
+    for place in range(groups):
+        for k in range(2):
+            start = k * INNER + place * inner
+            step(0, slice(start, start + inner), piece(place, k * inner, inner))
+    step(0, slice(2 * INNER, 2 * INNER + 2 * STATE),
+         sum(piece(place, 2 * inner, 2 * STATE) for place in range(groups)))
+    blocks = [piece(place, body, LANES) for place in range(groups)]
+    lanes = lax.broadcasted_iota(jnp.int32, blocks[0].shape, 1)
+    steps = sum(
+        pltpu.roll(jnp.where(lanes < heads, block, 0.0), place * heads, 1)
+        if place else jnp.where(lanes < heads, block, 0.0)
+        for place, block in enumerate(blocks)
+    )
+    step(0, slice(2 * INNER + 2 * STATE, 2 * INNER + 2 * STATE + groups * heads),
+         steps[:, : groups * heads])
+    router_ref[...] = pltpu.roll(sum(blocks), LANES - heads, 1)
+    step(1, slice(0, D), sum_out_ref[: given[1][0].shape[0], :])
+    step(3, slice(0, D), sum_down_ref[: given[3][0].shape[0], :])
+    start = got_ref.shape[2] - 2 * own_ff
+    for place in range(groups):
+        for k in range(2):
+            at = k * SHARED_FF + place * own_ff
+            step(2, slice(at, at + own_ff), piece(place, start + k * own_ff, own_ff))
 
 
 def on_device(
@@ -1512,26 +1614,6 @@
     conv_cols = inner + 2 * STATE
     body = 2 * inner + 2 * STATE
 
-    w_in_low = w_in.astype(bf16)
-    z_cols = w_in_low[:, :INNER].reshape(rows_in, groups, inner)
-    x_cols = w_in_low[:, INNER : 2 * INNER].reshape(rows_in, groups, inner)
-    bc_cols = jnp.broadcast_to(
-        w_in_low[:, None, 2 * INNER : 2 * INNER + 2 * STATE], (rows_in, groups, 2 * STATE)
-    )
-    dt_cols = w_in_low[:, 2 * INNER + 2 * STATE :].reshape(rows_in, groups, heads)
-    router_cols = jnp.broadcast_to(
-        w_router.astype(bf16)[:, None], (rows_in, groups, experts)
-    )
-    fill = jnp.zeros((rows_in, groups, LANES - heads - experts), bf16)
-    win_pieces = jnp.concatenate(
-        [z_cols, x_cols, bc_cols, dt_cols, router_cols, fill], axis=2
-    ).transpose(1, 0, 2)
-    sgu_pieces = (
-        w_shared_gu.astype(bf16)
-        .reshape(rows_in, 2, groups, own_ff)
-        .transpose(2, 0, 1, 3)
-        .reshape(groups, rows_in, 2 * own_ff)
-    )
     pairs = pltpu.SemaphoreType.DMA
     route_pad = jnp.pad(routes, ((0, 0), (0, LANES - top)))
     row_shape = jax.ShapeDtypeStruct((groups, tok, D), bf16)
@@ -1543,7 +1625,7 @@
     ed_held = jax.ShapeDtypeStruct((held, rows_ed, D), bf16)
     (
         x_all, cot_all, cot_came, routes_two, win, sgu, wout, sd, masks, doc_col, doc_row,
-        egu_kept, egu_sent, ed_kept, ed_sent,
+        egu_kept, egu_sent, ed_kept, ed_sent, conv_pad, head_rows, col_rows,
     ) = remote_call(
         start_kernel, 7,
         [
@@ -1551,25 +1633,31 @@
             jax.ShapeDtypeStruct((groups, tok, D), bf16),
             jax.ShapeDtypeStruct((tok, D), bf16),
             jax.ShapeDtypeStruct((2, groups, tok, LANES), jnp.int32),
-            jax.ShapeDtypeStruct((copies,) + win_pieces.shape, bf16),
-            jax.ShapeDtypeStruct((copies,) + sgu_pieces.shape, bf16),
+            jax.ShapeDtypeStruct((copies, groups, rows_in, body + LANES), bf16),
+            jax.ShapeDtypeStruct((copies, groups, rows_in, 2 * own_ff), bf16),
             jax.ShapeDtypeStruct((per_pair, groups, rows_out, D), bf16),
             jax.ShapeDtypeStruct((per_pair, groups, rows_sd, D), bf16),
             jax.ShapeDtypeStruct((length, LANES), f32),
             jax.ShapeDtypeStruct((length, 1), jnp.int32),
             jax.ShapeDtypeStruct((1, length), jnp.int32),
             gu_held, gu_held, ed_held, ed_held,
+            jax.ShapeDtypeStruct((8, conv_cols), f32),
+            jax.ShapeDtypeStruct((8, LANES), f32),
+            jax.ShapeDtypeStruct((8, inner), f32),
         ],
         [
             ((copies, rows_out, D), bf16), ((copies, rows_sd, D), bf16), ((tok, LANES), jnp.int32),
+            ((groups, rows_in, body + LANES), bf16), ((groups, rows_in, 2 * own_ff), bf16),
+            ((rows_out, D), bf16), ((rows_sd, D), bf16), ((2, max(8, rows_in), LANES), f32),
         ],
         [pairs((7 * (groups - 1),))] * 2
         + [pairs((2 * per_pair * (groups - 1),))] * 2
         + [pairs((2,))] * 2
         + [pairs((9 + 2 * per_pair,))]
         + line_sems(copies // 2) * 4,
-        lengths, tokens, cotangent, route_pad, win_pieces, sgu_pieces,
-        w_out.astype(bf16), w_shared_down.astype(bf16), w_expert_gu, w_expert_down,
+        lengths, tokens, cotangent, route_pad, w_in, w_router, w_shared_gu, w_out,
+        w_shared_down, w_expert_gu, w_expert_down, conv_params, head_params,
+        mixer_gain.reshape(1, INNER),
     )
     x_all = x_all.reshape(length, D)
     routes_two = routes_two.reshape(2 * length, LANES)
@@ -1579,25 +1667,6 @@
     sd = sd.reshape(own_ff, D)
     router = win[:, body:]
 
-
-    own_x = place * inner
-    conv_own = jnp.concatenate(
-        [
-            lax.dynamic_slice_in_dim(conv_params, own_x, inner, axis=1),
-            conv_params[:, INNER:],
-        ],
-        axis=1,
-    )
-    head_own = lax.dynamic_slice_in_dim(head_params, place * heads, heads, axis=1)
-    gain_own = lax.dynamic_slice_in_dim(mixer_gain, own_x, inner, axis=0)
-
-    conv_pad = jnp.pad(conv_own, ((0, 3), (0, 0)))
-    rate_abs = jnp.exp(head_own[0])
-    head_rows = jnp.pad(jnp.stack([rate_abs, head_own[1]]), ((0, 6), (0, LANES - heads)))
-    col_rows = jnp.pad(
-        jnp.stack([gain_own, jnp.repeat(head_own[2], HEAD_DIM)]), ((0, 6), (0, 0))
-    )
-    gain_rows = jnp.pad(norm_gains, ((0, 6), (0, 0)))
 
     square = ((length, length), f32)
     lane_rows = ((length, LANES), f32)
@@ -1621,8 +1690,8 @@
         [((length, D), bf16), square, square, lane_rows, lane_cols, ((length, inner), bf16),
          lane_rows],
         [pairs((groups,))] * 2 + spread_sems + [pairs(()), pairs((2,))],
-        x_all, win, gain_rows, conv_pad, masks, head_rows, col_rows, doc_col, doc_row, wout,
-        egu_kept, egu_sent, cot_all, cot_came, outside=(12, 13),
+        x_all, win, norm_gains, conv_pad, masks, head_rows, col_rows, doc_col, doc_row, wout,
+        egu_kept, egu_sent, cot_all, cot_came,
     )
     cot_two = cot_two.reshape(2 * length, D)
     hidden, mixer_res, two_own, ed_near, ed_came = remote_call(
@@ -1636,7 +1705,7 @@
         ],
         [((groups - 1, tok, D + LANES), bf16)],
         [pairs((groups,))] * 2 + spread_sems + [pairs(())],
-        res_part, tokens, gain_rows, ed_kept, ed_sent,
+        res_part, tokens, norm_gains, ed_kept, ed_sent,
     )
     gathered_shape = jax.ShapeDtypeStruct((groups, tok, D + LANES), bf16)
     own_rows = groups * rows_in
@@ -1747,22 +1816,23 @@
         + [
             ((planes_half - 1, held, 2, packed_rows, EXPERT_FF), bf16),
             ((planes_half, held, 2, packed_rows, EXPERT_FF), bf16),
+            ((planes_half, held, 2, packed_rows, EXPERT_FF), bf16),
         ],
         [
             pairs((3 * groups - 2,)), pairs((3 * groups - 2,)),
             pairs((held * (planes_half - 1) + 1,)), pairs((held * (planes_half - 1) + 1,)),
             pairs((held * planes_half,)), pairs((held * planes_half,)),
-            pairs(()),
+            pairs((planes_half,)), pairs(()),
         ],
-        back_parts, hidden, mixer_res, cotangent, weights_tok, router, gain_rows,
-        expert_grads.reshape((planes_half, 2) + expert_grads.shape[1:]),
+        back_parts, hidden, mixer_res, cotangent, weights_tok, router, norm_gains,
+        expert_grads.reshape((planes_half, 2) + expert_grads.shape[1:]), outside=(7,),
     )
     hidden_all = hidden_all.reshape(length, -1)
     grad_gain_two = gain_two[0]
 
     out_rows = -(-rows_out // tile) * tile
     (
-        grad_proj, conv_grads, col_grads, head_grads, expert_sum, grad_wout, out_own, out_other,
+        grad_proj, conv_grads, col_grads, head_grads, expert_sum, grad_wout, out_other,
     ) = remote_call(
         backward_kernel, 5,
         [
@@ -1772,13 +1842,12 @@
             jax.ShapeDtypeStruct((8, LANES), f32),
             jax.ShapeDtypeStruct((own_experts, packed_rows, EXPERT_FF), bf16),
             jax.ShapeDtypeStruct((copies, out_rows, D), bf16),
-            jax.ShapeDtypeStruct((tok, D), f32),
             jax.ShapeDtypeStruct((tok, D), bf16),
         ],
         [square, square, lane_rows, lane_cols, square, lane_rows, lane_cols, lane_rows, lane_rows,
          ((length, LANES), bf16), ((inner, D), bf16), ((packed_rows, EXPERT_FF), bf16),
-         ((2, groups - 1, tok, D), bf16), ((2, tok, D), bf16)],
-        [pairs(()), pairs(()), pairs((2 * groups - 2,)), pairs((2 * groups - 2,)), pairs((2,))],
+         ((groups - 1, tok, D), bf16), ((tok, D), bf16)],
+        [pairs(()), pairs(()), pairs((groups - 1,)), pairs((groups - 1,)), pairs(())],
         hidden_all, scale_words, wout, conv_pad, masks, head_rows, col_rows, doc_col, doc_row,
         packed, dt_raw, full_y, expert_sums, came_one, out_parts, outside=(14,),
     )
@@ -1790,14 +1859,14 @@
     first_shared = chunks_one + (wide_out + wide_down) // CHUNK
     shared_chunks = list(range(chunks_one)) + list(range(first_shared, chunks))
     shared_wide = len(shared_chunks) * CHUNK
-    small_wide = conv_cols + inner + LANES + 2 * D
+    small_wide = conv_cols + inner + LANES + CHUNK
     folds = own_rows // out_rows + own_rows // down_rows
     dense_sems = [pairs((chunks,))] * 2 + [pairs((2 * chunks * (planes_half - 1),))] * 2
     dense_sems += [pairs((chunks,))] * 2 + [pairs((chunks * (groups - 1),))] * 2
-    dense_sems += [pairs((groups - 1,))] * 2 + [pairs((1,))] * 2
+    dense_sems += [pairs((groups - 1,))] * 2 + [pairs((groups,))] * 2
     dense_sems += [pairs((planes_half + groups,))] * 2
     dense_sems += [pairs((per_pair * folds * (groups - 1),))] * 2
-    dense_sems += [pairs((chunks,)), pairs((per_pair * folds,)), pairs((2,))]
+    dense_sems += [pairs((chunks,)), pairs((per_pair * folds,)), pairs((3,))]
     got_rows, sum_out, sum_sd, grad_tokens, output, small = remote_call(
         functools.partial(dense_kernel, shared_chunks=shared_chunks, heads=heads), 6,
         [
@@ -1820,14 +1889,16 @@
             ((length, D), bf16),
             ((groups - 1, tok, D), bf16),
             ((tok, D), bf16),
+            ((groups - 1, tok, D), bf16),
+            ((tok, D), bf16),
             ((length, 1), f32),
             ((4, 8, small_wide), f32),
             ((planes_half + 1, 8, small_wide), f32),
         ],
         dense_sems,
-        x_all, tokens, win, gain_rows, grad_proj, two_own, grad_logits, grad_sgu, grad_wout,
-        grad_sd, grad_hidden, out_own, out_other, hidden, conv_grads, col_grads, head_grads, gain_two,
-        outside=(7, 8, 9),
+        x_all, tokens, win, norm_gains, grad_proj, two_own, grad_logits, grad_sgu, grad_wout,
+        grad_sd, grad_hidden, out_parts, out_other, hidden, conv_grads, col_grads, head_grads, gain_two,
+        outside=(7, 8, 9, 11),
     )
     sum_egu = jnp.concatenate(
         [expert_sum[:, :rows_egu], expert_sum[:, rows_egu : 2 * rows_egu]], axis=2
@@ -1857,35 +1928,33 @@
         [small[:, k, start : start + heads].reshape(HEADS) for k in range(2)] + [sum_skip]
     )
     start = start + LANES
-    gain_sums = jnp.sum(small[:, 0, start:], axis=0)
-    sum_gains = jnp.stack([gain_sums[D:], gain_sums[:D]])
-
-    def laid(source, start, size):
-        return source[:, :, start : start + size].transpose(1, 0, 2).reshape(rows_in, -1)
-
-    win_got = got_rows.astype(f32)
-    sum_in = jnp.concatenate(
-        [
-            laid(win_got, 0, inner),
-            laid(win_got, inner, inner),
-            jnp.sum(win_got[:, :, 2 * inner : body], axis=0),
-            laid(win_got, body, heads),
-        ],
-        axis=1,
-    )
-    sum_router = jnp.sum(win_got[:, :, body + heads : body + heads + experts], axis=0)
-    start = body + LANES + (wide_out + wide_down) % CHUNK
-    sum_sgu = (
-        win_got[:, :, start : start + 2 * own_ff]
-        .reshape(groups, rows_in, 2, own_ff)
-        .transpose(1, 2, 0, 3)
-        .reshape(rows_in, 2 * SHARED_FF)
-    )
-    sum_out = sum_out[:rows_out]
-    sum_sd = sum_sd[:rows_sd]
-    up_out = adam_step(w_out, w_out_first, w_out_second, sum_out)
-    up_sgu = adam_step(w_shared_gu, w_shared_gu_first, w_shared_gu_second, sum_sgu)
-    up_sd = adam_step(w_shared_down, w_shared_down_first, w_shared_down_second, sum_sd)
+    gain_sums = jnp.sum(small[:, :, start:], axis=0)
+    sum_gains = jnp.stack(
+        [gain_sums[D // CHUNK :].reshape(D), gain_sums[: D // CHUNK].reshape(D)]
+    )
+
+    given = (
+        (w_in, w_in_first, w_in_second),
+        (w_out, w_out_first, w_out_second),
+        (w_shared_gu, w_shared_gu_first, w_shared_gu_second),
+        (w_shared_down, w_shared_down_first, w_shared_down_second),
+    )
+    updated = vmem_call(
+        functools.partial(
+            update_kernel, inner=inner, own_ff=own_ff, heads=heads
+        ),
+        [jax.ShapeDtypeStruct(one[0].shape, f32) for one in given for _ in range(4)]
+        + [jax.ShapeDtypeStruct((rows_in, LANES), f32)],
+        [],
+        got_rows, sum_out, sum_sd, *[part for one in given for part in one],
+    )
+    up_in, up_out, up_sgu, up_sd = (updated[4 * k : 4 * k + 4] for k in range(4))
+    up_router = tuple(
+        part.T
+        for part in adam_step(
+            w_router.T, w_router_first.T, w_router_second.T, updated[16].T[:experts]
+        )
+    )
     up_egu = adam_step(w_expert_gu, w_expert_gu_first, w_expert_gu_second, sum_egu)
     up_ed = adam_step(w_expert_down, w_expert_down_first, w_expert_down_second, sum_ed)
     up_gains = adam_step(norm_gains, norm_gains_first, norm_gains_second, sum_gains)
@@ -1893,13 +1962,11 @@
     up_head = adam_step(head_params, head_params_first, head_params_second, sum_head)
     up_mixer = adam_step(mixer_gain, mixer_gain_first, mixer_gain_second, sum_mixer)
 
-    up_in = adam_step(w_in, w_in_first, w_in_second, sum_in)
-    up_router = adam_step(w_router, w_router_first, w_router_second, sum_router)
     large = (up_in, up_out, up_router, up_sgu, up_sd, up_egu, up_ed)
     little = (up_gains, up_conv, up_head, up_mixer)
     return (
         (output, grad_tokens)
-        + tuple(part for one in large for part in one[:4])
+        + tuple(part for one in large for part in tuple(one)[:4])
         + tuple(part for one in little for part in (one[0], one[4], one[2], one[3]))
     )
 

time: 638 us -> 598 us (0.937)
  Pallas kernels: 562 us -> 543 us
  other arithmetic: 27.9 us -> 15.7 us
  local copies, waits for them, and re-layouts: 36.8 us -> 28.4 us
    pallas_call x7, Pallas kernels: 514 us -> 486 us  [remote_call(): pl.pallas_call(kernel, out_shape=out_shapes, in_specs=[anywhere if k in o...]
    unnamed x101 -> x91, local copies, waits for them, and re-layouts: 11.3 us -> 23 us
    pallas_call x0 -> x1, Pallas kernels: none -> 8.92 us  [vmem_call(): pl.pallas_call(kernel, out_shape=out_shapes, in_specs=[spec] * len(operan...]
    add x7 -> x2, other arithmetic: 16.5 us -> 12.2 us  [adam_step(): return (gradient, weight + moved, moment_one, moment_two, moved)]
where the time goes in v4:
time: 598 us; the launch traced here: 589 us
  Pallas kernels  543 us (91%)
  local copies, waits for them, and re-layouts  28.4 us (5%)
  other arithmetic  15.7 us (3%)
    pallas_call x7, Pallas kernels, remote_call(): pl.pallas_call(kernel, out_shape=out_shapes, in_specs=[anywhere if k in o...  486 us
    pallas_call x3, Pallas kernels, grid_call(): pl.pallas_call(kernel, grid=(steps,), out_shape=out_shapes, in_specs=in_s...  48.1 us
    unnamed x91, local copies, waits for them, and re-layouts  23 us
    add x2, other arithmetic, adam_step(): return (gradient, weight + moved, moment_one, moment_two, moved)  12.2 us

profile of v4, /device:TPU:0, one launch (start us, length us, event | category | flops | bytes accessed | tf_op | source)
XLA Modules:
  0.0 589.0 jit_solution(4763887527433650063)
XLA Ops:
  0.7 0.8 copy.102.w_router_ref
  1.5 0.8 copy.104
  2.3 0.8 copy.106
  3.0 0.8 copy.101
  3.8 1.0 copy-done.1
  4.8 1.1 copy-done.5
  5.9 1.0 copy-done.8
  6.9 1.0 copy-done.10
  7.9 0.9 copy-done.15
  8.8 0.9 copy-done.18
  9.7 0.7 copy-done.22
  10.4 0.7 copy-done.24
  11.1 0.7 copy-done.26
  11.8 112.6 %shard_map.708 = (bf16[4,128,1536]{2,1,0:T(8,128)(2,1)}, bf16[4,128,1536]{2,1,0:T(8,128)(2,1)}, bf16[128,1536]{1,0:T(8,128)(2,1)S(1)}, s32[2,4,128,128]{3,2,1,0:...) custom-call(s32[1,3]{1,0:T(1,128)S(1)} %copy-done.26, ...), custom_call_target="tpu_custom_call" | custom-call | tf_op jit(solution)/shard_map/pallas_call | solution.py:1499
  124.4 2.0 slice.68.router_ref
  126.4 1.4 copy-done
  127.8 45.9 %shard_map.709 = (bf16[512,1792]{1,0:T(8,128)(2,1)}, f32[512,128]{1,0:T(8,128)S(1)}, bf16[512,768]{1,0:T(8,128)(2,1)S(1)}, bf16[512,1664]{1,0:T(8,128)(2,1)}, bf...) custom-call(bf16[512,1536]{1,0:T(8,128)(2,1)S(1)} %bitcast.59, ...), custom_call_target="tpu_custom_call" | custom-call | tf_op jit(solution)/shard_map/pallas_call | solution.py:1499
  173.7 1.4 copy-done.7
  175.1 27.9 %shard_map.710 = (f32[128,1536]{1,0:T(8,128)S(1)}, f32[128,1536]{1,0:T(8,128)S(1)}, bf16[128,1664]{1,0:T(8,128)(2,1)S(1)}, bf16[4,2,64,1536]{3,2,1,0:T(8,128)(2,1)S(1)}, bf16[2,64,1536]{2,1,0:T(8,128)(2,1)S(1)}) custom-call(bf16[512,1664]{1,0:T(8,128)(2,1)S(1)} %copy-done.7, bf16[128,1536]{1,0:T(8,128)(2,1)S(1)} %copy-done.2, f32[2,1536]{1,0:T(2,128)S(1)} %copy-done.20, ...), custom_call_target="tpu_custom_call" | custom-call | tf_op jit(solution)/shard_map/pallas_call | solution.py:1499
  203.0 50.4 %shard_map.711 = (bf16[2,4,128,1664]{3,2,1,0:T(8,128)(2,1)}, bf16[4,2,192,1024]{3,2,1,0:T(8,128)(2,1)}, bf16[4,2,64,1536]{3,2,1,0:T(8,128)(2,1)S(1)}, bf16[512,1...) custom-call(bf16[128,1664]{1,0:T(8,128)(2,1)S(1)} %get-tuple-element, ...), custom_call_target="tpu_custom_call" | custom-call | tf_op jit(solution)/shard_map/pallas_call | solution.py:1499
  253.5 1.1 copy-done.11
  254.6 1.1 copy-done.13
  255.8 0.9 slice.52
  256.7 12.9 %shard_map.712 = (bf16[2,512,1536]{2,1,0:T(8,128)(2,1)}, bf16[2,512,1536]{2,1,0:T(8,128)(2,1)}, bf16[2,512,1536]{2,1,0:T(8,128)(2,1)}, f32[1024,128]{1,0:T(8,128)}, bf16[8,128,128]{2,1,0:T(8,128)(2,1)}) custom-call(bf16[1024,1664]{1,0:T(8,128)(2,1)} %bitcast.73, bf16[1024,1536]{1,0:T(8,128)(2,1)} %bitcast.69, s32[1024,128]{1,0:T(8,128)} %bitcast.63, ...), custom_call_target="tpu_custom_call" | custom-call | tf_op jit(solution)/shard_map/pallas_call | solution.py:1531
  269.6 0.8 constant_dynamic-slice_fusion.weights_ref
  270.4 24.4 %shard_map.713 = (bf16[2,512,1536]{2,1,0:T(8,128)(2,1)}, bf16[2,512,1536]{2,1,0:T(8,128)(2,1)}, f32[2,512,128]{2,1,0:T(8,128)}, bf16[4,2,2,576,512]{4,3,2,1,0:T(8,128)(2,1)}) custom-call(bf16[2,512,1536]{2,1,0:T(8,128)(2,1)} %get-tuple-element.156.in_ref, bf16[2,512,1536]{2,1,0:T(8,128)(2,1)} %get-tuple-element.157.top_ref, ...), custom_call_target="tpu_custom_call" | custom-call | tf_op jit(solution)/shard_map/pallas_call | solution.py:1531
  294.8 0.0 copy-start.9
  294.8 10.8 %shard_map.714 = (bf16[1024,1536]{1,0:T(8,128)(2,1)}, bf16[1024,1664]{1,0:T(8,128)(2,1)}) custom-call(bf16[8,128,128]{2,1,0:T(8,128)(2,1)} %get-tuple-element.154.pick_ref, f32[1024,128]{1,0:T(8,128)} %get-tuple-element.155.weights_ref, s32[1]{0:T(128)} %bitcast.9.ids_ref, bf16[2,512,1536]{2,1,0:T(8,128)(2,1)} %get-tuple-element.163.out_ref, ...), custom_call_target="tpu_custom_call" | custom-call | tf_op jit(solution)/shard_map/pallas_call | solution.py:1531
  305.7 84.9 %shard_map.715 = (bf16[4,128,1664]{2,1,0:T(8,128)(2,1)S(1)}, f32[128,1536]{1,0:T(8,128)S(1)}, bf16[128,128]{1,0:T(8,128)(2,1)S(1)}, f32[8,1536]{1,0:T(8,128)S(1)...) custom-call(bf16[1024,1664]{1,0:T(8,128)(2,1)} %get-tuple-element.168.back_ref, ...), custom_call_target="tpu_custom_call" | custom-call | tf_op jit(solution)/shard_map/pallas_call | solution.py:1499
  390.5 0.0 copy-start.14
  390.6 41.4 %shard_map.716 = (bf16[512,1920]{1,0:T(8,128)(2,1)}, f32[8,1024]{1,0:T(8,128)S(1)}, f32[8,768]{1,0:T(8,128)S(1)}, f32[8,128]{1,0:T(8,128)S(1)}, bf16[4,576,512]{...) custom-call(bf16[512,1664]{1,0:T(8,128)(2,1)S(1)} %bitcast.60, ...), custom_call_target="tpu_custom_call" | custom-call | tf_op jit(solution)/shard_map/pallas_call | solution.py:1499
  431.9 0.0 copy-start.25
  432.0 0.0 copy-start.33
  432.0 0.0 copy-start.34
  432.0 0.0 copy-start.36
  432.0 0.0 copy-start.19
  432.1 123.3 %shard_map.717 = (bf16[4,48,2688]{2,1,0:T(8,128)(2,1)}, f32[96,1536]{1,0:T(8,128)S(1)}, f32[32,1536]{1,0:T(8,128)S(1)}, bf16[128,1536]{1,0:T(8,128)(2,1)S(1)}, b...) custom-call(bf16[512,1536]{1,0:T(8,128)(2,1)} %bitcast.58, bf16[128,1536]{1,0:T(8,128)(2,1)S(1)} %copy-done.2, ...), custom_call_target="tpu_custom_call" | custom-call | tf_op jit(solution)/shard_map/pallas_call | solution.py:1499
  555.3 0.0 copy-start.16
  555.3 0.8 copy-done.16
  556.2 0.1 stack_reshape_squeeze.6
  556.3 0.1 stack_reshape_squeeze.7
  556.5 0.0 copy-start.32
  556.5 0.1 reshape_squeeze.10
  556.6 0.1 reduce_sum.29
  556.7 0.1 stack_reshape.11
  556.8 0.6 add_multiply_fusion.3
  557.4 0.7 add_multiply_fusion.2
  558.1 0.6 add_multiply_fusion.1
  558.7 0.8 add_multiply_fusion
  559.5 1.2 fusion.18
  560.7 0.0 copy-start.27
  560.7 0.2 fusion.19
  560.9 1.2 copy-done.27
  562.1 0.5 copy-done.29
  562.6 4.6 multiply_add_fusion.2
  567.2 8.9 %shard_map.718 = (f32[48,6448]{1,0:T(8,128)}, f32[48,6448]{1,0:T(8,128)}, f32[48,6448]{1,0:T(8,128)}, f32[48,6448]{1,0:T(8,128)}, f32[96,1536]{1,0:T(8,128)}, /*...) custom-call(bf16[4,48,2688]{2,1,0:T(8,128)(2,1)} %get-tuple-element., ...), custom_call_target="tpu_custom_call" | custom-call | tf_op jit(solution)/shard_map/pallas_call | solution.py:1520
  576.1 0.8 fusion.10
  576.9 0.7 copy.111
  577.5 0.7 copy.109
  578.2 0.7 copy.110
  578.9 0.7 copy.108
  579.5 7.6 %multiply_add_fusion = (f32[4,192,1024]{2,1,0:T(8,128)}, f32[4,192,1024]{2,1,0:T(8,128)}, f32[4,192,1024]{2,1,0:T(8,128)}, f32[4,192,1024]{2,1,0:T(8,128)}) fusion(f32[4,192,1024]{2,1,0:T(8,128)} %gu_ref.1, f32[4,192,1024]{2,1,0:T(8,128)} %param.57, f32[4,192,1024]{2,1,0:T(8,128)} %param.58, bf16[4,192,512]{2,1,0:T(8,128)(2,1)S(1)} %get-tuple-element.381, ...), kind=kLoop, calls=%fused_computation.2 | loop fusion | flops 14942208 | bytes 23592960 | tf_op jit(solution)/shard_map/add | solution.py:89
  587.1 0.7 copy.116
  587.9 0.7 copy.117
  (61 shorter events, 0.2 us)
Async XLA Ops:
  3.8 1.0 copy-start.1
  4.8 1.1 copy-start.5
  5.9 1.0 copy-start.8
  6.9 1.0 copy-start.10
  7.9 0.9 copy-start.15
  8.8 0.9 copy-start.18
  9.7 0.7 copy-start.22
  10.4 0.7 copy-start.24
  11.1 0.7 copy-start.26
  11.8 114.6 %copy-start.20 = (f32[2,1536]{1,0:T(2,128)S(1)}, f32[2,1536]{1,0:T(2,128)}, u32[]{:S(2)}) copy-start(f32[2,1536]{1,0:T(2,128)} %gain_ref.7) | copy-start | bytes 36868
  124.4 49.3 %copy-start.17 = (s32[2,4,128,128]{3,2,1,0:T(8,128)}, s32[2,4,128,128]{3,2,1,0:T(8,128)S(1)}, u32[]{:S(2)}) copy-start(s32[2,4,128,128]{3,2,1,0:T(8,128)S(1)} %get-tuple-element.153) | copy-start | bytes 1572868
  126.4 1.4 copy-start
  127.8 45.9 %copy-start.2 = (bf16[128,1536]{1,0:T(8,128)(2,1)S(1)}, bf16[128,1536]{1,0:T(8,128)(2,1)}, u32[]{:S(2)}) copy-start(bf16[128,1536]{1,0:T(8,128)(2,1)} %tokens_ref.3) | copy-start | bytes 1179652
  173.7 1.5 copy-start.7
  203.0 50.4 %copy-start.12 = (bf16[4,2,64,1536]{3,2,1,0:T(8,128)(2,1)}, bf16[4,2,64,1536]{3,2,1,0:T(8,128)(2,1)S(1)}, u32[]{:S(2)}) copy-start(bf16[4,2,64,1536]{3,2,1,0:T(8,128)(2,1)S(1)} %get-tuple-element.161.down_near_ref) | copy-start | bytes 4718596
  203.0 102.6 %copy-start.4 = (f32[128,1536]{1,0:T(8,128)}, f32[128,1536]{1,0:T(8,128)S(1)}, u32[]{:S(2)}) copy-start(f32[128,1536]{1,0:T(8,128)S(1)} %get-tuple-element.169.hidden_ref) | copy-start | bytes 2359300
  253.5 1.1 copy-start.11
  254.6 1.1 copy-start.13
  294.8 10.8 %copy-start.3 = (bf16[1536,128]{1,0:T(8,128)(2,1)S(1)}, bf16[1536,128]{1,0:T(8,128)(2,1)}, u32[]{:S(2)}) copy-start(bf16[1536,128]{1,0:T(8,128)(2,1)} %slice.68.router_ref) | copy-start | bytes 1179652
  294.8 10.8 %copy-start.9 = (bf16[128,1536]{1,0:T(8,128)(2,1)S(1)}, bf16[128,1536]{1,0:T(8,128)(2,1)}, u32[]{:S(2)}) copy-start(bf16[128,1536]{1,0:T(8,128)(2,1)} %cot_ref.3) | copy-start | bytes 1179652
  305.6 84.9 %copy-start.6 = (bf16[512,1792]{1,0:T(8,128)(2,1)S(1)}, bf16[512,1792]{1,0:T(8,128)(2,1)}, u32[]{:S(2)}) copy-start(bf16[512,1792]{1,0:T(8,128)(2,1)} %get-tuple-element.173.packed_ref) | copy-start | bytes 5505028
  390.5 41.4 %copy-start.14 = (f32[128,1536]{1,0:T(8,128)}, f32[128,1536]{1,0:T(8,128)S(1)}, u32[]{:S(2)}) copy-start(f32[128,1536]{1,0:T(8,128)S(1)} %get-tuple-element.184.grad_hidden_ref) | copy-start | bytes 2359300
  431.9 124.8 %copy-start.25 = (f32[3,48]{1,0:T(4,128)S(1)}, f32[3,48]{1,0:T(4,128)}, u32[]{:S(2)}) copy-start(f32[3,48]{1,0:T(4,128)} %head_ref.1) | copy-start | bytes 1732
  431.9 124.8 %copy-start.37 = (f32[3,48]{1,0:T(4,128)S(1)}, f32[3,48]{1,0:T(4,128)}, u32[]{:S(2)}) copy-start(f32[3,48]{1,0:T(4,128)} %param.69) | copy-start | bytes 1732
  432.0 124.8 %copy-start.38 = (f32[3,48]{1,0:T(4,128)S(1)}, f32[3,48]{1,0:T(4,128)}, u32[]{:S(2)}) copy-start(f32[3,48]{1,0:T(4,128)} %param.70) | copy-start | bytes 1732
  432.0 125.4 %copy-start.33 = (f32[2,1536]{1,0:T(2,128)S(1)}, f32[2,1536]{1,0:T(2,128)}, u32[]{:S(2)}) copy-start(f32[2,1536]{1,0:T(2,128)} %param.63) | copy-start | bytes 36868
  432.0 125.4 %copy-start.34 = (f32[2,1536]{1,0:T(2,128)S(1)}, f32[2,1536]{1,0:T(2,128)}, u32[]{:S(2)}) copy-start(f32[2,1536]{1,0:T(2,128)} %param.64) | copy-start | bytes 36868
  432.0 126.1 %copy-start.23 = (f32[3072]{0:T(1024)S(1)}, f32[3072]{0:T(1024)}, u32[]{:S(2)}) copy-start(f32[3072]{0:T(1024)} %param.71) | copy-start | bytes 36868
  432.0 126.1 %copy-start.35 = (f32[3072]{0:T(1024)S(1)}, f32[3072]{0:T(1024)}, u32[]{:S(2)}) copy-start(f32[3072]{0:T(1024)} %param.72) | copy-start | bytes 36868
  432.0 126.1 %copy-start.36 = (f32[3072]{0:T(1024)S(1)}, f32[3072]{0:T(1024)}, u32[]{:S(2)}) copy-start(f32[3072]{0:T(1024)} %param.73) | copy-start | bytes 36868
  432.0 126.7 %copy-start.19 = (f32[5,3328]{1,0:T(8,128)S(1)}, f32[5,3328]{1,0:T(8,128)}, u32[]{:S(2)}) copy-start(f32[5,3328]{1,0:T(8,128)} %conv_ref.1) | copy-start | bytes 199684
  432.0 126.7 %copy-start.30 = (f32[5,3328]{1,0:T(8,128)S(1)}, f32[5,3328]{1,0:T(8,128)}, u32[]{:S(2)}) copy-start(f32[5,3328]{1,0:T(8,128)} %param.66) | copy-start | bytes 199684
  432.0 126.7 %copy-start.31 = (f32[5,3328]{1,0:T(8,128)S(1)}, f32[5,3328]{1,0:T(8,128)}, u32[]{:S(2)}) copy-start(f32[5,3328]{1,0:T(8,128)} %param.67) | copy-start | bytes 199684
  555.3 0.8 copy-start.16
  556.2 4.7 copy-start.21
  556.5 4.4 copy-start.32
  556.8 3.9 copy-start.28
  560.7 1.4 copy-start.27
  560.7 1.9 copy-start.29

commit v5 on v4

--- a/solution.py
+++ b/solution.py
@@ -281,12 +281,20 @@
 
 def backward_kernel(hid_ref, scale_ref, wout_ref, conv_ref, masks_ref, head_ref, cols_ref,
                     doc_col_ref, doc_row_ref, packed_ref, dt_ref, y_ref, sums_ref, came_one_ref, out_ref,
+                    sgu_ref,
                     proj_ref, conv_grad_ref, cols_grad_ref, head_grad_ref, total_ref, wout_send_ref,
-                    out_send_ref,
+                    out_send_ref, sgu_got_ref,
                     neg_ref, scores_ref, cum_ref, cum_t_ref, grad_scores_ref, row_ref, col_ref,
-                    step_ref, scaled_ref, low_ref, wout_grad_ref, theirs_ref, out_got_ref, out_mine_ref, send_sem, recv_sem, out_send, out_recv,
-                    out_local):
-    greet(group_ids() + [partner_id()])
+                    step_ref, scaled_ref, low_ref, wout_grad_ref, theirs_ref, out_got_ref, out_mine_ref, sgu_core_ref, sgu_mine_ref,
+                    sgu_slots_ref, sgu_plane_ref, sgu_came_ref, sgu_send_ref, send_sem, recv_sem,
+                    out_send, out_recv, out_local, sgu_send_sems, sgu_recv_sems, sgu_local_sems):
+    greet(group_ids() + near_ids())
+    core, zlo = lax.axis_index("core"), lax.axis_index("zlo")
+    sgu_sems = (sgu_send_sems, sgu_recv_sems)
+    sgu_core = remote(sgu_ref.at[:, 1 - core], sgu_core_ref, sgu_sems, 0, core_id())
+    sgu_mine = pltpu.make_async_copy(sgu_ref.at[:, core], sgu_mine_ref, sgu_local_sems.at[0])
+    sgu_core.start()
+    sgu_mine.start()
     tok = out_send_ref.shape[0]
     count = lax.axis_size("expert")
     out_sems = (out_send, out_recv)
@@ -315,6 +323,23 @@
         act = (gated * scale_mix * cols_ref[0:1, at]).astype(bf16)
         wout_grad_ref[at, :] = dot_tn(act, hid_ref[:, :D]).astype(bf16)
 
+    sgu_mine.wait()
+    sgu_core.wait()
+    mates = mate_ids()
+    planes = len(mates) + 1
+    for k in range(2 * planes):
+        sgu_core_ref[k] = (sgu_core_ref[k].astype(f32) + sgu_mine_ref[k].astype(f32)).astype(bf16)
+    sgu_planes = [
+        remote(
+            sgu_core_ref.at[pl.ds(h * planes + mate, 1)], sgu_slots_ref.at[number, pl.ds(h, 1)],
+            sgu_sems, 1 + 2 * number + h, {"zlo": mate},
+        )
+        for number, mate in enumerate(mates)
+        for h in range(2)
+    ]
+    for copy in sgu_planes:
+        copy.start()
+
     owners, rows_out, _ = wout_send_ref.shape
     real = inner // owners
     for k in range(owners):
@@ -340,8 +365,22 @@
     lanes_all = lax.broadcasted_iota(jnp.int32, (length, LANES), 1)
     lanes = lax.broadcasted_iota(jnp.int32, (LANES, LANES), 1)
 
+    base = 1 + 2 * len(mates)
+    sgu_half = remote(sgu_plane_ref.at[1 - half], sgu_came_ref, sgu_sems, base, partner_id())
+
+    def sgu_middle():
+        for copy in sgu_planes:
+            copy.wait()
+        for h in range(2):
+            total = sgu_core_ref[h * planes + zlo].astype(f32)
+            for number in range(len(mates)):
+                total = total + sgu_slots_ref[number, h].astype(f32)
+            sgu_plane_ref[h] = total.astype(bf16)
+        sgu_half.start()
+
     @pl.loop(0, inner // LANES)
     def _(pair):
+        pl.when(pair == inner // LANES // 2)(sgu_middle)
         at, x_at = pair_slices(pair, inner)
         grad_act = dot_nt(hid_ref[:, :D], wout_ref[at, :])
         conv_in = packed_ref[:, x_at].astype(f32)
@@ -397,6 +436,24 @@
         for k in range(CONV + 1):
             conv_grad_ref[k : k + 1, at] = taps[k]
 
+    sgu_half.wait()
+    low = (sgu_plane_ref[half].astype(f32) + sgu_came_ref[...].astype(f32)).astype(bf16)
+    rows_in = sgu_send_ref.shape[1]
+    for place in range(count):
+        sgu_send_ref[place] = low[place * rows_in : (place + 1) * rows_in]
+    me = lax.axis_index("expert")
+    sgu_rows = [
+        remote(
+            sgu_send_ref.at[other], sgu_got_ref.at[me], sgu_sems, base + 1 + number,
+            {"expert": other},
+        )
+        for number, other in enumerate(peers()[2])
+    ]
+    sgu_rows.append(
+        pltpu.make_async_copy(sgu_send_ref.at[me], sgu_got_ref.at[me], sgu_local_sems.at[1])
+    )
+    for copy in sgu_rows:
+        copy.start()
     grad_scores = grad_scores_ref[...].astype(bf16)
     for number, (grad, before) in enumerate(
         ((dot_tn(grad_scores, c_low), b_out), (dot(grad_scores, b_low), c_out))
@@ -416,7 +473,7 @@
     head_grad_ref[0:1] = jnp.sum(grad_decay * log_decay, axis=0, keepdims=True)
     head_grad_ref[1:2] = jnp.sum(grad_pre, axis=0, keepdims=True)
     proj_ref[:, body:] = grad_pre.astype(bf16)
-    for copy in out_copies:
+    for copy in out_copies + sgu_rows:
         copy.wait()
     total = out_mine_ref[...].astype(f32)
     for number in range(count - 1):
@@ -1174,7 +1231,7 @@
     across.wait()
 
 
-def dense_kernel(x_ref, tokens_ref, win_ref, gain_ref, proj_ref, two_ref, logits_ref, sgu_ref,
+def dense_kernel(x_ref, tokens_ref, win_ref, gain_ref, proj_ref, two_ref, logits_ref,
                  wout_ref, down_ref, grad_hidden_ref, out_ref, out_send_ref, hidden_ref,
                  conv_ref, cols_ref,
                  head_ref, gain_two_ref,
@@ -1205,11 +1262,11 @@
 
     wide_out = D * wout_ref.shape[1] // own_rows
     wide_down = D * down_ref.shape[1] // own_rows
-    start = wide_out + wide_down
-    beside = pltpu.make_async_copy(
-        sgu_ref, second_ref.at[:, :, :, start : start + sgu_ref.shape[3]], own_sems.at[0]
-    )
-    beside.start()
+    filled = wide_out + wide_down
+    if filled < second_ref.shape[3]:
+        second_ref[:, :, :, filled:] = jnp.zeros(
+            second_ref.shape[:3] + (second_ref.shape[3] - filled,), bf16
+        )
     each = wout_ref.shape[0] // count
     fold_copies = []
     number = 0
@@ -1325,10 +1382,8 @@
                 fold * rows : (fold + 1) * rows
             ]
 
-    alone = [chunk for chunk in range(chunks_one, chunks)
-             if (chunk - chunks_one) * CHUNK >= wide_out + wide_down]
-    mixed = [chunk for chunk in range(chunks_one, chunks) if chunk not in alone]
-    order = alone + list(range(chunks_one)) + mixed
+    mixed = list(range(chunks_one, chunks))
+    order = list(range(chunks_one)) + mixed
     ready = set()
 
     @pl.loop(0, length // LANES)
@@ -1350,14 +1405,10 @@
         if chunk in ready:
             return
         ready.add(chunk)
-        if chunk in alone:
-            beside.wait()
-        elif chunk in mixed:
+        if chunk in mixed:
             if not any(one in ready for one in mixed if one != chunk):
                 for copy in fold_copies:
                     copy.wait()
-                if not alone:
-                    beside.wait()
             for one in mixed:
                 ready.add(one)
                 send_core(one)
@@ -1539,7 +1590,7 @@
     )(*operands)
 
 
-def update_kernel(got_ref, sum_out_ref, sum_down_ref, *refs, inner, own_ff, heads):
+def update_kernel(got_ref, got_sgu_ref, sum_out_ref, sum_down_ref, *refs, inner, own_ff, heads):
     groups, _, _ = got_ref.shape
     names = 4
     given = [refs[3 * k : 3 * k + 3] for k in range(names)]
@@ -1574,11 +1625,11 @@
     router_ref[...] = pltpu.roll(sum(blocks), LANES - heads, 1)
     step(1, slice(0, D), sum_out_ref[: given[1][0].shape[0], :])
     step(3, slice(0, D), sum_down_ref[: given[3][0].shape[0], :])
-    start = got_ref.shape[2] - 2 * own_ff
     for place in range(groups):
         for k in range(2):
             at = k * SHARED_FF + place * own_ff
-            step(2, slice(at, at + own_ff), piece(place, start + k * own_ff, own_ff))
+            columns = slice(k * own_ff, (k + 1) * own_ff)
+            step(2, slice(at, at + own_ff), got_sgu_ref[place, :, columns].astype(f32))
 
 
 def on_device(
@@ -1833,6 +1884,7 @@
     out_rows = -(-rows_out // tile) * tile
     (
         grad_proj, conv_grads, col_grads, head_grads, expert_sum, grad_wout, out_other,
+        got_sgu,
     ) = remote_call(
         backward_kernel, 5,
         [
@@ -1843,21 +1895,27 @@
             jax.ShapeDtypeStruct((own_experts, packed_rows, EXPERT_FF), bf16),
             jax.ShapeDtypeStruct((copies, out_rows, D), bf16),
             jax.ShapeDtypeStruct((tok, D), bf16),
+            jax.ShapeDtypeStruct((groups, rows_in, 2 * own_ff), bf16),
         ],
         [square, square, lane_rows, lane_cols, square, lane_rows, lane_cols, lane_rows, lane_rows,
          ((length, LANES), bf16), ((inner, D), bf16), ((packed_rows, EXPERT_FF), bf16),
-         ((groups - 1, tok, D), bf16), ((tok, D), bf16)],
-        [pairs(()), pairs(()), pairs((groups - 1,)), pairs((groups - 1,)), pairs(())],
+         ((groups - 1, tok, D), bf16), ((tok, D), bf16),
+         ((copies // 2, own_rows, 2 * own_ff), bf16), ((copies // 2, own_rows, 2 * own_ff), bf16),
+         ((planes_half - 1, 2, own_rows, 2 * own_ff), bf16), ((2, own_rows, 2 * own_ff), bf16),
+         ((own_rows, 2 * own_ff), bf16), ((groups, rows_in, 2 * own_ff), bf16)],
+        [pairs(()), pairs(()), pairs((groups - 1,)), pairs((groups - 1,)), pairs(())]
+        + [pairs((2 * planes_half + groups - 1,))] * 2
+        + [pairs((2,))],
         hidden_all, scale_words, wout, conv_pad, masks, head_rows, col_rows, doc_col, doc_row,
-        packed, dt_raw, full_y, expert_sums, came_one, out_parts, outside=(14,),
+        packed, dt_raw, full_y, expert_sums, came_one, out_parts, grad_sgu,
+        outside=(14, 15),
     )
     wide_out = D * out_rows // own_rows
     wide_down = D * down_rows // own_rows
     chunks_one = (body + LANES) // CHUNK
-    chunks_two = -(-(wide_out + wide_down + 2 * own_ff) // CHUNK)
+    chunks_two = -(-(wide_out + wide_down) // CHUNK)
     chunks = chunks_one + chunks_two
-    first_shared = chunks_one + (wide_out + wide_down) // CHUNK
-    shared_chunks = list(range(chunks_one)) + list(range(first_shared, chunks))
+    shared_chunks = list(range(chunks_one))
     shared_wide = len(shared_chunks) * CHUNK
     small_wide = conv_cols + inner + LANES + CHUNK
     folds = own_rows // out_rows + own_rows // down_rows
@@ -1896,9 +1954,9 @@
             ((planes_half + 1, 8, small_wide), f32),
         ],
         dense_sems,
-        x_all, tokens, win, norm_gains, grad_proj, two_own, grad_logits, grad_sgu, grad_wout,
+        x_all, tokens, win, norm_gains, grad_proj, two_own, grad_logits, grad_wout,
         grad_sd, grad_hidden, out_parts, out_other, hidden, conv_grads, col_grads, head_grads, gain_two,
-        outside=(7, 8, 9, 11),
+        outside=(7, 8, 10),
     )
     sum_egu = jnp.concatenate(
         [expert_sum[:, :rows_egu], expert_sum[:, rows_egu : 2 * rows_egu]], axis=2
@@ -1946,7 +2004,7 @@
         [jax.ShapeDtypeStruct(one[0].shape, f32) for one in given for _ in range(4)]
         + [jax.ShapeDtypeStruct((rows_in, LANES), f32)],
         [],
-        got_rows, sum_out, sum_sd, *[part for one in given for part in one],
+        got_rows, got_sgu, sum_out, sum_sd, *[part for one in given for part in one],
     )
     up_in, up_out, up_sgu, up_sd = (updated[4 * k : 4 * k + 4] for k in range(4))
     up_router = tuple(

time: 598 us -> 592 us (0.990)
  Pallas kernels: 543 us -> 535 us
    pallas_call x7, Pallas kernels: 486 us -> 478 us  [remote_call(): pl.pallas_call(kernel, out_shape=out_shapes, in_specs=[anywhere if k in o...]
where the time goes in v5:
time: 592 us; the launch traced here: 583 us
  Pallas kernels  535 us (90%)
  local copies, waits for them, and re-layouts  31.1 us (5%)
  other arithmetic  15.7 us (3%)
    pallas_call x7, Pallas kernels, remote_call(): pl.pallas_call(kernel, out_shape=out_shapes, in_specs=[anywhere if k in o...  478 us
    pallas_call x3, Pallas kernels, grid_call(): pl.pallas_call(kernel, grid=(steps,), out_shape=out_shapes, in_specs=in_s...  48.3 us
    unnamed x91, local copies, waits for them, and re-layouts  25.6 us
    add x2, other arithmetic, adam_step(): return (gradient, weight + moved, moment_one, moment_two, moved)  12.2 us

profile of v5, /device:TPU:0, one launch (start us, length us, event | category | flops | bytes accessed | tf_op | source)
XLA Modules:
  0.0 583.5 jit_solution(6439490950911467296)
XLA Ops:
  0.7 0.8 copy.102.w_router_ref
  1.5 0.8 copy.104
  2.3 0.8 copy.106
  3.0 0.8 copy.101
  3.8 0.0 copy-start.1
  3.8 1.0 copy-done.1
  4.8 1.1 copy-done.4
  5.9 1.0 copy-done.6
  6.9 1.0 copy-done.8
  7.9 0.9 copy-done.13
  8.8 0.9 copy-done.17
  9.7 0.7 copy-done.22
  10.4 0.7 copy-done.24
  11.1 0.7 copy-done.26
  11.8 112.6 %shard_map.708 = (bf16[4,128,1536]{2,1,0:T(8,128)(2,1)}, bf16[4,128,1536]{2,1,0:T(8,128)(2,1)}, bf16[128,1536]{1,0:T(8,128)(2,1)S(1)}, s32[2,4,128,128]{3,2,1,0:...) custom-call(s32[1,3]{1,0:T(1,128)S(1)} %copy-done.26, ...), custom_call_target="tpu_custom_call" | custom-call | tf_op jit(solution)/shard_map/pallas_call | solution.py:1550
  124.4 0.0 copy-start.16
  124.4 2.0 slice.68.router_ref
  126.4 1.4 copy-done
  127.8 45.9 %shard_map.709 = (bf16[512,1792]{1,0:T(8,128)(2,1)}, f32[512,128]{1,0:T(8,128)S(1)}, bf16[512,768]{1,0:T(8,128)(2,1)S(1)}, bf16[512,1664]{1,0:T(8,128)(2,1)}, bf...) custom-call(bf16[512,1536]{1,0:T(8,128)(2,1)S(1)} %bitcast.59, ...), custom_call_target="tpu_custom_call" | custom-call | tf_op jit(solution)/shard_map/pallas_call | solution.py:1550
  173.7 1.4 copy-done.5
  175.1 27.9 %shard_map.710 = (f32[128,1536]{1,0:T(8,128)S(1)}, f32[128,1536]{1,0:T(8,128)S(1)}, bf16[128,1664]{1,0:T(8,128)(2,1)S(1)}, bf16[4,2,64,1536]{3,2,1,0:T(8,128)(2,1)S(1)}, bf16[2,64,1536]{2,1,0:T(8,128)(2,1)S(1)}) custom-call(bf16[512,1664]{1,0:T(8,128)(2,1)S(1)} %copy-done.5, bf16[128,1536]{1,0:T(8,128)(2,1)S(1)} %copy-done.2, f32[2,1536]{1,0:T(2,128)S(1)} %copy-done.19, ...), custom_call_target="tpu_custom_call" | custom-call | tf_op jit(solution)/shard_map/pallas_call | solution.py:1550
  203.0 1.1 copy-done.11
  204.2 49.6 %shard_map.711 = (bf16[2,4,128,1664]{3,2,1,0:T(8,128)(2,1)}, bf16[4,2,192,1024]{3,2,1,0:T(8,128)(2,1)}, bf16[4,2,64,1536]{3,2,1,0:T(8,128)(2,1)S(1)}, bf16[512,1...) custom-call(bf16[128,1664]{1,0:T(8,128)(2,1)S(1)} %get-tuple-element, ...), custom_call_target="tpu_custom_call" | custom-call | tf_op jit(solution)/shard_map/pallas_call | solution.py:1550
  253.7 1.1 copy-done.10
  254.9 1.1 copy-done.12
  256.0 0.9 slice.52
  256.9 12.9 %shard_map.712 = (bf16[2,512,1536]{2,1,0:T(8,128)(2,1)}, bf16[2,512,1536]{2,1,0:T(8,128)(2,1)}, bf16[2,512,1536]{2,1,0:T(8,128)(2,1)}, f32[1024,128]{1,0:T(8,128)}, bf16[8,128,128]{2,1,0:T(8,128)(2,1)}) custom-call(bf16[1024,1664]{1,0:T(8,128)(2,1)} %bitcast.73, bf16[1024,1536]{1,0:T(8,128)(2,1)} %bitcast.69, s32[1024,128]{1,0:T(8,128)} %bitcast.63, ...), custom_call_target="tpu_custom_call" | custom-call | tf_op jit(solution)/shard_map/pallas_call | solution.py:1582
  269.9 0.8 constant_dynamic-slice_fusion.weights_ref
  270.7 24.6 %shard_map.713 = (bf16[2,512,1536]{2,1,0:T(8,128)(2,1)}, bf16[2,512,1536]{2,1,0:T(8,128)(2,1)}, f32[2,512,128]{2,1,0:T(8,128)}, bf16[4,2,2,576,512]{4,3,2,1,0:T(8,128)(2,1)}) custom-call(bf16[2,512,1536]{2,1,0:T(8,128)(2,1)} %get-tuple-element.157.in_ref, bf16[2,512,1536]{2,1,0:T(8,128)(2,1)} %get-tuple-element.158.top_ref, ...), custom_call_target="tpu_custom_call" | custom-call | tf_op jit(solution)/shard_map/pallas_call | solution.py:1582
  295.3 10.8 %shard_map.714 = (bf16[1024,1536]{1,0:T(8,128)(2,1)}, bf16[1024,1664]{1,0:T(8,128)(2,1)}) custom-call(bf16[8,128,128]{2,1,0:T(8,128)(2,1)} %get-tuple-element.155.pick_ref, f32[1024,128]{1,0:T(8,128)} %get-tuple-element.156.weights_ref, s32[1]{0:T(128)} %bitcast.9.ids_ref, bf16[2,512,1536]{2,1,0:T(8,128)(2,1)} %get-tuple-element.164.out_ref, ...), custom_call_target="tpu_custom_call" | custom-call | tf_op jit(solution)/shard_map/pallas_call | solution.py:1582
  306.1 84.9 %shard_map.715 = (bf16[4,128,1664]{2,1,0:T(8,128)(2,1)S(1)}, f32[128,1536]{1,0:T(8,128)S(1)}, bf16[128,128]{1,0:T(8,128)(2,1)S(1)}, f32[8,1536]{1,0:T(8,128)S(1)...) custom-call(bf16[1024,1664]{1,0:T(8,128)(2,1)} %get-tuple-element.169.back_ref, ...), custom_call_target="tpu_custom_call" | custom-call | tf_op jit(solution)/shard_map/pallas_call | solution.py:1550
  391.0 48.6 %shard_map.716 = (bf16[512,1920]{1,0:T(8,128)(2,1)}, f32[8,1024]{1,0:T(8,128)S(1)}, f32[8,768]{1,0:T(8,128)S(1)}, f32[8,128]{1,0:T(8,128)S(1)}, bf16[4,576,512]{...) custom-call(bf16[512,1664]{1,0:T(8,128)(2,1)S(1)} %bitcast.60, ...), custom_call_target="tpu_custom_call" | custom-call | tf_op jit(solution)/shard_map/pallas_call | solution.py:1550
  439.6 0.7 copy-done.20
  440.3 0.0 copy-start.34
  440.3 0.0 copy-start.35
  440.3 0.0 copy-start.36
  440.3 0.0 copy-start.31
  440.4 108.4 %shard_map.717 = (bf16[4,48,1920]{2,1,0:T(8,128)(2,1)S(1)}, f32[96,1536]{1,0:T(8,128)S(1)}, f32[32,1536]{1,0:T(8,128)S(1)}, bf16[128,1536]{1,0:T(8,128)(2,1)S(1)...) custom-call(bf16[512,1536]{1,0:T(8,128)(2,1)} %bitcast.58, bf16[128,1536]{1,0:T(8,128)(2,1)S(1)} %copy-done.2, ...), custom_call_target="tpu_custom_call" | custom-call | tf_op jit(solution)/shard_map/pallas_call | solution.py:1550
  548.8 0.9 copy-done.14
  549.7 0.8 copy-done.15
  550.5 0.1 stack_reshape_squeeze.6
  550.6 0.1 stack_reshape_squeeze.7
  550.8 0.0 copy-start.32
  550.8 0.1 reshape_squeeze.10
  550.9 0.1 reduce_sum.29
  551.0 0.1 stack_reshape.11
  551.1 0.6 add_multiply_fusion.3
  551.7 0.7 add_multiply_fusion.2
  552.4 0.6 add_multiply_fusion.1
  553.0 0.8 add_multiply_fusion
  553.8 1.2 fusion.18
  555.0 0.2 fusion.19
  555.2 1.2 copy-done.27
  556.4 0.5 copy-done.29
  556.9 4.6 multiply_add_fusion.2
  561.5 9.0 %shard_map.718 = (f32[48,6448]{1,0:T(8,128)}, f32[48,6448]{1,0:T(8,128)}, f32[48,6448]{1,0:T(8,128)}, f32[48,6448]{1,0:T(8,128)}, f32[96,1536]{1,0:T(8,128)}, /*...) custom-call(bf16[4,48,1920]{2,1,0:T(8,128)(2,1)} %copy-done.14, ...), custom_call_target="tpu_custom_call" | custom-call | tf_op jit(solution)/shard_map/pallas_call | solution.py:1571
  570.5 0.8 fusion.10
  571.3 0.7 copy.111
  572.0 0.7 copy.109
  572.6 0.7 copy.110
  573.3 0.7 copy.108
  574.0 7.6 %multiply_add_fusion = (f32[4,192,1024]{2,1,0:T(8,128)}, f32[4,192,1024]{2,1,0:T(8,128)}, f32[4,192,1024]{2,1,0:T(8,128)}, f32[4,192,1024]{2,1,0:T(8,128)}) fusion(f32[4,192,1024]{2,1,0:T(8,128)} %gu_ref.1, f32[4,192,1024]{2,1,0:T(8,128)} %param.57, f32[4,192,1024]{2,1,0:T(8,128)} %param.58, bf16[4,192,512]{2,1,0:T(8,128)(2,1)S(1)} %get-tuple-element.383, ...), kind=kLoop, calls=%fused_computation.2 | loop fusion | flops 14942208 | bytes 23592960 | tf_op jit(solution)/shard_map/add | solution.py:89
  581.5 0.7 copy.116
  582.3 0.7 copy.117
  (61 shorter events, 0.2 us)
Async XLA Ops:
  3.8 1.0 copy-start.1
  4.8 1.1 copy-start.4
  5.9 1.0 copy-start.6
  6.9 1.0 copy-start.8
  7.9 0.9 copy-start.13
  8.8 0.9 copy-start.17
  9.7 0.7 copy-start.22
  10.4 0.7 copy-start.24
  11.1 0.7 copy-start.26
  11.8 114.6 %copy-start.19 = (f32[2,1536]{1,0:T(2,128)S(1)}, f32[2,1536]{1,0:T(2,128)}, u32[]{:S(2)}) copy-start(f32[2,1536]{1,0:T(2,128)} %gain_ref.7) | copy-start | bytes 36868
  124.4 49.3 %copy-start.16 = (s32[2,4,128,128]{3,2,1,0:T(8,128)}, s32[2,4,128,128]{3,2,1,0:T(8,128)S(1)}, u32[]{:S(2)}) copy-start(s32[2,4,128,128]{3,2,1,0:T(8,128)S(1)} %get-tuple-element.154) | copy-start | bytes 1572868
  126.4 1.4 copy-start
  127.8 45.9 %copy-start.2 = (bf16[128,1536]{1,0:T(8,128)(2,1)S(1)}, bf16[128,1536]{1,0:T(8,128)(2,1)}, u32[]{:S(2)}) copy-start(bf16[128,1536]{1,0:T(8,128)(2,1)} %tokens_ref.3) | copy-start | bytes 1179652
  173.7 1.5 copy-start.5
  203.0 1.1 copy-start.11
  253.7 1.1 copy-start.10
  254.9 1.1 copy-start.12
  295.3 10.8 %copy-start.3 = (bf16[1536,128]{1,0:T(8,128)(2,1)S(1)}, bf16[1536,128]{1,0:T(8,128)(2,1)}, u32[]{:S(2)}) copy-start(bf16[1536,128]{1,0:T(8,128)(2,1)} %slice.68.router_ref) | copy-start | bytes 1179652
  295.3 10.8 %copy-start.9 = (bf16[128,1536]{1,0:T(8,128)(2,1)S(1)}, bf16[128,1536]{1,0:T(8,128)(2,1)}, u32[]{:S(2)}) copy-start(bf16[128,1536]{1,0:T(8,128)(2,1)} %cot_ref.3) | copy-start | bytes 1179652
  306.1 84.9 %copy-start.7 = (bf16[4,2,192,512]{3,2,1,0:T(8,128)(2,1)S(1)}, bf16[4,2,192,512]{3,2,1,0:T(8,128)(2,1)}, u32[]{:S(2)}) copy-start(bf16[4,2,192,512]{3,2,1,0:T(8,128)(2,1)} %get-tuple-element.180.sgu_ref) | copy-start | bytes 4718596
  439.6 0.7 copy-start.20
  440.3 110.8 %copy-start.25 = (f32[3,48]{1,0:T(4,128)S(1)}, f32[3,48]{1,0:T(4,128)}, u32[]{:S(2)}) copy-start(f32[3,48]{1,0:T(4,128)} %head_ref.1) | copy-start | bytes 1732
  440.3 110.8 %copy-start.37 = (f32[3,48]{1,0:T(4,128)S(1)}, f32[3,48]{1,0:T(4,128)}, u32[]{:S(2)}) copy-start(f32[3,48]{1,0:T(4,128)} %param.69) | copy-start | bytes 1732
  440.3 110.8 %copy-start.38 = (f32[3,48]{1,0:T(4,128)S(1)}, f32[3,48]{1,0:T(4,128)}, u32[]{:S(2)}) copy-start(f32[3,48]{1,0:T(4,128)} %param.70) | copy-start | bytes 1732
  440.3 111.4 %copy-start.33 = (f32[2,1536]{1,0:T(2,128)S(1)}, f32[2,1536]{1,0:T(2,128)}, u32[]{:S(2)}) copy-start(f32[2,1536]{1,0:T(2,128)} %param.63) | copy-start | bytes 36868
  440.3 111.4 %copy-start.34 = (f32[2,1536]{1,0:T(2,128)S(1)}, f32[2,1536]{1,0:T(2,128)}, u32[]{:S(2)}) copy-start(f32[2,1536]{1,0:T(2,128)} %param.64) | copy-start | bytes 36868
  440.3 112.1 %copy-start.23 = (f32[3072]{0:T(1024)S(1)}, f32[3072]{0:T(1024)}, u32[]{:S(2)}) copy-start(f32[3072]{0:T(1024)} %param.71) | copy-start | bytes 36868
  440.3 112.1 %copy-start.35 = (f32[3072]{0:T(1024)S(1)}, f32[3072]{0:T(1024)}, u32[]{:S(2)}) copy-start(f32[3072]{0:T(1024)} %param.72) | copy-start | bytes 36868
  440.3 112.1 %copy-start.36 = (f32[3072]{0:T(1024)S(1)}, f32[3072]{0:T(1024)}, u32[]{:S(2)}) copy-start(f32[3072]{0:T(1024)} %param.73) | copy-start | bytes 36868
  440.3 112.7 %copy-start.18 = (f32[5,3328]{1,0:T(8,128)S(1)}, f32[5,3328]{1,0:T(8,128)}, u32[]{:S(2)}) copy-start(f32[5,3328]{1,0:T(8,128)} %conv_ref.1) | copy-start | bytes 199684
  440.3 112.7 %copy-start.30 = (f32[5,3328]{1,0:T(8,128)S(1)}, f32[5,3328]{1,0:T(8,128)}, u32[]{:S(2)}) copy-start(f32[5,3328]{1,0:T(8,128)} %param.66) | copy-start | bytes 199684
  440.3 112.7 %copy-start.31 = (f32[5,3328]{1,0:T(8,128)S(1)}, f32[5,3328]{1,0:T(8,128)}, u32[]{:S(2)}) copy-start(f32[5,3328]{1,0:T(8,128)} %param.67) | copy-start | bytes 199684
  548.8 0.9 copy-start.14
  549.7 0.8 copy-start.15
  550.5 4.7 copy-start.21
  550.8 4.4 copy-start.32
  551.1 3.9 copy-start.28
  555.0 1.4 copy-start.27
  555.0 1.9 copy-start.29
